TPU v7x, 512 devices: a whole 4x4x16 slice. The times are simulated.
512 devices in a mesh: row: 16 (over x, z_hi, core), lon: 32 (over y, z_lo).
Axes of the slice: x: 4, y: 4, z: 16 (z_hi: 2, z_lo: 8; z = z_hi * 8 + z_lo), core: 2. Of those that a mesh axis runs over, the one named last changes fastest.
Arguments:
- coarse: bfloat16 [128, 12, 32], P('lon')
- src_blocks: int32 [512, 4], P(('row', 'lon')), may hold values from 0 to 127, as said below
- slot_counts: int32 [512], P(('row', 'lon')), may hold values from 1 to 4
- remap_tiles: bfloat16 [512, 4, 32, 1024], P(('row', 'lon'))
- conv_a: float32 [3, 3, 12, 128], replicated, may hold values from -0.625 to 0.625
- conv_b: float32 [3, 3, 128, 128], replicated, may hold values from -0.1875 to 0.1875
- gain_a: float32 [128], replicated, may hold values from 0.5 to 1.5
- shift_a: float32 [128], replicated, may hold values from -3 to 3
- gain_b: float32 [128], replicated, may hold values from 0.5 to 1.5
- shift_b: float32 [128], replicated, may hold values from -3 to 3
Outputs:
- level_out: bfloat16 [128, 4096, 128], P('row', 'lon')
Inputs may be any that keep to these rules, and one draw needn't show every extreme that they name: `src_blocks`: block b is held by longitude index b // 4; every slot of a tile on longitude index l names a block held by longitude index l - 1, l or l + 1 (periodic). Slots at or past the tile's count are unused.
All inputs are finite; a program needn't handle non-finite values.
Results may differ from a plain program's by a relative error of at most 0.0022.
Values may be sent and summed in bfloat16 or wider, within the bound.
A program may use at most 64 MiB of HBM per device.

v0:
```python
import jax
import jax.numpy as jnp
from jax import lax
from jax.sharding import PartitionSpec as P

ROWS_DEV = 8
COLS_DEV = 128
CH = 128
GROUPS = 32


eps = 1e-05


def with_halo(cells, sides, width, closed):
    for axis, dim in sides:
        count = lax.axis_size(axis)
        ends = count if closed else count - 1
        head = lax.slice_in_dim(cells, 0, width, axis=dim)
        tail = lax.slice_in_dim(cells, cells.shape[dim] - width, cells.shape[dim], axis=dim)
        cells = jnp.concatenate(
            [
                lax.ppermute(tail, axis, [(i, (i + 1) % count) for i in range(ends)]),
                cells,
                lax.ppermute(head, axis, [((i + 1) % count, i) for i in range(ends)]),
            ],
            axis=dim,
        )
    return cells


def conv_first(field, weights):
    out_rows = field.shape[1] - 2
    out_cols = field.shape[2] - 2
    summed = jnp.zeros((out_rows, out_cols, weights.shape[3]), jnp.float32)
    for shift_row in range(3):
        for shift_col in range(3):
            window = field[:, shift_row : shift_row + out_rows, shift_col : shift_col + out_cols]
            summed = summed + jnp.einsum(
                "vrc,vo->rco",
                window,
                weights[shift_row, shift_col],
                precision=lax.Precision.HIGHEST,
                preferred_element_type=jnp.float32,
            )
    return summed


def conv_last(field, weights):
    out_rows = field.shape[0] - 2
    out_cols = field.shape[1] - 2
    summed = jnp.zeros((out_rows, out_cols, weights.shape[3]), jnp.float32)
    for shift_row in range(3):
        for shift_col in range(3):
            window = field[shift_row : shift_row + out_rows, shift_col : shift_col + out_cols, :]
            summed = summed + jnp.einsum(
                "rci,io->rco",
                window,
                weights[shift_row, shift_col],
                precision=lax.Precision.HIGHEST,
                preferred_element_type=jnp.float32,
            )
    return summed


def group_totals(values):
    return jnp.sum(values, axis=(0, 1)).reshape(GROUPS, CH // GROUPS).sum(axis=1)


def normalize(inside, whole, gain, shift):
    per_group = CH // GROUPS
    cell_count = (
        inside.shape[0] * inside.shape[1] * per_group * lax.axis_size("row") * lax.axis_size("lon")
    )
    average = lax.psum(group_totals(inside), ("row", "lon")) / cell_count
    centered = inside - jnp.repeat(average, per_group)[None, None, :]
    spread = lax.psum(group_totals(centered * centered), ("row", "lon")) / cell_count
    average_c = jnp.repeat(average, per_group)
    inverse = jnp.repeat(lax.rsqrt(spread + eps), per_group)
    return jax.nn.silu((whole - average_c) * inverse * gain + shift)


def per_device(
    coarse, src_blocks, slot_counts, remap_tiles, conv_a, conv_b, gain_a, shift_a, gain_b, shift_b
):
    slot_count = src_blocks.shape[1]
    vars_count = coarse.shape[1]
    held_blocks = coarse.shape[0]
    total_blocks = held_blocks * lax.axis_size("lon")
    coarse_table = with_halo(coarse, (("lon", 0),), held_blocks, True)
    local_ids = jnp.mod(src_blocks[0] - (lax.axis_index("lon") - 1) * held_blocks, total_blocks)
    live_slot = jnp.arange(slot_count) < slot_counts[0]
    picker = (
        (local_ids[:, None] == jnp.arange(coarse_table.shape[0])[None, :]) & live_slot[:, None]
    ).astype(jnp.bfloat16)
    blocks = jnp.einsum(
        "ki,ivb->kvb", picker, coarse_table, preferred_element_type=jnp.float32
    ).astype(jnp.bfloat16)
    fine_field = jnp.einsum(
        "kvb,kbc->vc", blocks, remap_tiles[0], preferred_element_type=jnp.float32
    )
    fine_field = fine_field.reshape(vars_count, ROWS_DEV, COLS_DEV)
    margin_width = 1
    padded = with_halo(fine_field, (("lon", 2),), margin_width, True)
    padded = with_halo(padded, (("row", 1),), margin_width, False)
    hidden_a = conv_first(padded, conv_a)
    activ_a = normalize(hidden_a, hidden_a, gain_a, shift_a)
    ready_field = with_halo(activ_a, (("lon", 1),), 1, True)
    ready_field = with_halo(ready_field, (("row", 0),), 1, False)
    hidden_b = conv_last(ready_field, conv_b)
    return normalize(hidden_b, hidden_b, gain_b, shift_b).astype(jnp.bfloat16)


def solution(mesh):
    return jax.shard_map(
        per_device,
        mesh=mesh,
        in_specs=(
            P("lon", None, None),
            P(("row", "lon"), None),
            P(("row", "lon")),
            P(("row", "lon"), None, None, None),
            P(),
            P(),
            P(),
            P(),
            P(),
            P(),
        ),
        out_specs=P("row", "lon", None),
        check_vma=False,
    )
```

profile of v0, /device:TPU:1, one launch (start us, length us, event | category | flops | bytes accessed | tf_op | source)
XLA Modules:
  0.0 525.6 jit_solution(2232523762760662468)
XLA Ops:
  0.0 4.5 collective-permute-start
  4.5 13.7 %collective-permute-start.1 = (bf16[4,12,32]{2,0,1:T(4,128)(2,1)}, bf16[4,12,32]{2,0,1:T(4,128)(2,1)S(1)}, u32[]{:S(2)}, u32[]{:S(2)}) collective-permute-start(bf16[4,12,32]{2,0,1:T(4,128)(2,1)} %param.10), channel_id=1, source_target_pairs={{1,0},{2,1},{3,2},{4,3},{5,4},{6,5},{7,6},{8,7},{9,8},{10,9},{11,1... | collective-permute-start | bytes 9224 | tf_op jit(solution)/shard_map/ppermute | solution.py:25
  18.9 0.7 and_select_fusion
  20.2 1.9 collective-permute-start.2
  22.1 12.1 %collective-permute-start.3 = (f32[12,8,1]{2,0,1:T(8,128)S(1)}, f32[12,8,1]{2,0,1:T(8,128)S(1)}, u32[]{:S(2)}, u32[]{:S(2)}) collective-permute-start(f32[12,8,1]{2,0,1:T(8,128)S(1)} %get-tuple-element.16), channel_id=1, source_target_pairs={{1,0},{2,1},{3,2},{4,3},{5,4},{6,5},{7,6},{8,7},{9,8},{10,9},{11,1... | collective-permute-start | bytes 1160 | tf_op jit(solution)/shard_map/ppermute | solution.py:25
  34.3 1.0 fusion.73
  35.7 14.9 %collective-permute-start.4 = (f32[12,1,130]{2,0,1:T(8,128)S(1)}, f32[12,1,130]{2,0,1:T(8,128)S(1)}, u32[]{:S(2)}, u32[]{:S(2)}) collective-permute-start(f32[12,1,130]{2,0,1:T(8,128)S(1)} %get-tuple-element.13), channel_id=1, source_target_pairs={{0,32},{32,64},{64,96},{96,128},{128,160},{160,192},{192,224},{224... | collective-permute-start | bytes 18728 | tf_op jit(solution)/shard_map/ppermute | solution.py:23
  50.6 1.9 collective-permute-start.5
  52.5 1.1 fusion.35
  53.6 10.8 %collective-permute-done.5 = f32[12,1,130]{2,0,1:T(8,128)S(1)} collective-permute-done((f32[12,1,130]{2,0,1:T(8,128)S(1)}, f32[12,1,130]{2,0,1:T(8,128)S(1)}, u32[]{:S(2)}, u32[]{:S(2)}) %collective-permute-start.5) | collective-permute-done | bytes 6272 | tf_op jit(solution)/shard_map/ppermute | solution.py:25
  64.5 1.1 fusion.37
  65.6 1.1 fusion.39
  66.7 1.1 fusion.28
  67.8 1.1 fusion.30
  68.9 1.0 fusion.32
  69.9 1.0 fusion.2
  70.9 1.1 fusion.101
  72.2 104.3 %psum.28 = f32[32]{0:T(128)S(1)} all-reduce(f32[32]{0:T(128)S(1)} %reduce_sum.73), channel_id=1, replica_groups=mesh['row'=16,'lon'=32] {'row','lon'}, use_global_device_ids=true, to_apply=%region_2.3 | all-reduce | flops 32 | bytes 256 | tf_op jit(solution)/shard_map/psum | solution.py:75
  177.1 98.5 %psum.29 = f32[32]{0:T(128)S(1)} all-reduce(f32[32]{0:T(128)S(1)} %reduce_sum.75), channel_id=1, replica_groups=mesh['row'=16,'lon'=32] {'row','lon'}, use_global_device_ids=true, to_apply=%region_5.6 | all-reduce | flops 32 | bytes 256 | tf_op jit(solution)/shard_map/psum | solution.py:77
  276.0 3.6 collective-permute-start.6
  279.6 10.6 %collective-permute-start.7 = (f32[8,1,128]{2,1,0:T(1,128)S(1)}, f32[8,1,128]{2,1,0:T(1,128)S(1)}, u32[]{:S(2)}, u32[]{:S(2)}) collective-permute-start(f32[8,1,128]{2,1,0:T(1,128)S(1)} %get-tuple-element.10), channel_id=1, source_target_pairs={{1,0},{2,1},{3,2},{4,3},{5,4},{6,5},{7,6},{8,7},{9,8},{10,9},{11,1... | collective-permute-start | bytes 12296 | tf_op jit(solution)/shard_map/ppermute | solution.py:25
  290.2 0.6 fusion.46
  290.8 10.9 %collective-permute-start.8 = (f32[1,130,128]{2,1,0:T(8,128)S(1)}, f32[1,130,128]{2,1,0:T(8,128)S(1)}, u32[]{:S(2)}, u32[]{:S(2)}) collective-permute-start(f32[1,130,128]{2,1,0:T(8,128)S(1)} %get-tuple-element.7), channel_id=1, source_target_pairs={{0,32},{32,64},{64,96},{96,128},{128,160},{160,192},{192,224},{224... | collective-permute-start | bytes 199688 | tf_op jit(solution)/shard_map/ppermute | solution.py:23
  301.8 1.9 collective-permute-start.9
  304.3 11.8 %collective-permute-done.9 = f32[1,130,128]{2,1,0:T(8,128)S(1)} collective-permute-done((f32[1,130,128]{2,1,0:T(8,128)S(1)}, f32[1,130,128]{2,1,0:T(8,128)S(1)}, u32[]{:S(2)}, u32[]{:S(2)}) %collective-permute-start.9) | collective-permute-done | bytes 66592 | tf_op jit(solution)/shard_map/ppermute | solution.py:25
  317.3 0.6 fusion.12
  318.5 0.6 fusion.16
  319.0 0.6 fusion.11
  319.7 0.6 fusion.102
  320.6 103.3 %psum.30 = f32[32]{0:T(128)S(1)} all-reduce(f32[32]{0:T(128)S(1)} %reduce_sum.77), channel_id=1, replica_groups=mesh['row'=16,'lon'=32] {'row','lon'}, use_global_device_ids=true, to_apply=%region_8.9 | all-reduce | flops 32 | bytes 256 | tf_op jit(solution)/shard_map/psum | solution.py:75
  424.4 99.5 %psum.31 = f32[32]{0:T(128)S(1)} all-reduce(f32[32]{0:T(128)S(1)} %reduce_sum.79), channel_id=1, replica_groups=mesh['row'=16,'lon'=32] {'row','lon'}, use_global_device_ids=true, to_apply=%region_11.12 | all-reduce | flops 32 | bytes 256 | tf_op jit(solution)/shard_map/psum | solution.py:77
  524.7 0.9 multiply_convert_fusion
  (60 shorter events, 6.2 us)
Async XLA Ops:
  0.0 19.8 %copy-start = (bf16[1,4,32,1024]{3,2,1,0:T(8,128)(2,1)S(1)}, bf16[1,4,32,1024]{3,2,1,0:T(8,128)(2,1)}, u32[]{:S(2)}) copy-start(bf16[1,4,32,1024]{3,2,1,0:T(8,128)(2,1)} %param.13) | copy-start | bytes 786436
  0.0 19.6 %copy-start.7 = (bf16[4,12,32]{2,0,1:T(4,128)(2,1)S(1)}, bf16[4,12,32]{2,0,1:T(4,128)(2,1)}, u32[]{:S(2)}) copy-start(bf16[4,12,32]{2,0,1:T(4,128)(2,1)} %param.10) | copy-start | bytes 9220
  0.0 19.5 %collective-permute-start = (bf16[4,12,32]{2,0,1:T(4,128)(2,1)}, bf16[4,12,32]{2,0,1:T(4,128)(2,1)S(1)}, u32[]{:S(2)}, u32[]{:S(2)}) collective-permute-start(bf16[4,12,32]{2,0,1:T(4,128)(2,1)} %param.10), channel_id=1, source_target_pairs={{0,1},{1,2},{2,3},{3,4},{4,5},{5,6},{6,7},{7,8},{8,9},{9,10},{10,1... | collective-permute-start | bytes 9224 | tf_op jit(solution)/shard_map/ppermute | solution.py:23
  4.5 15.0 %collective-permute-start.1 = (bf16[4,12,32]{2,0,1:T(4,128)(2,1)}, bf16[4,12,32]{2,0,1:T(4,128)(2,1)S(1)}, u32[]{:S(2)}, u32[]{:S(2)}) collective-permute-start(bf16[4,12,32]{2,0,1:T(4,128)(2,1)} %param.10), channel_id=1, source_target_pairs={{1,0},{2,1},{3,2},{4,3},{5,4},{6,5},{7,6},{8,7},{9,8},{10,9},{11,1... | collective-permute-start | bytes 9224 | tf_op jit(solution)/shard_map/ppermute | solution.py:25
  20.1 14.1 %copy-start.2 = (f32[3,3,12,128]{3,2,1,0:T(8,128)S(1)}, f32[3,3,12,128]{3,2,1,0:T(8,128)}, u32[]{:S(2)}) copy-start(f32[3,3,12,128]{3,2,1,0:T(8,128)} %param.14) | copy-start | bytes 165892
  20.2 15.1 %collective-permute-start.2 = (f32[12,8,1]{2,0,1:T(8,128)S(1)}, f32[12,8,1]{2,0,1:T(8,128)S(1)}, u32[]{:S(2)}, u32[]{:S(2)}) collective-permute-start(f32[12,8,1]{2,0,1:T(8,128)S(1)} %get-tuple-element.15), channel_id=1, source_target_pairs={{0,1},{1,2},{2,3},{3,4},{4,5},{5,6},{6,7},{7,8},{8,9},{9,10},{10,1... | collective-permute-start | bytes 1160 | tf_op jit(solution)/shard_map/ppermute | solution.py:23
  22.1 13.4 %collective-permute-start.3 = (f32[12,8,1]{2,0,1:T(8,128)S(1)}, f32[12,8,1]{2,0,1:T(8,128)S(1)}, u32[]{:S(2)}, u32[]{:S(2)}) collective-permute-start(f32[12,8,1]{2,0,1:T(8,128)S(1)} %get-tuple-element.16), channel_id=1, source_target_pairs={{1,0},{2,1},{3,2},{4,3},{5,4},{6,5},{7,6},{8,7},{9,8},{10,9},{11,1... | collective-permute-start | bytes 1160 | tf_op jit(solution)/shard_map/ppermute | solution.py:25
  35.7 17.9 %collective-permute-start.4 = (f32[12,1,130]{2,0,1:T(8,128)S(1)}, f32[12,1,130]{2,0,1:T(8,128)S(1)}, u32[]{:S(2)}, u32[]{:S(2)}) collective-permute-start(f32[12,1,130]{2,0,1:T(8,128)S(1)} %get-tuple-element.13), channel_id=1, source_target_pairs={{0,32},{32,64},{64,96},{96,128},{128,160},{160,192},{192,224},{224... | collective-permute-start | bytes 18728 | tf_op jit(solution)/shard_map/ppermute | solution.py:23
  50.6 13.8 %collective-permute-start.5 = (f32[12,1,130]{2,0,1:T(8,128)S(1)}, f32[12,1,130]{2,0,1:T(8,128)S(1)}, u32[]{:S(2)}, u32[]{:S(2)}) collective-permute-start(f32[12,1,130]{2,0,1:T(8,128)S(1)} %get-tuple-element.14), channel_id=1, source_target_pairs={{32,0},{64,32},{96,64},{128,96},{160,128},{192,160},{224,192},{256... | collective-permute-start | bytes 18728 | tf_op jit(solution)/shard_map/ppermute | solution.py:25
  176.7 99.1 %copy-start.3 = (f32[128]{0:T(128)S(1)}, f32[128]{0:T(128)}, u32[]{:S(2)}) copy-start(f32[128]{0:T(128)} %param.17) | copy-start | bytes 1540
  176.7 99.1 %copy-start.4 = (f32[128]{0:T(128)S(1)}, f32[128]{0:T(128)}, u32[]{:S(2)}) copy-start(f32[128]{0:T(128)} %param.16) | copy-start | bytes 1540
  176.9 113.3 %copy-start.1 = (f32[3,3,128,128]{3,2,1,0:T(8,128)S(1)}, f32[3,3,128,128]{3,2,1,0:T(8,128)}, u32[]{:S(2)}) copy-start(f32[3,3,128,128]{3,2,1,0:T(8,128)} %param.15) | copy-start | bytes 1769476
  276.0 14.8 %collective-permute-start.6 = (f32[8,1,128]{2,1,0:T(1,128)S(1)}, f32[8,1,128]{2,1,0:T(1,128)S(1)}, u32[]{:S(2)}, u32[]{:S(2)}) collective-permute-start(f32[8,1,128]{2,1,0:T(1,128)S(1)} %get-tuple-element.9), channel_id=1, source_target_pairs={{0,1},{1,2},{2,3},{3,4},{4,5},{5,6},{6,7},{7,8},{8,9},{9,10},{10,1... | collective-permute-start | bytes 12296 | tf_op jit(solution)/shard_map/ppermute | solution.py:23
  279.6 11.2 %collective-permute-start.7 = (f32[8,1,128]{2,1,0:T(1,128)S(1)}, f32[8,1,128]{2,1,0:T(1,128)S(1)}, u32[]{:S(2)}, u32[]{:S(2)}) collective-permute-start(f32[8,1,128]{2,1,0:T(1,128)S(1)} %get-tuple-element.10), channel_id=1, source_target_pairs={{1,0},{2,1},{3,2},{4,3},{5,4},{6,5},{7,6},{8,7},{9,8},{10,9},{11,1... | collective-permute-start | bytes 12296 | tf_op jit(solution)/shard_map/ppermute | solution.py:25
  290.8 13.4 %collective-permute-start.8 = (f32[1,130,128]{2,1,0:T(8,128)S(1)}, f32[1,130,128]{2,1,0:T(8,128)S(1)}, u32[]{:S(2)}, u32[]{:S(2)}) collective-permute-start(f32[1,130,128]{2,1,0:T(8,128)S(1)} %get-tuple-element.7), channel_id=1, source_target_pairs={{0,32},{32,64},{64,96},{96,128},{128,160},{160,192},{192,224},{224... | collective-permute-start | bytes 199688 | tf_op jit(solution)/shard_map/ppermute | solution.py:23
  301.8 14.3 %collective-permute-start.9 = (f32[1,130,128]{2,1,0:T(8,128)S(1)}, f32[1,130,128]{2,1,0:T(8,128)S(1)}, u32[]{:S(2)}, u32[]{:S(2)}) collective-permute-start(f32[1,130,128]{2,1,0:T(8,128)S(1)} %get-tuple-element.8), channel_id=1, source_target_pairs={{32,0},{64,32},{96,64},{128,96},{160,128},{192,160},{224,192},{256... | collective-permute-start | bytes 199688 | tf_op jit(solution)/shard_map/ppermute | solution.py:25
  524.0 0.7 copy-start.5
  524.0 0.7 copy-start.6
where the time goes:
time: 527 us; the launch traced here: 526 us
  blocking collectives  406 us (77%)
  starting transfers between devices  76.1 us (14%)
  waiting for transfers between devices  22.9 us (4%)
  matrix products  15.3 us (3%)
    psum x2, blocking collectives, normalize(): average = lax.psum(group_totals(inside), ('row', 'lon')) / cell_count  208 us
    psum x2, blocking collectives, normalize(): lax.psum(group_totals(centered * centered), ('row', 'lon')) / cell_count  198 us
    ppermute x5, starting transfers between devices, with_halo(): lax.ppermute(head, axis, [((i + 1) % count, i) for i in range(ends)])  40.2 us
    ppermute x5, starting transfers between devices, with_halo(): lax.ppermute(tail, axis, [(i, (i + 1) % count) for i in range(ends)])  35.9 us
    ppermute x5, waiting for transfers between devices, with_halo(): lax.ppermute(head, axis, [((i + 1) % count, i) for i in range(ends)])  22.9 us
  transfers between devices with their start and end apart: 10, of which 3 were waited for; matrix products, arithmetic and copies ran while one was open for 1% of the time, Pallas kernels for 0%

commit v1 on v0

v1 whole, which is shorter than its diff:
```python
import jax
import jax.numpy as jnp
from jax import lax
from jax.experimental import pallas as pl
from jax.experimental.pallas import tpu as pltpu
from jax.sharding import PartitionSpec as P

ROWS_DEV = 8
COLS_DEV = 128
VARS = 12
CH = 128
GROUPS = 32
SLOTS = 4
BCELLS = 32
BLK_DEV = 4
NBLK = 128
PER_GROUP = CH // GROUPS
MESH = pl.DeviceIdType.MESH
F32 = jnp.float32
BF16 = jnp.bfloat16

eps = 1e-05


def coords():
    row = lax.axis_index("row")
    lon = lax.axis_index("lon")
    core = lax.rem(row, 2)
    z_hi = lax.rem(lax.div(row, 2), 2)
    x = lax.div(row, 4)
    y = lax.div(lon, 8)
    z = z_hi * 8 + lax.rem(lon, 8)
    return row, lon, x, y, z, core


def device_at(x, y, z, core):
    return (x * 4 + lax.div(z, 8) * 2 + core, y * 8 + lax.rem(z, 8))


def moved(value, step, count):
    return lax.rem(value + step, count) if step else value


def along_z(place):
    _, _, x, y, z, core = place
    steps = sorted(range(1, 16), key=lambda d: -min(d, 16 - d))
    return [device_at(x, y, moved(z, d, 16), core) for d in steps]


def across(place):
    _, _, x, y, z, core = place
    steps = [(a, b, c) for a in range(4) for b in range(4) for c in range(2) if a or b or c]
    steps.sort(key=lambda s: -(min(s[0], 4 - s[0]) + min(s[1], 4 - s[1])))
    return [device_at(moved(x, a, 4), moved(y, b, 4), z, moved(core, c, 2)) for a, b, c in steps]


def coarse_neighbours(place):
    _, _, x, y, z, core = place
    z_lo = lax.rem(z, 8)
    y_up = lax.rem(y + lax.div(z_lo + 1, 8), 4)
    y_down = lax.rem(y + 3 + lax.div(z_lo + 7, 8), 4)
    up = device_at(x, y_up, lax.rem(z + 1, 16), core)
    down = device_at(x, y_down, lax.rem(z + 15, 16), core)
    return up, down


def iota(shape, dim):
    return lax.broadcasted_iota(jnp.int32, shape, dim)


def split(value):
    high = value.astype(BF16)
    low = (value - high.astype(F32)).astype(BF16)
    return high, low


def dot(a, b, dims=((1,), (0,))):
    return lax.dot_general(a, b, (dims, ((), ())), preferred_element_type=F32)


def over_group(row):
    lane = iota(row.shape, 1)
    near = jnp.where((lane & 1) == 0, pltpu.roll(row, CH - 1, 1), pltpu.roll(row, 1, 1))
    row = row + near
    far = jnp.where((lane & 2) == 0, pltpu.roll(row, CH - 2, 1), pltpu.roll(row, 2, 1))
    return row + far


def local_stats(rows, cells):
    total = sum(jnp.sum(r, axis=0, keepdims=True) for r in rows)
    mean = over_group(total) * (1.0 / (cells * PER_GROUP))
    dev = sum(jnp.sum((r - mean) * (r - mean), axis=0, keepdims=True) for r in rows)
    return mean, over_group(dev)


def merge(mean, dev, others, cells):
    count = others.shape[0] + 1
    means = others[:, 0:1, :]
    whole = (mean + jnp.sum(means, axis=0)) * (1.0 / count)
    off = means - whole
    own = mean - whole
    spread = own * own + jnp.sum(off * off, axis=0)
    return whole, dev + jnp.sum(others[:, 1:2, :], axis=0) + (cells * PER_GROUP) * spread


LEFT, MAIN, RIGHT, WIDE = 8, 16, 144, 160


def kernel(
    src_ref, cnt_ref, coarse_ref, remap_ref, ca_ref, cb_ref, vec_ref,
    hb_ref, fin_ref,
    coarse_v, remap_v, ca_v, cb_v, vec_v,
    tt, crit_out, far_out, crit, far,
    sel, edges, wa32, wa, wb,
    xs, gs, ha, act, hb,
    stat, buf_x, buf_z,
    in_sem, out_sem, send_sem, recv_sem,
):
    place = coords()
    row, lon = place[0], place[1]
    z_mates = along_z(place)
    xy_mates = across(place)
    up, down = coarse_neighbours(place)
    row_up, row_down = lax.rem(row + 15, 16), lax.rem(row + 1, 16)
    lon_left, lon_right = lax.rem(lon + 31, 32), lax.rem(lon + 1, 32)
    halo = [
        (row_down, lon), (row_up, lon),
        (row, lon_right), (row, lon_left),
        (row_down, lon_right), (row_up, lon_right),
        (row_down, lon_left), (row_up, lon_left),
    ]
    barrier = pltpu.get_barrier_semaphore()
    partners = halo + [up, down] + z_mates + xy_mates
    for mate in partners:
        pl.semaphore_signal(barrier, inc=1, device_id=mate, device_id_type=MESH)

    loads = [
        pltpu.make_async_copy(coarse_ref, coarse_v, in_sem.at[0]),
        pltpu.make_async_copy(remap_ref, remap_v, in_sem.at[1]),
        pltpu.make_async_copy(ca_ref, ca_v, in_sem.at[2]),
        pltpu.make_async_copy(cb_ref, cb_v, in_sem.at[3]),
        pltpu.make_async_copy(vec_ref, vec_v, in_sem.at[4]),
    ]
    for load in loads:
        load.start()

    lane = iota((1, 128), 1)
    target = jnp.full((1, 128), -1, jnp.int32)
    for k in range(SLOTS):
        local = lax.rem(src_ref[0, k] - (lon - 1) * BLK_DEV + 2 * NBLK, NBLK)
        first = jnp.where(k < cnt_ref[0], local * BCELLS, -1024)
        target = jnp.where(lane // BCELLS == k, first + (lane & (BCELLS - 1)), target)
    sel[...] = jnp.where(iota((3 * 128, 128), 0) == target, 1.0, 0.0).astype(BF16)

    loads[0].wait()
    tile = jnp.zeros((VARS, 128), F32)
    for b in range(BLK_DEV):
        put = jnp.where(iota((BCELLS, 128), 0) + b * BCELLS == iota((BCELLS, 128), 1), 1.0, 0.0)
        tile = tile + dot(coarse_v[b], put.astype(BF16))
    pad = jnp.concatenate([tile, jnp.zeros((16 - VARS, 128), F32)], axis=0)
    tt[1] = pad.astype(BF16)

    loads[1].wait()
    ri = lane >> 3
    ci = lane & 7
    col = jnp.where(ci == 6, 126, jnp.where(ci == 7, 127, jnp.where(ci < 2, ci, -4096)))
    rw = jnp.where(ri < 2, ri + 6, jnp.where(ri < 10, ri - 2, jnp.where(ri < 12, ri - 10, -4096)))
    cell = rw * COLS_DEV + col
    pick = jnp.where(iota((1024, 128), 0) == cell, 1.0, 0.0).astype(BF16)
    edges[:, 512:640] = dot(remap_v[...], pick).astype(BF16)
    edges[:, 0:256] = remap_v[:, 0:256]
    edges[:, 256:512] = remap_v[:, 768:1024]

    pl.semaphore_wait(barrier, len(partners))

    for slot, mate in ((0, up), (2, down)):
        pltpu.make_async_remote_copy(
            src_ref=tt.at[1], dst_ref=tt.at[slot], send_sem=send_sem.at[0], recv_sem=recv_sem.at[0 if slot == 0 else 1],
            device_id=mate, device_id_type=MESH,
        ).start()
    middle = dot(tt[1], sel[128:256, :])

    loads[2].wait()
    wa32[...] = jnp.zeros_like(wa32)
    for dy in range(3):
        for part in range(3):
            first = (dy * 3 + part) * VARS
            for dx in range(3):
                wa32[first : first + VARS, dx * CH : (dx + 1) * CH] = ca_v[dy, dx]
    line = iota((128, 3 * CH), 0)
    twelfth = (line * 43) >> 9
    part_of = twelfth - 3 * ((twelfth * 11) >> 5)
    whole = wa32[...]
    high, low = split(whole)
    wa[...] = jnp.where(part_of == 2, low.astype(F32), high.astype(F32)).astype(BF16)

    twelfth_l = (lane * 43) >> 9
    var_l = jnp.where(lane < 9 * VARS, lane - 12 * twelfth_l, 4096)
    part_l = twelfth_l - 3 * ((twelfth_l * 11) >> 5)
    want = jnp.where(part_l == 1, var_l + 16, var_l)
    spread_msg = jnp.where(iota((32, 128), 0) == want, 1.0, 0.0).astype(BF16)
    spread_var = jnp.where(iota((16, 128), 0) == var_l, 1.0, 0.0).astype(BF16)

    for slot in (0, 2):
        pltpu.make_async_remote_copy(
            src_ref=tt.at[1], dst_ref=tt.at[slot], send_sem=send_sem.at[0], recv_sem=recv_sem.at[0 if slot == 0 else 1],
            device_id=up, device_id_type=MESH,
        ).wait_recv()
    blocks = middle + dot(tt[0], sel[0:128, :]) + dot(tt[2], sel[256:384, :])
    blocks = blocks.astype(BF16)

    fine_edges = dot(blocks, edges[...])
    high, low = split(fine_edges)
    for slot, first in ((0, 384), (1, 0), (2, 512)):
        crit_out[slot, 0:16, :] = high[:, first : first + 128]
        crit_out[slot, 16:32, :] = low[:, first : first + 128]
    for slot, first in ((0, 256), (1, 128)):
        far_out[slot, 0:16, :] = high[:, first : first + 128]
        far_out[slot, 16:32, :] = low[:, first : first + 128]
    for slot, mate in enumerate(halo):
        pltpu.make_async_remote_copy(
            src_ref=crit_out.at[min(slot, 2)], dst_ref=crit.at[slot], send_sem=send_sem.at[1], recv_sem=recv_sem.at[2],
            device_id=mate, device_id_type=MESH,
        ).start()
    for slot in range(2):
        pltpu.make_async_remote_copy(
            src_ref=far_out.at[slot], dst_ref=far.at[slot], send_sem=send_sem.at[2], recv_sem=recv_sem.at[3],
            device_id=halo[slot], device_id_type=MESH,
        ).start()

    spread_blocks = dot(blocks, spread_var, ((0,), (0,))).astype(BF16)
    fine = dot(remap_v[...], spread_blocks, ((0,), (0,)))
    high, low = split(fine)
    packed = jnp.where(part_l == 1, low.astype(F32), high.astype(F32)).astype(BF16)
    xs[2:10] = packed.reshape(ROWS_DEV, COLS_DEV, 128)

    third = jnp.broadcast_to(lane, (128, 128))

    def patches(before, here, after, lanes):
        before = jnp.where(lanes < 3 * VARS, before.astype(F32), 0.0)
        here = jnp.where((lanes >= 3 * VARS) & (lanes < 6 * VARS), here.astype(F32), 0.0)
        after = jnp.where(lanes >= 6 * VARS, after.astype(F32), 0.0)
        return (before + here + after).astype(BF16)

    def taps(out_rows):
        field = [patches(xs[i], xs[i + 1], xs[i + 2], third) for i in out_rows]
        result = dot(jnp.concatenate(field, axis=0), wa[...])
        for n, i in enumerate(out_rows):
            for dx in range(3):
                gs[dx, i, MAIN:RIGHT, :] = result[n * 128 : (n + 1) * 128, dx * CH : (dx + 1) * CH]

    def joined(i, first, size):
        return gs[0, i, first - 1 : first - 1 + size, :] + gs[1, i, first : first + size, :] + gs[2, i, first + 1 : first + 1 + size, :]

    taps(list(range(2, 8)))

    loads[3].wait()
    for dy in range(3):
        for dx in range(3):
            high, low = split(cb_v[dy, dx])
            span = slice(dx * CH, (dx + 1) * CH)
            wb[dy * 384 : dy * 384 + 128, span] = high
            wb[dy * 384 + 128 : dy * 384 + 256, span] = high
            wb[dy * 384 + 256 : dy * 384 + 384, span] = low
    loads[4].wait()

    not_first = jnp.where(row > 0, 1.0, 0.0).astype(F32)
    not_last = jnp.where(row < 15, 1.0, 0.0).astype(F32)
    pltpu.make_async_copy(crit, crit, recv_sem.at[2]).wait()
    top = crit[0].astype(F32) * not_first
    bottom = crit[1].astype(F32) * not_last
    left = jnp.where(
        ri < 2, crit[4].astype(F32) * not_first, jnp.where(ri < 10, crit[2].astype(F32), crit[5].astype(F32) * not_last)
    )
    right = jnp.where(
        ri < 2, crit[6].astype(F32) * not_first, jnp.where(ri < 10, crit[3].astype(F32), crit[7].astype(F32) * not_last)
    )
    sides = jnp.where(ci >= 4, left, right)
    around = jnp.concatenate([top, bottom, sides], axis=1).astype(BF16)
    placed = dot(around, spread_msg, ((0,), (0,))).astype(BF16)
    xs[1] = placed[0:128]
    xs[10] = placed[128:256]
    side = placed[256:352].astype(F32).reshape(12, 8, 128)
    side_lane = jnp.broadcast_to(lane.reshape(1, 1, 128), (10, 8, 128))
    side_patches = patches(side[0:10], side[1:11], side[2:12], side_lane).reshape(80, 128)
    side_taps = dot(side_patches, wa[...]).reshape(10, 8, 3 * CH)
    for dx in range(3):
        piece = side_taps[:, :, dx * CH : (dx + 1) * CH]
        gs[dx, :, LEFT:MAIN, :] = piece
        gs[dx, :, RIGHT : RIGHT + 8, :] = piece
    taps([1, 8])
    for i in range(1, 9):
        ha[i, MAIN:RIGHT, :] = joined(i, MAIN, 128)

    def all_reduce(turn, mean, dev, beside):
        cells = ROWS_DEV * COLS_DEV
        for stage, (mates, buf) in enumerate(((xy_mates, buf_x), (z_mates, buf_z))):
            sem = 4 + turn * 2 + stage
            stat[turn, stage, 0:1, :] = mean
            stat[turn, stage, 1:2, :] = dev
            for j, mate in enumerate(mates):
                pltpu.make_async_remote_copy(
                    src_ref=stat.at[turn, stage], dst_ref=buf.at[turn, j], send_sem=send_sem.at[sem - 1], recv_sem=recv_sem.at[sem],
                    device_id=mate, device_id_type=MESH,
                ).start()
            if stage == 0:
                beside()
            pltpu.make_async_copy(buf.at[turn], buf.at[turn], recv_sem.at[sem]).wait()
            mean, dev = merge(mean, dev, buf[turn], cells)
            cells = cells * (len(mates) + 1)
        return mean, lax.rsqrt(dev * (1.0 / (cells * PER_GROUP)) + eps)

    def around_a():
        pltpu.make_async_copy(far, far, recv_sem.at[3]).wait()
        beyond = jnp.concatenate([far[0].astype(F32) * not_first, far[1].astype(F32) * not_last], axis=1).astype(BF16)
        placed = dot(beyond, spread_msg, ((0,), (0,))).astype(BF16)
        xs[0] = placed[0:128]
        xs[11] = placed[128:256]
        taps([0, 9])
        for i in (0, 9):
            ha[i, MAIN:RIGHT, :] = joined(i, MAIN, 128)
        for i in range(10):
            ha[i, LEFT:MAIN, :] = joined(i, LEFT, 8)
            ha[i, RIGHT : RIGHT + 8, :] = joined(i, RIGHT, 8)

    mean, dev = local_stats([ha[i, MAIN:RIGHT, :] for i in range(1, 9)], ROWS_DEV * COLS_DEV)
    mean, inverse = all_reduce(0, mean, dev, around_a)

    scale = inverse * vec_v[0:1, :]
    shift = vec_v[1:2, :]
    for i in range(10):
        for first, size, at in ((MAIN, 128, 0), (LEFT, 16, 128)):
            if size == 128:
                value = ha[i, MAIN:RIGHT, :]
            else:
                value = jnp.concatenate([ha[i, RIGHT : RIGHT + 8, :], ha[i, LEFT:MAIN, :]], axis=0)
            normed = (value - mean) * scale + shift
            half = normed * 0.5
            value = half + half * jnp.tanh(half)
            if i == 0:
                value = value * not_first
            if i == 9:
                value = value * not_last
            high, low = split(value)
            act[i, at : at + size, 0:128] = high
            act[i, at : at + size, 128:256] = low
            act[i, at : at + size, 256:384] = high

    field = jnp.concatenate([act[0:8], act[1:9], act[2:10]], axis=2).reshape(8 * 144, 9 * CH)
    result = dot(field, wb[...]).reshape(8, 144, 3 * CH)
    for dx in range(3):
        span = slice(dx * CH, (dx + 1) * CH)
        gs[dx, 0:8, MAIN:RIGHT, :] = result[:, 0:128, span]
        gs[dx, 0:8, RIGHT : RIGHT + 8, :] = result[:, 128:136, span]
        gs[dx, 0:8, LEFT:MAIN, :] = result[:, 136:144, span]
    for i in range(8):
        hb[i] = joined(i, MAIN, 128)
    store = pltpu.make_async_copy(hb, hb_ref, out_sem)
    store.start()
    mean, dev = local_stats([hb[i] for i in range(8)], ROWS_DEV * COLS_DEV)
    mean, inverse = all_reduce(1, mean, dev, lambda: None)
    fin_ref[0:1, :] = mean
    fin_ref[1:2, :] = inverse * vec_v[2:3, :]
    store.wait()

    pltpu.make_async_copy(tt.at[pl.ds(0, 2)], tt.at[pl.ds(0, 2)], send_sem.at[0]).wait()
    pltpu.make_async_copy(crit, crit, send_sem.at[1]).wait()
    pltpu.make_async_copy(far, far, send_sem.at[2]).wait()
    for turn in range(2):
        pltpu.make_async_copy(buf_x.at[turn], buf_x.at[turn], send_sem.at[3 + 2 * turn]).wait()
        pltpu.make_async_copy(buf_z.at[turn], buf_z.at[turn], send_sem.at[4 + 2 * turn]).wait()


def per_device(
    coarse, src_blocks, slot_counts, remap_tiles, conv_a, conv_b, gain_a, shift_a, gain_b, shift_b
):
    anywhere = pl.BlockSpec(memory_space=pl.ANY)
    scalar = pl.BlockSpec(memory_space=pltpu.SMEM)
    vectors = jnp.stack([gain_a, shift_a, gain_b, shift_b])
    hidden, final = pl.pallas_call(
        kernel,
        name="stem",
        out_shape=(
            jax.ShapeDtypeStruct((ROWS_DEV, COLS_DEV, CH), F32),
            jax.ShapeDtypeStruct((2, CH), F32),
        ),
        in_specs=[scalar, scalar, anywhere, anywhere, anywhere, anywhere, anywhere],
        out_specs=(anywhere, pl.BlockSpec(memory_space=pltpu.VMEM)),
        scratch_shapes=[
            pltpu.VMEM((BLK_DEV, VARS, BCELLS), BF16),
            pltpu.VMEM((128, 1024), BF16),
            pltpu.VMEM((3, 3, VARS, CH), F32),
            pltpu.VMEM((3, 3, CH, CH), F32),
            pltpu.VMEM((4, CH), F32),
            pltpu.VMEM((3, 16, 128), BF16),
            pltpu.VMEM((3, 32, 128), BF16),
            pltpu.VMEM((2, 32, 128), BF16),
            pltpu.VMEM((8, 32, 128), BF16),
            pltpu.VMEM((2, 32, 128), BF16),
            pltpu.VMEM((384, 128), BF16),
            pltpu.VMEM((128, 640), BF16),
            pltpu.VMEM((128, 3 * CH), F32),
            pltpu.VMEM((128, 3 * CH), BF16),
            pltpu.VMEM((9 * CH, 3 * CH), BF16),
            pltpu.VMEM((12, COLS_DEV, 128), BF16),
            pltpu.VMEM((3, 10, WIDE, CH), F32),
            pltpu.VMEM((10, WIDE, CH), F32),
            pltpu.VMEM((10, 144, 3 * CH), BF16),
            pltpu.VMEM((ROWS_DEV, COLS_DEV, CH), F32),
            pltpu.VMEM((2, 2, 2, CH), F32),
            pltpu.VMEM((2, 31, 2, CH), F32),
            pltpu.VMEM((2, 15, 2, CH), F32),
            pltpu.SemaphoreType.DMA((5,)),
            pltpu.SemaphoreType.DMA,
            pltpu.SemaphoreType.DMA((7,)),
            pltpu.SemaphoreType.DMA((8,)),
        ],
        compiler_params=pltpu.CompilerParams(
            collective_id=0, has_side_effects=True, vmem_limit_bytes=40 * 1024 * 1024
        ),
    )(
        src_blocks, slot_counts, coarse, remap_tiles.reshape(SLOTS * BCELLS, 1024),
        conv_a, conv_b, vectors,
    )
    normed = (hidden - final[0]) * final[1] + shift_b
    return jax.nn.silu(normed).astype(BF16)


def solution(mesh):
    return jax.shard_map(
        per_device,
        mesh=mesh,
        in_specs=(
            P("lon", None, None),
            P(("row", "lon"), None),
            P(("row", "lon")),
            P(("row", "lon"), None, None, None),
            P(),
            P(),
            P(),
            P(),
            P(),
            P(),
        ),
        out_specs=P("row", "lon", None),
        check_vma=False,
    )
```

time: 527 us -> 62.1 us (0.12)
  blocking collectives: 406 us -> 0 us
  starting transfers between devices: 76.1 us -> 0 us
  Pallas kernels: 0 us -> 55.3 us
  waiting for transfers between devices: 22.9 us -> 0 us
  matrix products: 15.3 us -> 0 us
    psum x4 -> x0, blocking collectives: 406 us -> none  [the longest x2 208 us: normalize(): average = lax.psum(group_totals(inside), ('row', 'lon')) / cell_count]
    ppermute x10 -> x0, starting transfers between devices: 76.1 us -> none  [the longest x5 40.2 us: with_halo(): lax.ppermute(head, axis, [((i + 1) % count, i) for i in range(ends)])]
    pallas_call x0 -> x1, Pallas kernels: none -> 55.3 us  [per_device(): pl.pallas_call(kernel, name='stem', out_shape=(jax.ShapeDtypeStruct((ROWS...]
    ppermute x10 -> x0, waiting for transfers between devices: 22.9 us -> none  [the longest x5 22.9 us: with_halo(): lax.ppermute(head, axis, [((i + 1) % count, i) for i in range(ends)])]
    dot_general x20 -> x0, matrix products: 15.3 us -> none  [the longest x9 9.5 us: conv_first(): jnp.einsum('vrc,vo->rco', window, weights[shift_row, shift_col], precisio...]
  transfers between devices with their start and end apart: 10 -> 0, of which waited for: 3 -> 0; matrix products, arithmetic and copies ran while one was open for 1% -> 0% of each run, Pallas kernels for 0% -> 0%
where the time goes in v1:
time: 62.1 us; the launch traced here: 61.8 us
  Pallas kernels  55.3 us (89%)
  local copies, waits for them, and re-layouts  4.2 us (7%)
  other arithmetic  1.58 us (3%)
  between operations  0.71 us (1%)
    pallas_call x1, Pallas kernels, per_device(): pl.pallas_call(kernel, name='stem', out_shape=(jax.ShapeDtypeStruct((ROWS...  55.3 us
    unnamed x13, local copies, waits for them, and re-layouts  4.19 us

profile of v1, /device:TPU:1, one launch (start us, length us, event | category | flops | bytes accessed | tf_op | source)
XLA Modules:
  0.0 61.8 jit_solution(15442425984249971143)
XLA Ops:
  0.0 0.0 copy-start.4
  0.7 0.7 %pad_maximum_fusion.vec_ref = f32[4,128]{1,0:T(4,128)S(1)} fusion(f32[1,128]{1,0:T(1,128)} %bitcast.10, f32[1,128]{1,0:T(1,128)} %bitcast.11, f32[1,128]{1,0:T(1,128)} %bitcast.12, f32[1,128]{1,0:T(1,128)} %bitcast.13), kind=kLoop, calls=%fused_computation.1 | loop fusion | flops 1536 | bytes 4096 | tf_op jit(solution)/shard_map/stack | solution.py:379
  1.4 0.0 copy-done.4
  1.4 0.0 copy-start.3
  1.4 0.6 %copy-done.3 = s32[1,4]{1,0:T(1,128)S(1)} copy-done((s32[1,4]{1,0:T(1,128)S(1)}, s32[1,4]{1,0:T(1,128)}, u32[]{:S(2)}) %copy-start.3) | copy-done | bytes 40
  2.0 0.0 copy-start
  2.0 1.1 %copy-done = f32[3,3,128,128]{3,2,1,0:T(8,128)S(1)} copy-done((f32[3,3,128,128]{3,2,1,0:T(8,128)S(1)}, f32[3,3,128,128]{3,2,1,0:T(8,128)}, u32[]{:S(2)}) %copy-start) | copy-done | bytes 589848
  3.1 0.0 copy-start.1
  3.1 0.9 %copy-done.1 = bf16[1,4,32,1024]{3,2,1,0:T(8,128)(2,1)S(1)} copy-done((bf16[1,4,32,1024]{3,2,1,0:T(8,128)(2,1)S(1)}, bf16[1,4,32,1024]{3,2,1,0:T(8,128)(2,1)}, u32[]{:S(2)}) %copy-start.1) | copy-done | bytes 262168
  4.1 0.0 copy-start.2
  4.1 0.9 %copy-done.2 = f32[3,3,12,128]{3,2,1,0:T(8,128)S(1)} copy-done((f32[3,3,12,128]{3,2,1,0:T(8,128)S(1)}, f32[3,3,12,128]{3,2,1,0:T(8,128)}, u32[]{:S(2)}) %copy-start.2) | copy-done | bytes 55320
  4.9 55.3 %stem.1 = (f32[8,128,128]{2,1,0:T(8,128)S(1)}, f32[2,128]{1,0:T(2,128)S(1)}) custom-call(s32[1,4]{1,0:T(1,128)S(1)} %copy-done.3, s32[1]{0:T(128)S(6)} %copy.12.cnt_ref, bf16[4,12,32]{2,1,0:T(8,128)(2,1)S(1)} %copy.11.coarse_ref, bf16[128,1024]{1,0:T(8,128)(2,1)S(1)} %bitcast.9, f32[3,3,12,128]{3,2,1,0:T(8,128)S(1)} %copy-done.2, ...), custom_call_target="tpu_custom_call" | custom-call | tf_op jit(solution)/shard_map/stem/pallas_call | solution.py:380
  60.3 0.0 copy-start.5
  60.3 0.6 %copy-done.5 = f32[128]{0:T(128)S(1)} copy-done((f32[128]{0:T(128)S(1)}, f32[128]{0:T(128)}, u32[]{:S(2)}) %copy-start.5) | copy-done | bytes 536
  60.9 0.9 %multiply_convert_fusion = bf16[8,128,128]{2,1,0:T(8,128)(2,1)} fusion(f32[8,128,128]{2,1,0:T(8,128)S(1)} %get-tuple-element.7, f32[128]{0:T(128)S(1)} %copy-done.5, f32[128]{0:T(128)S(1)} %get-tuple-element.10, f32[128]{0:T(128)S(1)} %get-tuple-element.9), kind=kLoop, calls=%fused_computation | loop fusion | flops 1048576 | bytes 787968 | tf_op jit(solution)/shard_map/convert_element_type | solution.py:426
  (2 shorter events, 0.0 us)
Async XLA Ops:
  0.0 1.4 %copy-start.4 = (bf16[4,12,32]{2,0,1:T(4,128)(2,1)S(1)}, bf16[4,12,32]{2,0,1:T(4,128)(2,1)}, u32[]{:S(2)}) copy-start(bf16[4,12,32]{2,0,1:T(4,128)(2,1)} %param.10) | copy-start | bytes 9220
  1.4 0.7 %copy-start.3 = (s32[1,4]{1,0:T(1,128)S(1)}, s32[1,4]{1,0:T(1,128)}, u32[]{:S(2)}) copy-start(s32[1,4]{1,0:T(1,128)} %src_ref.1) | copy-start | bytes 52
  2.0 1.1 %copy-start = (f32[3,3,128,128]{3,2,1,0:T(8,128)S(1)}, f32[3,3,128,128]{3,2,1,0:T(8,128)}, u32[]{:S(2)}) copy-start(f32[3,3,128,128]{3,2,1,0:T(8,128)} %cb_ref.1) | copy-start | bytes 1769476
  3.1 0.9 %copy-start.1 = (bf16[1,4,32,1024]{3,2,1,0:T(8,128)(2,1)S(1)}, bf16[1,4,32,1024]{3,2,1,0:T(8,128)(2,1)}, u32[]{:S(2)}) copy-start(bf16[1,4,32,1024]{3,2,1,0:T(8,128)(2,1)} %param.13) | copy-start | bytes 786436
  4.1 0.9 %copy-start.2 = (f32[3,3,12,128]{3,2,1,0:T(8,128)S(1)}, f32[3,3,12,128]{3,2,1,0:T(8,128)}, u32[]{:S(2)}) copy-start(f32[3,3,12,128]{3,2,1,0:T(8,128)} %ca_ref.1) | copy-start | bytes 165892
  60.3 0.7 %copy-start.5 = (f32[128]{0:T(128)S(1)}, f32[128]{0:T(128)}, u32[]{:S(2)}) copy-start(f32[128]{0:T(128)} %param.19) | copy-start | bytes 1540

commit v2 on v1

--- a/solution.py
+++ b/solution.py
@@ -43,15 +43,16 @@
 
 def along_z(place):
     _, _, x, y, z, core = place
-    steps = sorted(range(1, 16), key=lambda d: -min(d, 16 - d))
-    return [device_at(x, y, moved(z, d, 16), core) for d in steps]
+    steps = [(d, c) for d in range(16) for c in range(2) if d or c]
+    steps.sort(key=lambda s: -min(s[0], 16 - s[0]))
+    return [device_at(x, y, moved(z, d, 16), moved(core, c, 2)) for d, c in steps]
 
 
 def across(place):
     _, _, x, y, z, core = place
-    steps = [(a, b, c) for a in range(4) for b in range(4) for c in range(2) if a or b or c]
+    steps = [(a, b) for a in range(4) for b in range(4) if a or b]
     steps.sort(key=lambda s: -(min(s[0], 4 - s[0]) + min(s[1], 4 - s[1])))
-    return [device_at(moved(x, a, 4), moved(y, b, 4), z, moved(core, c, 2)) for a, b, c in steps]
+    return [device_at(moved(x, a, 4), moved(y, b, 4), z, core) for a, b in steps]
 
 
 def coarse_neighbours(place):
@@ -107,7 +108,7 @@
 
 
 def kernel(
-    src_ref, cnt_ref, coarse_ref, remap_ref, ca_ref, cb_ref, vec_ref,
+    src_ref, cnt_ref, coarse_ref, remap_ref, ca_ref, cb_ref, gain_a_ref, shift_a_ref, gain_b_ref, shift_b_ref,
     hb_ref, fin_ref,
     coarse_v, remap_v, ca_v, cb_v, vec_v,
     tt, crit_out, far_out, crit, far,
@@ -139,8 +140,9 @@
         pltpu.make_async_copy(remap_ref, remap_v, in_sem.at[1]),
         pltpu.make_async_copy(ca_ref, ca_v, in_sem.at[2]),
         pltpu.make_async_copy(cb_ref, cb_v, in_sem.at[3]),
-        pltpu.make_async_copy(vec_ref, vec_v, in_sem.at[4]),
     ]
+    for i, ref in enumerate((gain_a_ref, shift_a_ref, gain_b_ref, shift_b_ref)):
+        loads.append(pltpu.make_async_copy(ref, vec_v.at[i], in_sem.at[4 + i]))
     for load in loads:
         load.start()
 
@@ -153,10 +155,11 @@
     sel[...] = jnp.where(iota((3 * 128, 128), 0) == target, 1.0, 0.0).astype(BF16)
 
     loads[0].wait()
+    held = coarse_v[...].astype(F32)
     tile = jnp.zeros((VARS, 128), F32)
     for b in range(BLK_DEV):
         put = jnp.where(iota((BCELLS, 128), 0) + b * BCELLS == iota((BCELLS, 128), 1), 1.0, 0.0)
-        tile = tile + dot(coarse_v[b], put.astype(BF16))
+        tile = tile + dot(held[:, b, :].astype(BF16), put.astype(BF16))
     pad = jnp.concatenate([tile, jnp.zeros((16 - VARS, 128), F32)], axis=0)
     tt[1] = pad.astype(BF16)
 
@@ -262,7 +265,8 @@
             wb[dy * 384 : dy * 384 + 128, span] = high
             wb[dy * 384 + 128 : dy * 384 + 256, span] = high
             wb[dy * 384 + 256 : dy * 384 + 384, span] = low
-    loads[4].wait()
+    for load in loads[4:]:
+        load.wait()
 
     not_first = jnp.where(row > 0, 1.0, 0.0).astype(F32)
     not_last = jnp.where(row < 15, 1.0, 0.0).astype(F32)
@@ -294,7 +298,7 @@
 
     def all_reduce(turn, mean, dev, beside):
         cells = ROWS_DEV * COLS_DEV
-        for stage, (mates, buf) in enumerate(((xy_mates, buf_x), (z_mates, buf_z))):
+        for stage, (mates, buf) in enumerate(((z_mates, buf_z), (xy_mates, buf_x))):
             sem = 4 + turn * 2 + stage
             stat[turn, stage, 0:1, :] = mean
             stat[turn, stage, 1:2, :] = dev
@@ -326,8 +330,8 @@
     mean, dev = local_stats([ha[i, MAIN:RIGHT, :] for i in range(1, 9)], ROWS_DEV * COLS_DEV)
     mean, inverse = all_reduce(0, mean, dev, around_a)
 
-    scale = inverse * vec_v[0:1, :]
-    shift = vec_v[1:2, :]
+    scale = inverse * vec_v[0]
+    shift = vec_v[1]
     for i in range(10):
         for first, size, at in ((MAIN, 128, 0), (LEFT, 16, 128)):
             if size == 128:
@@ -360,15 +364,16 @@
     mean, dev = local_stats([hb[i] for i in range(8)], ROWS_DEV * COLS_DEV)
     mean, inverse = all_reduce(1, mean, dev, lambda: None)
     fin_ref[0:1, :] = mean
-    fin_ref[1:2, :] = inverse * vec_v[2:3, :]
+    fin_ref[1:2, :] = inverse * vec_v[2]
+    fin_ref[2:3, :] = vec_v[3]
     store.wait()
 
     pltpu.make_async_copy(tt.at[pl.ds(0, 2)], tt.at[pl.ds(0, 2)], send_sem.at[0]).wait()
     pltpu.make_async_copy(crit, crit, send_sem.at[1]).wait()
     pltpu.make_async_copy(far, far, send_sem.at[2]).wait()
     for turn in range(2):
-        pltpu.make_async_copy(buf_x.at[turn], buf_x.at[turn], send_sem.at[3 + 2 * turn]).wait()
-        pltpu.make_async_copy(buf_z.at[turn], buf_z.at[turn], send_sem.at[4 + 2 * turn]).wait()
+        pltpu.make_async_copy(buf_z.at[turn], buf_z.at[turn], send_sem.at[3 + 2 * turn]).wait()
+        pltpu.make_async_copy(buf_x.at[turn], buf_x.at[turn], send_sem.at[4 + 2 * turn]).wait()
 
 
 def per_device(
@@ -376,22 +381,22 @@
 ):
     anywhere = pl.BlockSpec(memory_space=pl.ANY)
     scalar = pl.BlockSpec(memory_space=pltpu.SMEM)
-    vectors = jnp.stack([gain_a, shift_a, gain_b, shift_b])
+    vectors = [v.reshape(1, CH) for v in (gain_a, shift_a, gain_b, shift_b)]
     hidden, final = pl.pallas_call(
         kernel,
         name="stem",
         out_shape=(
-            jax.ShapeDtypeStruct((ROWS_DEV, COLS_DEV, CH), F32),
-            jax.ShapeDtypeStruct((2, CH), F32),
+            pltpu.VMEM((ROWS_DEV, COLS_DEV, CH), F32),
+            pltpu.VMEM((3, CH), F32),
         ),
-        in_specs=[scalar, scalar, anywhere, anywhere, anywhere, anywhere, anywhere],
+        in_specs=[scalar, scalar] + [anywhere] * 8,
         out_specs=(anywhere, pl.BlockSpec(memory_space=pltpu.VMEM)),
         scratch_shapes=[
-            pltpu.VMEM((BLK_DEV, VARS, BCELLS), BF16),
+            pltpu.VMEM((VARS, BLK_DEV, BCELLS), BF16),
             pltpu.VMEM((128, 1024), BF16),
             pltpu.VMEM((3, 3, VARS, CH), F32),
             pltpu.VMEM((3, 3, CH, CH), F32),
-            pltpu.VMEM((4, CH), F32),
+            pltpu.VMEM((4, 1, CH), F32),
             pltpu.VMEM((3, 16, 128), BF16),
             pltpu.VMEM((3, 32, 128), BF16),
             pltpu.VMEM((2, 32, 128), BF16),
@@ -408,21 +413,21 @@
             pltpu.VMEM((10, 144, 3 * CH), BF16),
             pltpu.VMEM((ROWS_DEV, COLS_DEV, CH), F32),
             pltpu.VMEM((2, 2, 2, CH), F32),
+            pltpu.VMEM((2, 15, 2, CH), F32),
             pltpu.VMEM((2, 31, 2, CH), F32),
-            pltpu.VMEM((2, 15, 2, CH), F32),
-            pltpu.SemaphoreType.DMA((5,)),
+            pltpu.SemaphoreType.DMA((8,)),
             pltpu.SemaphoreType.DMA,
             pltpu.SemaphoreType.DMA((7,)),
             pltpu.SemaphoreType.DMA((8,)),
         ],
         compiler_params=pltpu.CompilerParams(
-            collective_id=0, has_side_effects=True, vmem_limit_bytes=40 * 1024 * 1024
+            collective_id=0, has_side_effects=True, vmem_limit_bytes=60 * 1024 * 1024
         ),
     )(
-        src_blocks, slot_counts, coarse, remap_tiles.reshape(SLOTS * BCELLS, 1024),
-        conv_a, conv_b, vectors,
+        src_blocks, slot_counts, jnp.transpose(coarse, (1, 0, 2)), remap_tiles.reshape(SLOTS * BCELLS, 1024),
+        conv_a, conv_b, *vectors,
     )
-    normed = (hidden - final[0]) * final[1] + shift_b
+    normed = (hidden - final[0]) * final[1] + final[2]
     return jax.nn.silu(normed).astype(BF16)
 
 

time: 62.1 us -> 57.4 us (0.924)
  local copies, waits for them, and re-layouts: 4.2 us -> 0.01 us
  other arithmetic: 1.58 us -> 0.87 us
    unnamed x13 -> x0, local copies, waits for them, and re-layouts: 4.19 us -> none
    another operation x1 -> x0, other arithmetic: 0.72 us -> none  [per_device(): vectors = jnp.stack([gain_a, shift_a, gain_b, shift_b])]
where the time goes in v2:
time: 57.4 us; the launch traced here: 57.2 us
  Pallas kernels  55.6 us (97%)
  other arithmetic  0.87 us (2%)
  between operations  0.67 us (1%)
    pallas_call x1, Pallas kernels, per_device(): pl.pallas_call(kernel, name='stem', out_shape=(pltpu.VMEM((ROWS_DEV, COLS...  55.6 us

profile of v2, /device:TPU:1, one launch (start us, length us, event | category | flops | bytes accessed | tf_op | source)
XLA Modules:
  0.0 57.2 jit_solution(5201827031633029553)
XLA Ops:
  0.7 55.6 %stem.1 = (f32[8,128,128]{2,1,0:T(8,128)S(1)}, f32[3,128]{1,0:T(4,128)S(1)}) custom-call(s32[1,4]{1,0:T(1,128)} %src_ref.1, s32[1]{0:T(128)S(6)} %copy.11.cnt_ref, bf16[12,4,32]{2,1,0:T(4,128)(2,1)} %bitcast.13, bf16[128,1024]{1,0:T(8,128)(2,1)} %bitcast.12, f32[3,3,12,128]{3,2,1,0:T(8,128)} %ca_ref.1, f32[3,3,128,128]{3,2,1,0:T(8,128)} %cb_ref.1, ...), custom_call_target="tpu_custom_call" | custom-call | tf_op jit(solution)/shard_map/stem/pallas_call | solution.py:385
  56.3 0.9 %multiply_convert_fusion = bf16[8,128,128]{2,1,0:T(8,128)(2,1)} fusion(f32[8,128,128]{2,1,0:T(8,128)S(1)} %get-tuple-element.7, f32[128]{0:T(128)S(1)} %get-tuple-element.10, f32[128]{0:T(128)S(1)} %get-tuple-element.11, f32[128]{0:T(128)S(1)} %get-tuple-element.9), kind=kLoop, calls=%fused_computation | loop fusion | flops 1048576 | bytes 787968 | tf_op jit(solution)/shard_map/convert_element_type | solution.py:431
  (1 shorter events, 0.0 us)

commit v3 on v2

--- a/solution.py
+++ b/solution.py
@@ -55,14 +55,14 @@
     return [device_at(moved(x, a, 4), moved(y, b, 4), z, core) for a, b in steps]
 
 
-def coarse_neighbours(place):
+def coarse_mates(place):
     _, _, x, y, z, core = place
     z_lo = lax.rem(z, 8)
-    y_up = lax.rem(y + lax.div(z_lo + 1, 8), 4)
-    y_down = lax.rem(y + 3 + lax.div(z_lo + 7, 8), 4)
-    up = device_at(x, y_up, lax.rem(z + 1, 16), core)
-    down = device_at(x, y_down, lax.rem(z + 15, 16), core)
-    return up, down
+    mates = []
+    for step in (2, 1, -1, -2):
+        turn = lax.rem(y + 3 + lax.div(z_lo + 8 + step, 8), 4)
+        mates.append(device_at(x, turn, lax.rem(z + 16 + step, 16), core))
+    return mates
 
 
 def iota(shape, dim):
@@ -111,8 +111,8 @@
     src_ref, cnt_ref, coarse_ref, remap_ref, ca_ref, cb_ref, gain_a_ref, shift_a_ref, gain_b_ref, shift_b_ref,
     hb_ref, fin_ref,
     coarse_v, remap_v, ca_v, cb_v, vec_v,
-    tt, crit_out, far_out, crit, far,
-    sel, edges, wa32, wa, wb,
+    tt, near_out, corner_out, far_out, near, corner, far,
+    copies, choices, wa32, wa, wb,
     xs, gs, ha, act, hb,
     stat, buf_x, buf_z,
     in_sem, out_sem, send_sem, recv_sem,
@@ -121,7 +121,7 @@
     row, lon = place[0], place[1]
     z_mates = along_z(place)
     xy_mates = across(place)
-    up, down = coarse_neighbours(place)
+    lon_mates = coarse_mates(place)
     row_up, row_down = lax.rem(row + 15, 16), lax.rem(row + 1, 16)
     lon_left, lon_right = lax.rem(lon + 31, 32), lax.rem(lon + 1, 32)
     halo = [
@@ -131,7 +131,7 @@
         (row_down, lon_left), (row_up, lon_left),
     ]
     barrier = pltpu.get_barrier_semaphore()
-    partners = halo + [up, down] + z_mates + xy_mates
+    partners = halo + lon_mates + z_mates + xy_mates
     for mate in partners:
         pl.semaphore_signal(barrier, inc=1, device_id=mate, device_id_type=MESH)
 
@@ -147,12 +147,16 @@
         load.start()
 
     lane = iota((1, 128), 1)
-    target = jnp.full((1, 128), -1, jnp.int32)
+    own_choice = jnp.zeros((1, 128), F32)
     for k in range(SLOTS):
         local = lax.rem(src_ref[0, k] - (lon - 1) * BLK_DEV + 2 * NBLK, NBLK)
-        first = jnp.where(k < cnt_ref[0], local * BCELLS, -1024)
-        target = jnp.where(lane // BCELLS == k, first + (lane & (BCELLS - 1)), target)
-    sel[...] = jnp.where(iota((3 * 128, 128), 0) == target, 1.0, 0.0).astype(BF16)
+        local = jnp.where(k < cnt_ref[0], local, -64)
+        own_choice = jnp.where((lane >> 5) == k, local.astype(F32), own_choice)
+    choice_tile = jnp.broadcast_to(own_choice, (16, 128)).astype(BF16)
+
+    for q in range(BLK_DEV):
+        want = q * BCELLS + (lane & (BCELLS - 1))
+        copies[:, q * 128 : (q + 1) * 128] = jnp.where(iota((128, 128), 0) == want, 1.0, 0.0).astype(BF16)
 
     loads[0].wait()
     held = coarse_v[...].astype(F32)
@@ -161,27 +165,26 @@
         put = jnp.where(iota((BCELLS, 128), 0) + b * BCELLS == iota((BCELLS, 128), 1), 1.0, 0.0)
         tile = tile + dot(held[:, b, :].astype(BF16), put.astype(BF16))
     pad = jnp.concatenate([tile, jnp.zeros((16 - VARS, 128), F32)], axis=0)
-    tt[1] = pad.astype(BF16)
+    tt[2] = pad.astype(BF16)
 
     loads[1].wait()
+    near_out[0, 0:128, :] = remap_v[:, 896:1024]
+    near_out[1, 0:128, :] = remap_v[:, 0:128]
     ri = lane >> 3
     ci = lane & 7
     col = jnp.where(ci == 6, 126, jnp.where(ci == 7, 127, jnp.where(ci < 2, ci, -4096)))
-    rw = jnp.where(ri < 2, ri + 6, jnp.where(ri < 10, ri - 2, jnp.where(ri < 12, ri - 10, -4096)))
+    rw = jnp.where((ri >= 2) & (ri < 10), ri - 2, -4096)
     cell = rw * COLS_DEV + col
     pick = jnp.where(iota((1024, 128), 0) == cell, 1.0, 0.0).astype(BF16)
-    edges[:, 512:640] = dot(remap_v[...], pick).astype(BF16)
-    edges[:, 0:256] = remap_v[:, 0:256]
-    edges[:, 256:512] = remap_v[:, 768:1024]
-
-    pl.semaphore_wait(barrier, len(partners))
-
-    for slot, mate in ((0, up), (2, down)):
-        pltpu.make_async_remote_copy(
-            src_ref=tt.at[1], dst_ref=tt.at[slot], send_sem=send_sem.at[0], recv_sem=recv_sem.at[0 if slot == 0 else 1],
-            device_id=mate, device_id_type=MESH,
-        ).start()
-    middle = dot(tt[1], sel[128:256, :])
+    near_out[2, 0:128, :] = dot(remap_v[...], pick).astype(BF16)
+    for i in range(3):
+        near_out[i, 128:144, :] = choice_tile
+    for i, (row0, col0) in enumerate(((6, 126), (0, 126), (6, 0), (0, 0))):
+        at = iota((16, 1024), 0)
+        cell = (row0 + (at >> 1)) * COLS_DEV + col0 + (at & 1)
+        pick = jnp.where((iota((16, 1024), 1) == cell) & (at < 4), 1.0, 0.0).astype(BF16)
+        cells = dot(pick, remap_v[...], ((1,), (1,)))
+        corner_out[i] = jnp.where(iota((16, 128), 0) < 8, cells, own_choice).astype(BF16)
 
     loads[2].wait()
     wa32[...] = jnp.zeros_like(wa32)
@@ -203,59 +206,35 @@
     want = jnp.where(part_l == 1, var_l + 16, var_l)
     spread_msg = jnp.where(iota((32, 128), 0) == want, 1.0, 0.0).astype(BF16)
     spread_var = jnp.where(iota((16, 128), 0) == var_l, 1.0, 0.0).astype(BF16)
-
-    for slot in (0, 2):
+    not_first = jnp.where(row > 0, 1.0, 0.0).astype(F32)
+    not_last = jnp.where(row < 15, 1.0, 0.0).astype(F32)
+
+    pl.semaphore_wait(barrier, len(partners))
+
+    for slot in (0, 1):
         pltpu.make_async_remote_copy(
-            src_ref=tt.at[1], dst_ref=tt.at[slot], send_sem=send_sem.at[0], recv_sem=recv_sem.at[0 if slot == 0 else 1],
-            device_id=up, device_id_type=MESH,
-        ).wait_recv()
-    blocks = middle + dot(tt[0], sel[0:128, :]) + dot(tt[2], sel[256:384, :])
-    blocks = blocks.astype(BF16)
-
-    fine_edges = dot(blocks, edges[...])
-    high, low = split(fine_edges)
-    for slot, first in ((0, 384), (1, 0), (2, 512)):
-        crit_out[slot, 0:16, :] = high[:, first : first + 128]
-        crit_out[slot, 16:32, :] = low[:, first : first + 128]
-    for slot, first in ((0, 256), (1, 128)):
-        far_out[slot, 0:16, :] = high[:, first : first + 128]
-        far_out[slot, 16:32, :] = low[:, first : first + 128]
-    for slot, mate in enumerate(halo):
-        pltpu.make_async_remote_copy(
-            src_ref=crit_out.at[min(slot, 2)], dst_ref=crit.at[slot], send_sem=send_sem.at[1], recv_sem=recv_sem.at[2],
-            device_id=mate, device_id_type=MESH,
-        ).start()
-    for slot in range(2):
-        pltpu.make_async_remote_copy(
-            src_ref=far_out.at[slot], dst_ref=far.at[slot], send_sem=send_sem.at[2], recv_sem=recv_sem.at[3],
+            src_ref=near_out.at[slot], dst_ref=near.at[slot], send_sem=send_sem.at[0], recv_sem=recv_sem.at[0],
             device_id=halo[slot], device_id_type=MESH,
         ).start()
-
-    spread_blocks = dot(blocks, spread_var, ((0,), (0,))).astype(BF16)
-    fine = dot(remap_v[...], spread_blocks, ((0,), (0,)))
-    high, low = split(fine)
-    packed = jnp.where(part_l == 1, low.astype(F32), high.astype(F32)).astype(BF16)
-    xs[2:10] = packed.reshape(ROWS_DEV, COLS_DEV, 128)
-
-    third = jnp.broadcast_to(lane, (128, 128))
-
-    def patches(before, here, after, lanes):
-        before = jnp.where(lanes < 3 * VARS, before.astype(F32), 0.0)
-        here = jnp.where((lanes >= 3 * VARS) & (lanes < 6 * VARS), here.astype(F32), 0.0)
-        after = jnp.where(lanes >= 6 * VARS, after.astype(F32), 0.0)
-        return (before + here + after).astype(BF16)
-
-    def taps(out_rows):
-        field = [patches(xs[i], xs[i + 1], xs[i + 2], third) for i in out_rows]
-        result = dot(jnp.concatenate(field, axis=0), wa[...])
-        for n, i in enumerate(out_rows):
-            for dx in range(3):
-                gs[dx, i, MAIN:RIGHT, :] = result[n * 128 : (n + 1) * 128, dx * CH : (dx + 1) * CH]
-
-    def joined(i, first, size):
-        return gs[0, i, first - 1 : first - 1 + size, :] + gs[1, i, first : first + size, :] + gs[2, i, first + 1 : first + 1 + size, :]
-
-    taps(list(range(2, 8)))
+    for slot in range(4):
+        pltpu.make_async_remote_copy(
+            src_ref=corner_out.at[slot], dst_ref=corner.at[slot], send_sem=send_sem.at[1], recv_sem=recv_sem.at[1],
+            device_id=halo[4 + slot], device_id_type=MESH,
+        ).start()
+    for slot in (2, 3):
+        pltpu.make_async_remote_copy(
+            src_ref=near_out.at[2], dst_ref=near.at[slot], send_sem=send_sem.at[0], recv_sem=recv_sem.at[0],
+            device_id=halo[slot], device_id_type=MESH,
+        ).start()
+    along_lon = [
+        pltpu.make_async_remote_copy(
+            src_ref=tt.at[2], dst_ref=tt.at[slot], send_sem=send_sem.at[7], recv_sem=recv_sem.at[8 + i],
+            device_id=mate, device_id_type=MESH,
+        )
+        for i, (slot, mate) in enumerate(zip((0, 1, 3, 4), lon_mates))
+    ]
+    for copy in along_lon:
+        copy.start()
 
     loads[3].wait()
     for dy in range(3):
@@ -268,19 +247,74 @@
     for load in loads[4:]:
         load.wait()
 
-    not_first = jnp.where(row > 0, 1.0, 0.0).astype(F32)
-    not_last = jnp.where(row < 15, 1.0, 0.0).astype(F32)
-    pltpu.make_async_copy(crit, crit, recv_sem.at[2]).wait()
-    top = crit[0].astype(F32) * not_first
-    bottom = crit[1].astype(F32) * not_last
-    left = jnp.where(
-        ri < 2, crit[4].astype(F32) * not_first, jnp.where(ri < 10, crit[2].astype(F32), crit[5].astype(F32) * not_last)
-    )
-    right = jnp.where(
-        ri < 2, crit[6].astype(F32) * not_first, jnp.where(ri < 10, crit[3].astype(F32), crit[7].astype(F32) * not_last)
-    )
-    sides = jnp.where(ci >= 4, left, right)
-    around = jnp.concatenate([top, bottom, sides], axis=1).astype(BF16)
+    for copy in along_lon:
+        copy.wait_recv()
+    choices[...] = dot(tt[...].reshape(80, 128), copies[...])
+
+    def chosen(choice, first_tile):
+        total = jnp.zeros((16, 128), F32)
+        for j in range(3 * BLK_DEV):
+            t, q = first_tile + j // BLK_DEV, j % BLK_DEV
+            total = jnp.where(choice == j, choices[t * 16 : t * 16 + 16, q * 128 : (q + 1) * 128], total)
+        return total
+
+    blocks = chosen(own_choice, 1).astype(BF16)
+
+    for slot, first in ((0, 768), (1, 128)):
+        high, low = split(dot(blocks, remap_v[:, first : first + 128]))
+        far_out[slot, 0:16, :] = high
+        far_out[slot, 16:32, :] = low
+        pltpu.make_async_remote_copy(
+            src_ref=far_out.at[slot], dst_ref=far.at[slot], send_sem=send_sem.at[2], recv_sem=recv_sem.at[3],
+            device_id=halo[slot], device_id_type=MESH,
+        ).start()
+
+    spread_blocks = dot(blocks, spread_var, ((0,), (0,))).astype(BF16)
+    fine = dot(remap_v[...], spread_blocks, ((0,), (0,)))
+    high, low = split(fine)
+    packed = jnp.where(part_l == 1, low.astype(F32), high.astype(F32)).astype(BF16)
+    xs[2:10] = packed.reshape(ROWS_DEV, COLS_DEV, 128)
+
+    third = jnp.broadcast_to(lane, (128, 128))
+
+    def patches(before, here, after, lanes):
+        before = jnp.where(lanes < 3 * VARS, before.astype(F32), 0.0)
+        here = jnp.where((lanes >= 3 * VARS) & (lanes < 6 * VARS), here.astype(F32), 0.0)
+        after = jnp.where(lanes >= 6 * VARS, after.astype(F32), 0.0)
+        return (before + here + after).astype(BF16)
+
+    def taps(out_rows):
+        field = [patches(xs[i], xs[i + 1], xs[i + 2], third) for i in out_rows]
+        result = dot(jnp.concatenate(field, axis=0), wa[...])
+        for n, i in enumerate(out_rows):
+            for dx in range(3):
+                gs[dx, i, MAIN:RIGHT, :] = result[n * 128 : (n + 1) * 128, dx * CH : (dx + 1) * CH]
+
+    def joined(i, first, size):
+        return gs[0, i, first - 1 : first - 1 + size, :] + gs[1, i, first : first + size, :] + gs[2, i, first + 1 : first + 1 + size, :]
+
+    taps(list(range(2, 8)))
+
+    pltpu.make_async_copy(corner, corner, recv_sem.at[1]).wait()
+    pltpu.make_async_copy(near, near, recv_sem.at[0]).wait()
+
+    def near_fine(slot, first_tile):
+        held = chosen(near[slot, 128:129, :].astype(F32), first_tile)
+        return dot(held.astype(BF16), near[slot, 0:128, :])
+
+    top = near_fine(0, 1) * not_first
+    bottom = near_fine(1, 1) * not_last
+    sides = jnp.where(ci >= 4, near_fine(2, 0), near_fine(3, 2))
+    for slot, first_tile, known, first_lane in (
+        (0, 0, not_first, 6), (1, 0, not_last, 86), (2, 2, not_first, 0), (3, 2, not_last, 80),
+    ):
+        tile = corner[slot].astype(F32)
+        held = chosen(tile[8:9, :], first_tile) * known
+        for n in range(4):
+            value = jnp.sum(held * tile[n : n + 1, :], axis=1, keepdims=True)
+            sides = jnp.where(lane == first_lane + (n >> 1) * 8 + (n & 1), value, sides)
+    high, low = split(jnp.concatenate([top, bottom, sides], axis=1))
+    around = jnp.concatenate([high, low], axis=0)
     placed = dot(around, spread_msg, ((0,), (0,))).astype(BF16)
     xs[1] = placed[0:128]
     xs[10] = placed[128:256]
@@ -368,8 +402,9 @@
     fin_ref[2:3, :] = vec_v[3]
     store.wait()
 
-    pltpu.make_async_copy(tt.at[pl.ds(0, 2)], tt.at[pl.ds(0, 2)], send_sem.at[0]).wait()
-    pltpu.make_async_copy(crit, crit, send_sem.at[1]).wait()
+    pltpu.make_async_copy(near, near, send_sem.at[0]).wait()
+    pltpu.make_async_copy(corner, corner, send_sem.at[1]).wait()
+    pltpu.make_async_copy(tt.at[pl.ds(0, 4)], tt.at[pl.ds(0, 4)], send_sem.at[7]).wait()
     pltpu.make_async_copy(far, far, send_sem.at[2]).wait()
     for turn in range(2):
         pltpu.make_async_copy(buf_z.at[turn], buf_z.at[turn], send_sem.at[3 + 2 * turn]).wait()
@@ -397,13 +432,15 @@
             pltpu.VMEM((3, 3, VARS, CH), F32),
             pltpu.VMEM((3, 3, CH, CH), F32),
             pltpu.VMEM((4, 1, CH), F32),
-            pltpu.VMEM((3, 16, 128), BF16),
-            pltpu.VMEM((3, 32, 128), BF16),
+            pltpu.VMEM((5, 16, 128), BF16),
+            pltpu.VMEM((3, 144, 128), BF16),
+            pltpu.VMEM((4, 16, 128), BF16),
             pltpu.VMEM((2, 32, 128), BF16),
-            pltpu.VMEM((8, 32, 128), BF16),
+            pltpu.VMEM((4, 144, 128), BF16),
+            pltpu.VMEM((4, 16, 128), BF16),
             pltpu.VMEM((2, 32, 128), BF16),
-            pltpu.VMEM((384, 128), BF16),
-            pltpu.VMEM((128, 640), BF16),
+            pltpu.VMEM((128, BLK_DEV * 128), BF16),
+            pltpu.VMEM((80, BLK_DEV * 128), F32),
             pltpu.VMEM((128, 3 * CH), F32),
             pltpu.VMEM((128, 3 * CH), BF16),
             pltpu.VMEM((9 * CH, 3 * CH), BF16),
@@ -417,8 +454,8 @@
             pltpu.VMEM((2, 31, 2, CH), F32),
             pltpu.SemaphoreType.DMA((8,)),
             pltpu.SemaphoreType.DMA,
-            pltpu.SemaphoreType.DMA((7,)),
             pltpu.SemaphoreType.DMA((8,)),
+            pltpu.SemaphoreType.DMA((12,)),
         ],
         compiler_params=pltpu.CompilerParams(
             collective_id=0, has_side_effects=True, vmem_limit_bytes=60 * 1024 * 1024

time: 57.4 us -> 56.9 us (level)
  no operation moved by 1% of the time
where the time goes in v3:
time: 56.9 us; the launch traced here: 56.7 us
  Pallas kernels  55.2 us (97%)
  other arithmetic  0.87 us (2%)
  between operations  0.67 us (1%)
    pallas_call x1, Pallas kernels, per_device(): pl.pallas_call(kernel, name='stem', out_shape=(pltpu.VMEM((ROWS_DEV, COLS...  55.2 us

profile of v3, /device:TPU:1, one launch (start us, length us, event | category | flops | bytes accessed | tf_op | source)
XLA Modules:
  0.0 56.7 jit_solution(16823719755726144979)
XLA Ops:
  0.7 55.2 %stem.1 = (f32[8,128,128]{2,1,0:T(8,128)S(1)}, f32[3,128]{1,0:T(4,128)S(1)}) custom-call(s32[1,4]{1,0:T(1,128)} %src_ref.1, s32[1]{0:T(128)S(6)} %copy.11.cnt_ref, bf16[12,4,32]{2,1,0:T(4,128)(2,1)} %bitcast.13, bf16[128,1024]{1,0:T(8,128)(2,1)} %bitcast.12, f32[3,3,12,128]{3,2,1,0:T(8,128)} %ca_ref.1, f32[3,3,128,128]{3,2,1,0:T(8,128)} %cb_ref.1, ...), custom_call_target="tpu_custom_call" | custom-call | tf_op jit(solution)/shard_map/stem/pallas_call | solution.py:420
  55.8 0.9 %multiply_convert_fusion = bf16[8,128,128]{2,1,0:T(8,128)(2,1)} fusion(f32[8,128,128]{2,1,0:T(8,128)S(1)} %get-tuple-element.7, f32[128]{0:T(128)S(1)} %get-tuple-element.10, f32[128]{0:T(128)S(1)} %get-tuple-element.11, f32[128]{0:T(128)S(1)} %get-tuple-element.9), kind=kLoop, calls=%fused_computation | loop fusion | flops 1048576 | bytes 787968 | tf_op jit(solution)/shard_map/convert_element_type | solution.py:468
  (1 shorter events, 0.0 us)

commit v4 on v3

--- a/solution.py
+++ b/solution.py
@@ -111,8 +111,9 @@
     src_ref, cnt_ref, coarse_ref, remap_ref, ca_ref, cb_ref, gain_a_ref, shift_a_ref, gain_b_ref, shift_b_ref,
     hb_ref, fin_ref,
     coarse_v, remap_v, ca_v, cb_v, vec_v,
-    tt, near_out, corner_out, far_out, near, corner, far,
-    copies, choices, wa32, wa, wb,
+    tt, row_out, col_out, corner_out, mate_out, next_out,
+    row_in, col_in, corner_in, mate_in, next_in,
+    copies, choices, side, wa32, wa, wb,
     xs, gs, ha, act, hb,
     stat, buf_x, buf_z,
     in_sem, out_sem, send_sem, recv_sem,
@@ -130,6 +131,9 @@
         (row_down, lon_right), (row_up, lon_right),
         (row_down, lon_left), (row_up, lon_left),
     ]
+    odd = lax.rem(row, 2)
+    core_mate = (row + 1 - 2 * odd, lon)
+    far_mate = (lax.rem(row + 2 * odd + 15, 16), lon)
     barrier = pltpu.get_barrier_semaphore()
     partners = halo + lon_mates + z_mates + xy_mates
     for mate in partners:
@@ -168,23 +172,26 @@
     tt[2] = pad.astype(BF16)
 
     loads[1].wait()
-    near_out[0, 0:128, :] = remap_v[:, 896:1024]
-    near_out[1, 0:128, :] = remap_v[:, 0:128]
-    ri = lane >> 3
-    ci = lane & 7
-    col = jnp.where(ci == 6, 126, jnp.where(ci == 7, 127, jnp.where(ci < 2, ci, -4096)))
-    rw = jnp.where((ri >= 2) & (ri < 10), ri - 2, -4096)
-    cell = rw * COLS_DEV + col
-    pick = jnp.where(iota((1024, 128), 0) == cell, 1.0, 0.0).astype(BF16)
-    near_out[2, 0:128, :] = dot(remap_v[...], pick).astype(BF16)
-    for i in range(3):
-        near_out[i, 128:144, :] = choice_tile
+    at = iota((224, 1), 0)
+    inner = at & 15
+    cell = jnp.where(at < 128, at + odd * (7 * COLS_DEV), -1)
+    column = (inner & 7) * COLS_DEV + (inner >> 3)
+    cell = jnp.where((at >= 128) & (at < 144), column + 126, cell)
+    cell = jnp.where((at >= 144) & (at < 160), column, cell)
     for i, (row0, col0) in enumerate(((6, 126), (0, 126), (6, 0), (0, 0))):
-        at = iota((16, 1024), 0)
-        cell = (row0 + (at >> 1)) * COLS_DEV + col0 + (at & 1)
-        pick = jnp.where((iota((16, 1024), 1) == cell) & (at < 4), 1.0, 0.0).astype(BF16)
-        cells = dot(pick, remap_v[...], ((1,), (1,)))
+        here = (at >= 160 + 16 * i) & (at < 164 + 16 * i)
+        cell = jnp.where(here, (row0 + (inner >> 1)) * COLS_DEV + col0 + (inner & 1), cell)
+    pick = jnp.where(iota((224, 1024), 1) == cell, 1.0, 0.0).astype(BF16)
+    weights = dot(pick, remap_v[...], ((1,), (1,))).astype(BF16)
+    row_out[0:128, :] = weights[0:128]
+    row_out[128:144, :] = choice_tile
+    for i in range(2):
+        col_out[i, 0:16, :] = weights[128 + 16 * i : 144 + 16 * i]
+        col_out[i, 16:32, :] = choice_tile
+    for i in range(4):
+        cells = weights[160 + 16 * i : 176 + 16 * i].astype(F32)
         corner_out[i] = jnp.where(iota((16, 128), 0) < 8, cells, own_choice).astype(BF16)
+    side[...] = jnp.zeros_like(side)
 
     loads[2].wait()
     wa32[...] = jnp.zeros_like(wa32)
@@ -211,21 +218,18 @@
 
     pl.semaphore_wait(barrier, len(partners))
 
-    for slot in (0, 1):
-        pltpu.make_async_remote_copy(
-            src_ref=near_out.at[slot], dst_ref=near.at[slot], send_sem=send_sem.at[0], recv_sem=recv_sem.at[0],
-            device_id=halo[slot], device_id_type=MESH,
-        ).start()
-    for slot in range(4):
-        pltpu.make_async_remote_copy(
-            src_ref=corner_out.at[slot], dst_ref=corner.at[slot], send_sem=send_sem.at[1], recv_sem=recv_sem.at[1],
-            device_id=halo[4 + slot], device_id_type=MESH,
-        ).start()
-    for slot in (2, 3):
-        pltpu.make_async_remote_copy(
-            src_ref=near_out.at[2], dst_ref=near.at[slot], send_sem=send_sem.at[0], recv_sem=recv_sem.at[0],
-            device_id=halo[slot], device_id_type=MESH,
-        ).start()
+    def send(src, dst, mate, out, into):
+        copy = pltpu.make_async_remote_copy(
+            src_ref=src, dst_ref=dst, send_sem=send_sem.at[out], recv_sem=recv_sem.at[into],
+            device_id=mate, device_id_type=MESH,
+        )
+        copy.start()
+
+    send(row_out, row_in, far_mate, 0, 0)
+    for i in range(4):
+        send(corner_out.at[i], corner_in.at[i], halo[4 + i], 1, 1)
+    for i in range(2):
+        send(col_out.at[i], col_in.at[i], halo[2 + i], 8, 2)
     along_lon = [
         pltpu.make_async_remote_copy(
             src_ref=tt.at[2], dst_ref=tt.at[slot], send_sem=send_sem.at[7], recv_sem=recv_sem.at[8 + i],
@@ -260,14 +264,14 @@
 
     blocks = chosen(own_choice, 1).astype(BF16)
 
-    for slot, first in ((0, 768), (1, 128)):
-        high, low = split(dot(blocks, remap_v[:, first : first + 128]))
-        far_out[slot, 0:16, :] = high
-        far_out[slot, 16:32, :] = low
-        pltpu.make_async_remote_copy(
-            src_ref=far_out.at[slot], dst_ref=far.at[slot], send_sem=send_sem.at[2], recv_sem=recv_sem.at[3],
-            device_id=halo[slot], device_id_type=MESH,
-        ).start()
+    four = jnp.concatenate([remap_v[:, 0:256], remap_v[:, 768:1024]], axis=1)
+    four = dot(blocks, four)
+    is_odd = odd == 1
+    mate_out[0] = jnp.where(is_odd, four[:, 0:128], four[:, 384:512])
+    mate_out[1] = jnp.where(is_odd, four[:, 128:256], four[:, 256:384])
+    next_out[...] = jnp.where(is_odd, four[:, 256:384], four[:, 128:256])
+    send(mate_out, mate_in, core_mate, 2, 3)
+    send(next_out, next_in, far_mate, 9, 12)
 
     spread_blocks = dot(blocks, spread_var, ((0,), (0,))).astype(BF16)
     fine = dot(remap_v[...], spread_blocks, ((0,), (0,)))
@@ -295,32 +299,44 @@
 
     taps(list(range(2, 8)))
 
-    pltpu.make_async_copy(corner, corner, recv_sem.at[1]).wait()
-    pltpu.make_async_copy(near, near, recv_sem.at[0]).wait()
-
-    def near_fine(slot, first_tile):
-        held = chosen(near[slot, 128:129, :].astype(F32), first_tile)
-        return dot(held.astype(BF16), near[slot, 0:128, :])
-
-    top = near_fine(0, 1) * not_first
-    bottom = near_fine(1, 1) * not_last
-    sides = jnp.where(ci >= 4, near_fine(2, 0), near_fine(3, 2))
-    for slot, first_tile, known, first_lane in (
-        (0, 0, not_first, 6), (1, 0, not_last, 86), (2, 2, not_first, 0), (3, 2, not_last, 80),
-    ):
-        tile = corner[slot].astype(F32)
-        held = chosen(tile[8:9, :], first_tile) * known
+    def placed(fine):
+        high, low = split(fine)
+        return dot(jnp.concatenate([high, low], axis=0), spread_msg, ((0,), (0,))).astype(BF16)
+
+    pltpu.make_async_copy(mate_in, mate_in, recv_sem.at[3]).wait()
+    xs[10 - 9 * odd] = placed(mate_in[0])
+    xs[11 - 11 * odd] = placed(mate_in[1])
+
+    pltpu.make_async_copy(col_in, col_in, recv_sem.at[2]).wait()
+    pltpu.make_async_copy(corner_in, corner_in, recv_sem.at[1]).wait()
+    pltpu.make_async_copy(row_in, row_in, recv_sem.at[0]).wait()
+    far_known = jnp.where(is_odd, not_last, not_first)
+
+    def fine_of(cells, choice, first_tile, known):
+        held = chosen(choice.astype(F32), first_tile) * known
+        return dot(cells, held.astype(BF16), ((1,), (1,)))
+
+    parts = [
+        fine_of(row_in[0:128, :], row_in[128:129, :], 1, far_known),
+        fine_of(col_in[0, 0:16, :], col_in[0, 16:17, :], 0, 1.0),
+        fine_of(col_in[1, 0:16, :], col_in[1, 16:17, :], 2, 1.0),
+    ]
+    for i, (first_tile, known) in enumerate(((0, not_first), (0, not_last), (2, not_first), (2, not_last))):
+        parts.append(fine_of(corner_in[i], corner_in[i, 8:9, :], first_tile, known))
+    high, low = split(jnp.concatenate(parts, axis=0))
+    cells = dot(jnp.concatenate([high, low], axis=1), spread_msg)
+    xs[1 + 9 * odd] = cells[0:128].astype(BF16)
+    for i, first in enumerate((6, 0)):
+        for n in range(16):
+            line = ((n & 7) + 2) * 8 + first + (n >> 3)
+            side[line : line + 1, :] = cells[128 + 16 * i + n : 129 + 16 * i + n]
+    for i, first in enumerate((6, 86, 0, 80)):
         for n in range(4):
-            value = jnp.sum(held * tile[n : n + 1, :], axis=1, keepdims=True)
-            sides = jnp.where(lane == first_lane + (n >> 1) * 8 + (n & 1), value, sides)
-    high, low = split(jnp.concatenate([top, bottom, sides], axis=1))
-    around = jnp.concatenate([high, low], axis=0)
-    placed = dot(around, spread_msg, ((0,), (0,))).astype(BF16)
-    xs[1] = placed[0:128]
-    xs[10] = placed[128:256]
-    side = placed[256:352].astype(F32).reshape(12, 8, 128)
+            line = first + (n >> 1) * 8 + (n & 1)
+            side[line : line + 1, :] = cells[160 + 16 * i + n : 161 + 16 * i + n]
+    edge = side[...].reshape(12, 8, 128)
     side_lane = jnp.broadcast_to(lane.reshape(1, 1, 128), (10, 8, 128))
-    side_patches = patches(side[0:10], side[1:11], side[2:12], side_lane).reshape(80, 128)
+    side_patches = patches(edge[0:10], edge[1:11], edge[2:12], side_lane).reshape(80, 128)
     side_taps = dot(side_patches, wa[...]).reshape(10, 8, 3 * CH)
     for dx in range(3):
         piece = side_taps[:, :, dx * CH : (dx + 1) * CH]
@@ -349,11 +365,8 @@
         return mean, lax.rsqrt(dev * (1.0 / (cells * PER_GROUP)) + eps)
 
     def around_a():
-        pltpu.make_async_copy(far, far, recv_sem.at[3]).wait()
-        beyond = jnp.concatenate([far[0].astype(F32) * not_first, far[1].astype(F32) * not_last], axis=1).astype(BF16)
-        placed = dot(beyond, spread_msg, ((0,), (0,))).astype(BF16)
-        xs[0] = placed[0:128]
-        xs[11] = placed[128:256]
+        pltpu.make_async_copy(next_in, next_in, recv_sem.at[12]).wait()
+        xs[11 * odd] = placed(next_in[...] * far_known)
         taps([0, 9])
         for i in (0, 9):
             ha[i, MAIN:RIGHT, :] = joined(i, MAIN, 128)
@@ -402,10 +415,12 @@
     fin_ref[2:3, :] = vec_v[3]
     store.wait()
 
-    pltpu.make_async_copy(near, near, send_sem.at[0]).wait()
-    pltpu.make_async_copy(corner, corner, send_sem.at[1]).wait()
+    pltpu.make_async_copy(row_in, row_in, send_sem.at[0]).wait()
+    pltpu.make_async_copy(corner_in, corner_in, send_sem.at[1]).wait()
+    pltpu.make_async_copy(col_in, col_in, send_sem.at[8]).wait()
+    pltpu.make_async_copy(mate_in, mate_in, send_sem.at[2]).wait()
+    pltpu.make_async_copy(next_in, next_in, send_sem.at[9]).wait()
     pltpu.make_async_copy(tt.at[pl.ds(0, 4)], tt.at[pl.ds(0, 4)], send_sem.at[7]).wait()
-    pltpu.make_async_copy(far, far, send_sem.at[2]).wait()
     for turn in range(2):
         pltpu.make_async_copy(buf_z.at[turn], buf_z.at[turn], send_sem.at[3 + 2 * turn]).wait()
         pltpu.make_async_copy(buf_x.at[turn], buf_x.at[turn], send_sem.at[4 + 2 * turn]).wait()
@@ -433,14 +448,19 @@
             pltpu.VMEM((3, 3, CH, CH), F32),
             pltpu.VMEM((4, 1, CH), F32),
             pltpu.VMEM((5, 16, 128), BF16),
-            pltpu.VMEM((3, 144, 128), BF16),
+            pltpu.VMEM((144, 128), BF16),
+            pltpu.VMEM((2, 32, 128), BF16),
             pltpu.VMEM((4, 16, 128), BF16),
+            pltpu.VMEM((2, 16, 128), F32),
+            pltpu.VMEM((16, 128), F32),
+            pltpu.VMEM((144, 128), BF16),
             pltpu.VMEM((2, 32, 128), BF16),
-            pltpu.VMEM((4, 144, 128), BF16),
             pltpu.VMEM((4, 16, 128), BF16),
-            pltpu.VMEM((2, 32, 128), BF16),
+            pltpu.VMEM((2, 16, 128), F32),
+            pltpu.VMEM((16, 128), F32),
             pltpu.VMEM((128, BLK_DEV * 128), BF16),
             pltpu.VMEM((80, BLK_DEV * 128), F32),
+            pltpu.VMEM((96, 128), F32),
             pltpu.VMEM((128, 3 * CH), F32),
             pltpu.VMEM((128, 3 * CH), BF16),
             pltpu.VMEM((9 * CH, 3 * CH), BF16),
@@ -454,8 +474,8 @@
             pltpu.VMEM((2, 31, 2, CH), F32),
             pltpu.SemaphoreType.DMA((8,)),
             pltpu.SemaphoreType.DMA,
-            pltpu.SemaphoreType.DMA((8,)),
-            pltpu.SemaphoreType.DMA((12,)),
+            pltpu.SemaphoreType.DMA((10,)),
+            pltpu.SemaphoreType.DMA((13,)),
         ],
         compiler_params=pltpu.CompilerParams(
             collective_id=0, has_side_effects=True, vmem_limit_bytes=60 * 1024 * 1024

time: 56.9 us -> 56.2 us (0.988)
  Pallas kernels: 55.2 us -> 54.5 us
    pallas_call x1, Pallas kernels: 55.2 us -> 54.5 us  [per_device(): pl.pallas_call(kernel, name='stem', out_shape=(pltpu.VMEM((ROWS_DEV, COLS...]
where the time goes in v4:
time: 56.2 us; the launch traced here: 56.1 us
  Pallas kernels  54.5 us (97%)
  other arithmetic  0.87 us (2%)
  between operations  0.67 us (1%)
    pallas_call x1, Pallas kernels, per_device(): pl.pallas_call(kernel, name='stem', out_shape=(pltpu.VMEM((ROWS_DEV, COLS...  54.5 us

profile of v4, /device:TPU:1, one launch (start us, length us, event | category | flops | bytes accessed | tf_op | source)
XLA Modules:
  0.0 56.1 jit_solution(592476390868663700)
XLA Ops:
  0.7 54.5 %stem.1 = (f32[8,128,128]{2,1,0:T(8,128)S(1)}, f32[3,128]{1,0:T(4,128)S(1)}) custom-call(s32[1,4]{1,0:T(1,128)} %src_ref.1, s32[1]{0:T(128)S(6)} %copy.11.cnt_ref, bf16[12,4,32]{2,1,0:T(4,128)(2,1)} %bitcast.13, bf16[128,1024]{1,0:T(8,128)(2,1)} %bitcast.12, f32[3,3,12,128]{3,2,1,0:T(8,128)} %ca_ref.1, f32[3,3,128,128]{3,2,1,0:T(8,128)} %cb_ref.1, ...), custom_call_target="tpu_custom_call" | custom-call | tf_op jit(solution)/shard_map/stem/pallas_call | solution.py:435
  55.2 0.9 %multiply_convert_fusion = bf16[8,128,128]{2,1,0:T(8,128)(2,1)} fusion(f32[8,128,128]{2,1,0:T(8,128)S(1)} %get-tuple-element.7, f32[128]{0:T(128)S(1)} %get-tuple-element.10, f32[128]{0:T(128)S(1)} %get-tuple-element.11, f32[128]{0:T(128)S(1)} %get-tuple-element.9), kind=kLoop, calls=%fused_computation | loop fusion | flops 1048576 | bytes 787968 | tf_op jit(solution)/shard_map/convert_element_type | solution.py:488
  (1 shorter events, 0.0 us)

commit v5 on v4

--- a/solution.py
+++ b/solution.py
@@ -80,18 +80,34 @@
 
 
 def over_group(row):
-    lane = iota(row.shape, 1)
-    near = jnp.where((lane & 1) == 0, pltpu.roll(row, CH - 1, 1), pltpu.roll(row, 1, 1))
-    row = row + near
-    far = jnp.where((lane & 2) == 0, pltpu.roll(row, CH - 2, 1), pltpu.roll(row, 2, 1))
-    return row + far
-
-
-def local_stats(rows, cells):
-    total = sum(jnp.sum(r, axis=0, keepdims=True) for r in rows)
-    mean = over_group(total) * (1.0 / (cells * PER_GROUP))
-    dev = sum(jnp.sum((r - mean) * (r - mean), axis=0, keepdims=True) for r in rows)
-    return mean, over_group(dev)
+    place = iota(row.shape, 1) & (PER_GROUP - 1)
+    total = row
+    for step in range(1, PER_GROUP):
+        after = pltpu.roll(row, CH - step, 1)
+        before = pltpu.roll(row, step, 1)
+        total = total + jnp.where(place < PER_GROUP - step, after, 0.0) + jnp.where(place >= step, before, 0.0)
+    return total
+
+
+def local_stats(rows):
+    cells = len(rows) * rows[0].shape[0]
+    about = jnp.sum(rows[0], axis=0, keepdims=True) * (1.0 / rows[0].shape[0])
+    first, second = 0.0, 0.0
+    for r in rows:
+        off = r - about
+        first = first + off
+        second = second + off * off
+    first = jnp.sum(first, axis=0, keepdims=True)
+    mean_off = first * (1.0 / cells)
+    dev = jnp.sum(second, axis=0, keepdims=True) - first * mean_off
+    return about + mean_off, dev
+
+
+def to_groups(mean, dev, cells):
+    whole = over_group(mean) * (1.0 / PER_GROUP)
+    apart = mean - whole
+    spread = over_group(dev + cells * (apart * apart)) * (1.0 / (cells * PER_GROUP))
+    return whole, lax.rsqrt(spread + eps)
 
 
 def merge(mean, dev, others, cells):
@@ -101,20 +117,81 @@
     off = means - whole
     own = mean - whole
     spread = own * own + jnp.sum(off * off, axis=0)
-    return whole, dev + jnp.sum(others[:, 1:2, :], axis=0) + (cells * PER_GROUP) * spread
+    return whole, dev + jnp.sum(others[:, 1:2, :], axis=0) + cells * spread
 
 
 LEFT, MAIN, RIGHT, WIDE = 8, 16, 144, 160
 
 
+def prepare_b(cb_v, wba, wbb):
+    for dy in range(3):
+        for dx in range(2):
+            span = slice(dx * CH, (dx + 1) * CH)
+            high, low = split(cb_v[dy, dx])
+            wba[dy * 256 : dy * 256 + 128, span] = high
+            wba[dy * 256 + 128 : dy * 256 + 256, span] = high
+            wba[768 + dy * 128 : 896 + dy * 128, span] = low
+        high, low = split(cb_v[dy, 2])
+        for part, value in enumerate((high, high, low)):
+            if dy < 2:
+                wbb[part * 256 + dy * 128 : part * 256 + dy * 128 + 128, 0:CH] = value
+            else:
+                wbb[part * 256 : part * 256 + 128, CH : 2 * CH] = jnp.zeros((CH, CH), BF16)
+                wbb[part * 256 + 128 : part * 256 + 256, CH : 2 * CH] = value
+
+
+def activate(value, mean, scale, shift):
+    half = ((value - mean) * scale + shift) * 0.5
+    return half + half * jnp.tanh(half)
+
+
+def second_conv(ha, hl, act, gs, hb, wba, wbb, mean, scale, shift, not_first, not_last):
+    for i in range(10):
+        value = activate(ha[i, MAIN:RIGHT, :], mean, scale, shift)
+        if i == 0:
+            value = value * not_first
+        if i == 9:
+            value = value * not_last
+        act[i, :, 0:128], act[i, :, 128:256] = split(value)
+    known = iota((16, 1), 0)
+    known = jnp.where(known == 0, not_first, jnp.where(known == 9, not_last, 1.0))
+    for i in range(2):
+        hl[i, 0:16, :] = activate(hl[i, 0:16, :], mean, scale, shift) * known
+
+    def side(i, dy):
+        return split(hl[i, dy : dy + 16, :])
+
+    def rows(first, size, part):
+        return act[first : first + size, :, part * 128 : part * 128 + 128].reshape(size * 128, 128)
+
+    pieces = [act[dy : dy + 8].reshape(1024, 256) for dy in range(3)] + [rows(dy, 8, 0) for dy in range(3)]
+    at_side = [side(0, dy) for dy in range(3)]
+    at_side = [part for pair in at_side for part in pair] + [pair[0] for pair in at_side]
+    field = jnp.concatenate([jnp.concatenate(pieces, axis=1), jnp.concatenate(at_side, axis=1)], axis=0)
+    early = dot(field, wba[...])
+
+    pieces = [rows(0, 9, 0), rows(1, 9, 0), rows(0, 9, 1), rows(1, 9, 1), rows(0, 9, 0), rows(1, 9, 0)]
+    (high0, low0), (high1, low1) = side(1, 0), side(1, 1)
+    at_side = [high0, high1, low0, low1, high0, high1]
+    field = jnp.concatenate([jnp.concatenate(pieces, axis=1), jnp.concatenate(at_side, axis=1)], axis=0)
+    late = dot(field, wbb[...])
+
+    for i in range(8):
+        gs[0, i, MAIN:RIGHT, :] = early[i * 128 : (i + 1) * 128, 0:128]
+        gs[0, i, MAIN - 1 : MAIN, :] = early[1024 + i : 1025 + i, 0:128]
+        gs[2, i, MAIN:RIGHT, :] = late[i * 128 : (i + 1) * 128, 0:128] + late[(i + 1) * 128 : (i + 2) * 128, 128:256]
+        gs[2, i, RIGHT : RIGHT + 1, :] = late[1152 + i : 1153 + i, 0:128] + late[1153 + i : 1154 + i, 128:256]
+        hb[i] = gs[0, i, MAIN - 1 : RIGHT - 1, :] + early[i * 128 : (i + 1) * 128, 128:256] + gs[2, i, MAIN + 1 : RIGHT + 1, :]
+
+
 def kernel(
-    src_ref, cnt_ref, coarse_ref, remap_ref, ca_ref, cb_ref, gain_a_ref, shift_a_ref, gain_b_ref, shift_b_ref,
+    src_hbm, cnt_ref, coarse_ref, remap_ref, ca_ref, cb_ref, gain_a_ref, shift_a_ref, gain_b_ref, shift_b_ref,
     hb_ref, fin_ref,
-    coarse_v, remap_v, ca_v, cb_v, vec_v,
+    src_ref, coarse_v, remap_v, ca_v, cb_v, vec_v,
     tt, row_out, col_out, corner_out, mate_out, next_out,
     row_in, col_in, corner_in, mate_in, next_in,
-    copies, choices, side, wa32, wa, wb,
-    xs, gs, ha, act, hb,
+    copies, choices, side, wa32, wa, wba, wbb,
+    xs, gs, ha, hl, act, hb,
     stat, buf_x, buf_z,
     in_sem, out_sem, send_sem, recv_sem,
 ):
@@ -147,9 +224,11 @@
     ]
     for i, ref in enumerate((gain_a_ref, shift_a_ref, gain_b_ref, shift_b_ref)):
         loads.append(pltpu.make_async_copy(ref, vec_v.at[i], in_sem.at[4 + i]))
-    for load in loads:
+    sources = pltpu.make_async_copy(src_hbm, src_ref, in_sem.at[8])
+    for load in [sources] + loads:
         load.start()
 
+    sources.wait()
     lane = iota((1, 128), 1)
     own_choice = jnp.zeros((1, 128), F32)
     for k in range(SLOTS):
@@ -192,6 +271,7 @@
         cells = weights[160 + 16 * i : 176 + 16 * i].astype(F32)
         corner_out[i] = jnp.where(iota((16, 128), 0) < 8, cells, own_choice).astype(BF16)
     side[...] = jnp.zeros_like(side)
+    hl[...] = jnp.zeros_like(hl)
 
     loads[2].wait()
     wa32[...] = jnp.zeros_like(wa32)
@@ -239,17 +319,6 @@
     ]
     for copy in along_lon:
         copy.start()
-
-    loads[3].wait()
-    for dy in range(3):
-        for dx in range(3):
-            high, low = split(cb_v[dy, dx])
-            span = slice(dx * CH, (dx + 1) * CH)
-            wb[dy * 384 : dy * 384 + 128, span] = high
-            wb[dy * 384 + 128 : dy * 384 + 256, span] = high
-            wb[dy * 384 + 256 : dy * 384 + 384, span] = low
-    for load in loads[4:]:
-        load.wait()
 
     for copy in along_lon:
         copy.wait_recv()
@@ -362,53 +431,28 @@
             pltpu.make_async_copy(buf.at[turn], buf.at[turn], recv_sem.at[sem]).wait()
             mean, dev = merge(mean, dev, buf[turn], cells)
             cells = cells * (len(mates) + 1)
-        return mean, lax.rsqrt(dev * (1.0 / (cells * PER_GROUP)) + eps)
+        return to_groups(mean, dev, cells)
 
     def around_a():
+        for load in loads[3:]:
+            load.wait()
+        prepare_b(cb_v, wba, wbb)
         pltpu.make_async_copy(next_in, next_in, recv_sem.at[12]).wait()
         xs[11 * odd] = placed(next_in[...] * far_known)
         taps([0, 9])
         for i in (0, 9):
             ha[i, MAIN:RIGHT, :] = joined(i, MAIN, 128)
         for i in range(10):
-            ha[i, LEFT:MAIN, :] = joined(i, LEFT, 8)
-            ha[i, RIGHT : RIGHT + 8, :] = joined(i, RIGHT, 8)
-
-    mean, dev = local_stats([ha[i, MAIN:RIGHT, :] for i in range(1, 9)], ROWS_DEV * COLS_DEV)
+            hl[0, i : i + 1, :] = joined(i, MAIN - 1, 1)
+            hl[1, i : i + 1, :] = joined(i, RIGHT, 1)
+
+    mean, dev = local_stats([ha[i, MAIN:RIGHT, :] for i in range(1, 9)])
     mean, inverse = all_reduce(0, mean, dev, around_a)
 
-    scale = inverse * vec_v[0]
-    shift = vec_v[1]
-    for i in range(10):
-        for first, size, at in ((MAIN, 128, 0), (LEFT, 16, 128)):
-            if size == 128:
-                value = ha[i, MAIN:RIGHT, :]
-            else:
-                value = jnp.concatenate([ha[i, RIGHT : RIGHT + 8, :], ha[i, LEFT:MAIN, :]], axis=0)
-            normed = (value - mean) * scale + shift
-            half = normed * 0.5
-            value = half + half * jnp.tanh(half)
-            if i == 0:
-                value = value * not_first
-            if i == 9:
-                value = value * not_last
-            high, low = split(value)
-            act[i, at : at + size, 0:128] = high
-            act[i, at : at + size, 128:256] = low
-            act[i, at : at + size, 256:384] = high
-
-    field = jnp.concatenate([act[0:8], act[1:9], act[2:10]], axis=2).reshape(8 * 144, 9 * CH)
-    result = dot(field, wb[...]).reshape(8, 144, 3 * CH)
-    for dx in range(3):
-        span = slice(dx * CH, (dx + 1) * CH)
-        gs[dx, 0:8, MAIN:RIGHT, :] = result[:, 0:128, span]
-        gs[dx, 0:8, RIGHT : RIGHT + 8, :] = result[:, 128:136, span]
-        gs[dx, 0:8, LEFT:MAIN, :] = result[:, 136:144, span]
-    for i in range(8):
-        hb[i] = joined(i, MAIN, 128)
+    second_conv(ha, hl, act, gs, hb, wba, wbb, mean, inverse * vec_v[0], vec_v[1], not_first, not_last)
     store = pltpu.make_async_copy(hb, hb_ref, out_sem)
     store.start()
-    mean, dev = local_stats([hb[i] for i in range(8)], ROWS_DEV * COLS_DEV)
+    mean, dev = local_stats([hb[i] for i in range(8)])
     mean, inverse = all_reduce(1, mean, dev, lambda: None)
     fin_ref[0:1, :] = mean
     fin_ref[1:2, :] = inverse * vec_v[2]
@@ -430,7 +474,6 @@
     coarse, src_blocks, slot_counts, remap_tiles, conv_a, conv_b, gain_a, shift_a, gain_b, shift_b
 ):
     anywhere = pl.BlockSpec(memory_space=pl.ANY)
-    scalar = pl.BlockSpec(memory_space=pltpu.SMEM)
     vectors = [v.reshape(1, CH) for v in (gain_a, shift_a, gain_b, shift_b)]
     hidden, final = pl.pallas_call(
         kernel,
@@ -439,9 +482,10 @@
             pltpu.VMEM((ROWS_DEV, COLS_DEV, CH), F32),
             pltpu.VMEM((3, CH), F32),
         ),
-        in_specs=[scalar, scalar] + [anywhere] * 8,
+        in_specs=[anywhere, pl.BlockSpec(memory_space=pltpu.SMEM)] + [anywhere] * 8,
         out_specs=(anywhere, pl.BlockSpec(memory_space=pltpu.VMEM)),
         scratch_shapes=[
+            pltpu.SMEM((1, SLOTS), jnp.int32),
             pltpu.VMEM((VARS, BLK_DEV, BCELLS), BF16),
             pltpu.VMEM((128, 1024), BF16),
             pltpu.VMEM((3, 3, VARS, CH), F32),
@@ -463,16 +507,18 @@
             pltpu.VMEM((96, 128), F32),
             pltpu.VMEM((128, 3 * CH), F32),
             pltpu.VMEM((128, 3 * CH), BF16),
-            pltpu.VMEM((9 * CH, 3 * CH), BF16),
+            pltpu.VMEM((9 * CH, 2 * CH), BF16),
+            pltpu.VMEM((6 * CH, 2 * CH), BF16),
             pltpu.VMEM((12, COLS_DEV, 128), BF16),
             pltpu.VMEM((3, 10, WIDE, CH), F32),
             pltpu.VMEM((10, WIDE, CH), F32),
-            pltpu.VMEM((10, 144, 3 * CH), BF16),
+            pltpu.VMEM((2, 24, CH), F32),
+            pltpu.VMEM((10, COLS_DEV, 2 * CH), BF16),
             pltpu.VMEM((ROWS_DEV, COLS_DEV, CH), F32),
             pltpu.VMEM((2, 2, 2, CH), F32),
             pltpu.VMEM((2, 15, 2, CH), F32),
             pltpu.VMEM((2, 31, 2, CH), F32),
-            pltpu.SemaphoreType.DMA((8,)),
+            pltpu.SemaphoreType.DMA((9,)),
             pltpu.SemaphoreType.DMA,
             pltpu.SemaphoreType.DMA((10,)),
             pltpu.SemaphoreType.DMA((13,)),

time: 56.2 us -> 55 us (0.979)
  Pallas kernels: 54.5 us -> 53.3 us
    pallas_call x1, Pallas kernels: 54.5 us -> 53.3 us  [per_device(): pl.pallas_call(kernel, name='stem', out_shape=(pltpu.VMEM((ROWS_DEV, COLS...]
where the time goes in v5:
time: 55 us; the launch traced here: 54.8 us
  Pallas kernels  53.3 us (97%)
  other arithmetic  0.87 us (2%)
  between operations  0.67 us (1%)
    pallas_call x1, Pallas kernels, per_device(): pl.pallas_call(kernel, name='stem', out_shape=(pltpu.VMEM((ROWS_DEV, COLS...  53.3 us

profile of v5, /device:TPU:1, one launch (start us, length us, event | category | flops | bytes accessed | tf_op | source)
XLA Modules:
  0.0 54.8 jit_solution(16963749413538670000)
XLA Ops:
  0.7 53.3 %stem.1 = (f32[8,128,128]{2,1,0:T(8,128)S(1)}, f32[3,128]{1,0:T(4,128)S(1)}) custom-call(s32[1,4]{1,0:T(1,128)} %src_hbm.1, s32[1]{0:T(128)S(6)} %copy.11.cnt_ref, bf16[12,4,32]{2,1,0:T(4,128)(2,1)} %bitcast.13, bf16[128,1024]{1,0:T(8,128)(2,1)} %bitcast.12, f32[3,3,12,128]{3,2,1,0:T(8,128)} %ca_ref.1, f32[3,3,128,128]{3,2,1,0:T(8,128)} %cb_ref.1, ...), custom_call_target="tpu_custom_call" | custom-call | tf_op jit(solution)/shard_map/stem/pallas_call | solution.py:478
  54.0 0.9 %multiply_convert_fusion = bf16[8,128,128]{2,1,0:T(8,128)(2,1)} fusion(f32[8,128,128]{2,1,0:T(8,128)S(1)} %get-tuple-element.7, f32[128]{0:T(128)S(1)} %get-tuple-element.10, f32[128]{0:T(128)S(1)} %get-tuple-element.11, f32[128]{0:T(128)S(1)} %get-tuple-element.9), kind=kLoop, calls=%fused_computation | loop fusion | flops 1048576 | bytes 787968 | tf_op jit(solution)/shard_map/convert_element_type | solution.py:534
  (1 shorter events, 0.0 us)

commit v6 on v5

--- a/solution.py
+++ b/solution.py
@@ -89,18 +89,25 @@
     return total
 
 
-def local_stats(rows):
-    cells = len(rows) * rows[0].shape[0]
-    about = jnp.sum(rows[0], axis=0, keepdims=True) * (1.0 / rows[0].shape[0])
+def local_stats(rows, extra=()):
+    size = rows[0].shape[0]
+    about = jnp.sum(rows[0], axis=0, keepdims=True) * (1.0 / size)
     first, second = 0.0, 0.0
+    lines = jnp.asarray(len(rows), F32)
     for r in rows:
         off = r - about
         first = first + off
         second = second + off * off
+    for r, counts in extra:
+        off = jnp.where(counts, r - about, 0.0)
+        first = first + off
+        second = second + off * off
+        lines = lines + jnp.where(counts, 1.0, 0.0)
+    cells = jnp.full((1, CH), lines * size)
     first = jnp.sum(first, axis=0, keepdims=True)
-    mean_off = first * (1.0 / cells)
+    mean_off = first / cells
     dev = jnp.sum(second, axis=0, keepdims=True) - first * mean_off
-    return about + mean_off, dev
+    return about + mean_off, dev, cells
 
 
 def to_groups(mean, dev, cells):
@@ -110,14 +117,14 @@
     return whole, lax.rsqrt(spread + eps)
 
 
-def merge(mean, dev, others, cells):
-    count = others.shape[0] + 1
-    means = others[:, 0:1, :]
-    whole = (mean + jnp.sum(means, axis=0)) * (1.0 / count)
+def merge(mean, dev, cells, others):
+    means, devs, counts = others[:, 0:1, :], others[:, 1:2, :], others[:, 2:3, :]
+    every = cells + jnp.sum(counts, axis=0)
+    whole = (mean * cells + jnp.sum(means * counts, axis=0)) / every
     off = means - whole
     own = mean - whole
-    spread = own * own + jnp.sum(off * off, axis=0)
-    return whole, dev + jnp.sum(others[:, 1:2, :], axis=0) + cells * spread
+    spread = own * own * cells + jnp.sum(off * off * counts, axis=0)
+    return whole, dev + jnp.sum(devs, axis=0) + spread, every
 
 
 LEFT, MAIN, RIGHT, WIDE = 8, 16, 144, 160
@@ -188,8 +195,8 @@
     src_hbm, cnt_ref, coarse_ref, remap_ref, ca_ref, cb_ref, gain_a_ref, shift_a_ref, gain_b_ref, shift_b_ref,
     hb_ref, fin_ref,
     src_ref, coarse_v, remap_v, ca_v, cb_v, vec_v,
-    tt, row_out, col_out, corner_out, mate_out, next_out,
-    row_in, col_in, corner_in, mate_in, next_in,
+    tt, row_out, col_out, corner_out, mate_out,
+    row_in, col_in, corner_in, mate_in,
     copies, choices, side, wa32, wa, wba, wbb,
     xs, gs, ha, hl, act, hb,
     stat, buf_x, buf_z,
@@ -200,17 +207,16 @@
     z_mates = along_z(place)
     xy_mates = across(place)
     lon_mates = coarse_mates(place)
-    row_up, row_down = lax.rem(row + 15, 16), lax.rem(row + 1, 16)
     lon_left, lon_right = lax.rem(lon + 31, 32), lax.rem(lon + 1, 32)
+    odd = lax.rem(row, 2)
+    is_odd = odd == 1
+    early = lax.rem(lax.div(row, 2), 2) == 0
+    near_row = row + 1 - 2 * odd
+    far_row = lax.rem(row + 2 * odd + 15, 16)
     halo = [
-        (row_down, lon), (row_up, lon),
-        (row, lon_right), (row, lon_left),
-        (row_down, lon_right), (row_up, lon_right),
-        (row_down, lon_left), (row_up, lon_left),
+        (far_row, lon), (far_row, lon_right), (far_row, lon_left), (near_row, lon),
+        (near_row, lon_right), (near_row, lon_left), (row, lon_right), (row, lon_left),
     ]
-    odd = lax.rem(row, 2)
-    core_mate = (row + 1 - 2 * odd, lon)
-    far_mate = (lax.rem(row + 2 * odd + 15, 16), lon)
     barrier = pltpu.get_barrier_semaphore()
     partners = halo + lon_mates + z_mates + xy_mates
     for mate in partners:
@@ -251,27 +257,28 @@
     tt[2] = pad.astype(BF16)
 
     loads[1].wait()
-    at = iota((224, 1), 0)
+    at = iota((352, 1), 0)
     inner = at & 15
-    cell = jnp.where(at < 128, at + odd * (7 * COLS_DEV), -1)
+    cell = jnp.where(at < 128, at + odd * (7 * COLS_DEV), at + odd * (5 * COLS_DEV))
     column = (inner & 7) * COLS_DEV + (inner >> 3)
-    cell = jnp.where((at >= 128) & (at < 144), column + 126, cell)
-    cell = jnp.where((at >= 144) & (at < 160), column, cell)
-    for i, (row0, col0) in enumerate(((6, 126), (0, 126), (6, 0), (0, 0))):
-        here = (at >= 160 + 16 * i) & (at < 164 + 16 * i)
-        cell = jnp.where(here, (row0 + (inner >> 1)) * COLS_DEV + col0 + (inner & 1), cell)
-    pick = jnp.where(iota((224, 1024), 1) == cell, 1.0, 0.0).astype(BF16)
+    cell = jnp.where((at >= 256) & (at < 272), column + 126, cell)
+    cell = jnp.where((at >= 272) & (at < 288), column, cell)
+    for i, (row0, col0) in enumerate(((6 * odd, 126), (6 * odd, 0), (6 - 6 * odd, 126), (6 - 6 * odd, 0))):
+        here = jnp.where(inner < 4, (row0 + (inner >> 1)) * COLS_DEV + col0 + (inner & 1), -1)
+        cell = jnp.where((at >= 288 + 16 * i) & (at < 304 + 16 * i), here, cell)
+    pick = jnp.where(iota((352, 1024), 1) == cell, 1.0, 0.0).astype(BF16)
     weights = dot(pick, remap_v[...], ((1,), (1,))).astype(BF16)
-    row_out[0:128, :] = weights[0:128]
-    row_out[128:144, :] = choice_tile
+    row_out[0:256, :] = weights[0:256]
+    row_out[256:272, :] = choice_tile
     for i in range(2):
-        col_out[i, 0:16, :] = weights[128 + 16 * i : 144 + 16 * i]
+        col_out[i, 0:16, :] = weights[256 + 16 * i : 272 + 16 * i]
         col_out[i, 16:32, :] = choice_tile
     for i in range(4):
-        cells = weights[160 + 16 * i : 176 + 16 * i].astype(F32)
+        cells = weights[288 + 16 * i : 304 + 16 * i].astype(F32)
         corner_out[i] = jnp.where(iota((16, 128), 0) < 8, cells, own_choice).astype(BF16)
     side[...] = jnp.zeros_like(side)
     hl[...] = jnp.zeros_like(hl)
+    xs[...] = jnp.zeros_like(xs)
 
     loads[2].wait()
     wa32[...] = jnp.zeros_like(wa32)
@@ -305,11 +312,13 @@
         )
         copy.start()
 
-    send(row_out, row_in, far_mate, 0, 0)
-    for i in range(4):
-        send(corner_out.at[i], corner_in.at[i], halo[4 + i], 1, 1)
+    send(row_out, row_in, halo[0], 0, 0)
     for i in range(2):
-        send(col_out.at[i], col_in.at[i], halo[2 + i], 8, 2)
+        send(corner_out.at[i], corner_in.at[i], halo[1 + i], 1, 1)
+    for i in range(2):
+        send(col_out.at[i], col_in.at[i], halo[6 + i], 8, 2)
+    for i in range(2):
+        send(corner_out.at[2 + i], corner_in.at[2 + i], halo[4 + i], 9, 12)
     along_lon = [
         pltpu.make_async_remote_copy(
             src_ref=tt.at[2], dst_ref=tt.at[slot], send_sem=send_sem.at[7], recv_sem=recv_sem.at[8 + i],
@@ -335,12 +344,9 @@
 
     four = jnp.concatenate([remap_v[:, 0:256], remap_v[:, 768:1024]], axis=1)
     four = dot(blocks, four)
-    is_odd = odd == 1
     mate_out[0] = jnp.where(is_odd, four[:, 0:128], four[:, 384:512])
     mate_out[1] = jnp.where(is_odd, four[:, 128:256], four[:, 256:384])
-    next_out[...] = jnp.where(is_odd, four[:, 256:384], four[:, 128:256])
-    send(mate_out, mate_in, core_mate, 2, 3)
-    send(next_out, next_in, far_mate, 9, 12)
+    send(mate_out, mate_in, halo[3], 2, 3)
 
     spread_blocks = dot(blocks, spread_var, ((0,), (0,))).astype(BF16)
     fine = dot(remap_v[...], spread_blocks, ((0,), (0,)))
@@ -376,51 +382,75 @@
     xs[10 - 9 * odd] = placed(mate_in[0])
     xs[11 - 11 * odd] = placed(mate_in[1])
 
-    pltpu.make_async_copy(col_in, col_in, recv_sem.at[2]).wait()
-    pltpu.make_async_copy(corner_in, corner_in, recv_sem.at[1]).wait()
-    pltpu.make_async_copy(row_in, row_in, recv_sem.at[0]).wait()
     far_known = jnp.where(is_odd, not_last, not_first)
+    has_far = far_known > 0.5
 
     def fine_of(cells, choice, first_tile, known):
         held = chosen(choice.astype(F32), first_tile) * known
         return dot(cells, held.astype(BF16), ((1,), (1,)))
 
-    parts = [
-        fine_of(row_in[0:128, :], row_in[128:129, :], 1, far_known),
+    def spread_cells(parts):
+        high, low = split(jnp.concatenate(parts, axis=0))
+        return dot(jnp.concatenate([high, low], axis=1), spread_msg)
+
+    def put_corner(cells, first_row, place):
+        for n in range(4):
+            side[first_row + (n >> 1), place + (n & 1) : place + (n & 1) + 1, :] = cells[n : n + 1]
+
+    def far_edges():
+        pltpu.make_async_copy(corner_in.at[pl.ds(0, 2)], corner_in.at[pl.ds(0, 2)], recv_sem.at[1]).wait()
+        pltpu.make_async_copy(row_in, row_in, recv_sem.at[0]).wait()
+        cells = spread_cells([
+            fine_of(row_in[0:256, :], row_in[256:257, :], 1, far_known),
+            fine_of(corner_in[0], corner_in[0, 8:9, :], 0, far_known),
+            fine_of(corner_in[1], corner_in[1, 8:9, :], 2, far_known),
+        ])
+        xs[1 + 9 * odd] = cells[0:128].astype(BF16)
+        xs[11 * odd] = cells[128:256].astype(BF16)
+        put_corner(cells[256:272], 10 * odd, 6)
+        put_corner(cells[272:288], 10 * odd, 0)
+
+    pltpu.make_async_copy(col_in, col_in, recv_sem.at[2]).wait()
+    pltpu.make_async_copy(corner_in.at[pl.ds(2, 2)], corner_in.at[pl.ds(2, 2)], recv_sem.at[12]).wait()
+    cells = spread_cells([
         fine_of(col_in[0, 0:16, :], col_in[0, 16:17, :], 0, 1.0),
         fine_of(col_in[1, 0:16, :], col_in[1, 16:17, :], 2, 1.0),
-    ]
-    for i, (first_tile, known) in enumerate(((0, not_first), (0, not_last), (2, not_first), (2, not_last))):
-        parts.append(fine_of(corner_in[i], corner_in[i, 8:9, :], first_tile, known))
-    high, low = split(jnp.concatenate(parts, axis=0))
-    cells = dot(jnp.concatenate([high, low], axis=1), spread_msg)
-    xs[1 + 9 * odd] = cells[0:128].astype(BF16)
-    for i, first in enumerate((6, 0)):
+        fine_of(corner_in[2], corner_in[2, 8:9, :], 0, 1.0),
+        fine_of(corner_in[3], corner_in[3, 8:9, :], 2, 1.0),
+    ])
+    for i, place_at in enumerate((6, 0)):
         for n in range(16):
-            line = ((n & 7) + 2) * 8 + first + (n >> 3)
-            side[line : line + 1, :] = cells[128 + 16 * i + n : 129 + 16 * i + n]
-    for i, first in enumerate((6, 86, 0, 80)):
-        for n in range(4):
-            line = first + (n >> 1) * 8 + (n & 1)
-            side[line : line + 1, :] = cells[160 + 16 * i + n : 161 + 16 * i + n]
-    edge = side[...].reshape(12, 8, 128)
-    side_lane = jnp.broadcast_to(lane.reshape(1, 1, 128), (10, 8, 128))
-    side_patches = patches(edge[0:10], edge[1:11], edge[2:12], side_lane).reshape(80, 128)
-    side_taps = dot(side_patches, wa[...]).reshape(10, 8, 3 * CH)
-    for dx in range(3):
-        piece = side_taps[:, :, dx * CH : (dx + 1) * CH]
-        gs[dx, :, LEFT:MAIN, :] = piece
-        gs[dx, :, RIGHT : RIGHT + 8, :] = piece
-    taps([1, 8])
-    for i in range(1, 9):
+            at_col = place_at + (n >> 3)
+            side[(n & 7) + 2, at_col : at_col + 1, :] = cells[16 * i + n : 16 * i + n + 1]
+    put_corner(cells[32:48], 10 - 10 * odd, 6)
+    put_corner(cells[48:64], 10 - 10 * odd, 0)
+    near_border, far_border, far_beyond = 8 - 7 * odd, 1 + 7 * odd, 9 * odd
+    taps([near_border])
+
+    def far_rows():
+        taps([far_border, far_beyond])
+        side_lane = jnp.broadcast_to(lane.reshape(1, 1, 128), (10, 8, 128))
+        side_patches = patches(side[0:10], side[1:11], side[2:12], side_lane).reshape(80, 128)
+        side_taps = dot(side_patches, wa[...]).reshape(10, 8, 3 * CH)
+        for dx in range(3):
+            piece = side_taps[:, :, dx * CH : (dx + 1) * CH]
+            gs[dx, :, LEFT:MAIN, :] = piece
+            gs[dx, :, RIGHT : RIGHT + 8, :] = piece
+        for i in (far_border, far_beyond):
+            ha[i, MAIN:RIGHT, :] = joined(i, MAIN, 128)
+
+    pl.when(early)(far_edges)
+    far_rows()
+    for i in range(2, 8):
         ha[i, MAIN:RIGHT, :] = joined(i, MAIN, 128)
-
-    def all_reduce(turn, mean, dev, beside):
-        cells = ROWS_DEV * COLS_DEV
+    ha[near_border, MAIN:RIGHT, :] = joined(near_border, MAIN, 128)
+
+    def all_reduce(turn, mean, dev, cells, beside):
         for stage, (mates, buf) in enumerate(((z_mates, buf_z), (xy_mates, buf_x))):
             sem = 4 + turn * 2 + stage
             stat[turn, stage, 0:1, :] = mean
             stat[turn, stage, 1:2, :] = dev
+            stat[turn, stage, 2:3, :] = cells
             for j, mate in enumerate(mates):
                 pltpu.make_async_remote_copy(
                     src_ref=stat.at[turn, stage], dst_ref=buf.at[turn, j], send_sem=send_sem.at[sem - 1], recv_sem=recv_sem.at[sem],
@@ -429,41 +459,46 @@
             if stage == 0:
                 beside()
             pltpu.make_async_copy(buf.at[turn], buf.at[turn], recv_sem.at[sem]).wait()
-            mean, dev = merge(mean, dev, buf[turn], cells)
-            cells = cells * (len(mates) + 1)
+            mean, dev, cells = merge(mean, dev, cells, buf[turn])
         return to_groups(mean, dev, cells)
 
     def around_a():
         for load in loads[3:]:
             load.wait()
         prepare_b(cb_v, wba, wbb)
-        pltpu.make_async_copy(next_in, next_in, recv_sem.at[12]).wait()
-        xs[11 * odd] = placed(next_in[...] * far_known)
-        taps([0, 9])
-        for i in (0, 9):
-            ha[i, MAIN:RIGHT, :] = joined(i, MAIN, 128)
+        pl.when(jnp.logical_not(early))(far_edges)
+        far_rows()
+        near_beyond = 9 - 9 * odd
+        taps([near_beyond])
+        ha[near_beyond, MAIN:RIGHT, :] = joined(near_beyond, MAIN, 128)
         for i in range(10):
             hl[0, i : i + 1, :] = joined(i, MAIN - 1, 1)
             hl[1, i : i + 1, :] = joined(i, RIGHT, 1)
 
-    mean, dev = local_stats([ha[i, MAIN:RIGHT, :] for i in range(1, 9)])
-    mean, inverse = all_reduce(0, mean, dev, around_a)
+    mean, dev, cells = local_stats(
+        [ha[i, MAIN:RIGHT, :] for i in range(2, 8)] + [ha[near_border, MAIN:RIGHT, :]],
+        [
+            (ha[far_border, MAIN:RIGHT, :], jnp.logical_or(early, jnp.logical_not(has_far))),
+            (ha[far_beyond, MAIN:RIGHT, :], jnp.logical_and(early, has_far)),
+        ],
+    )
+    mean, inverse = all_reduce(0, mean, dev, cells, around_a)
 
     second_conv(ha, hl, act, gs, hb, wba, wbb, mean, inverse * vec_v[0], vec_v[1], not_first, not_last)
     store = pltpu.make_async_copy(hb, hb_ref, out_sem)
     store.start()
-    mean, dev = local_stats([hb[i] for i in range(8)])
-    mean, inverse = all_reduce(1, mean, dev, lambda: None)
+    mean, dev, cells = local_stats([hb[i] for i in range(8)])
+    mean, inverse = all_reduce(1, mean, dev, cells, lambda: None)
     fin_ref[0:1, :] = mean
     fin_ref[1:2, :] = inverse * vec_v[2]
     fin_ref[2:3, :] = vec_v[3]
     store.wait()
 
     pltpu.make_async_copy(row_in, row_in, send_sem.at[0]).wait()
-    pltpu.make_async_copy(corner_in, corner_in, send_sem.at[1]).wait()
+    pltpu.make_async_copy(corner_in.at[pl.ds(0, 2)], corner_in.at[pl.ds(0, 2)], send_sem.at[1]).wait()
+    pltpu.make_async_copy(corner_in.at[pl.ds(2, 2)], corner_in.at[pl.ds(2, 2)], send_sem.at[9]).wait()
     pltpu.make_async_copy(col_in, col_in, send_sem.at[8]).wait()
     pltpu.make_async_copy(mate_in, mate_in, send_sem.at[2]).wait()
-    pltpu.make_async_copy(next_in, next_in, send_sem.at[9]).wait()
     pltpu.make_async_copy(tt.at[pl.ds(0, 4)], tt.at[pl.ds(0, 4)], send_sem.at[7]).wait()
     for turn in range(2):
         pltpu.make_async_copy(buf_z.at[turn], buf_z.at[turn], send_sem.at[3 + 2 * turn]).wait()
@@ -492,19 +527,17 @@
             pltpu.VMEM((3, 3, CH, CH), F32),
             pltpu.VMEM((4, 1, CH), F32),
             pltpu.VMEM((5, 16, 128), BF16),
-            pltpu.VMEM((144, 128), BF16),
+            pltpu.VMEM((272, 128), BF16),
             pltpu.VMEM((2, 32, 128), BF16),
             pltpu.VMEM((4, 16, 128), BF16),
             pltpu.VMEM((2, 16, 128), F32),
-            pltpu.VMEM((16, 128), F32),
-            pltpu.VMEM((144, 128), BF16),
+            pltpu.VMEM((272, 128), BF16),
             pltpu.VMEM((2, 32, 128), BF16),
             pltpu.VMEM((4, 16, 128), BF16),
             pltpu.VMEM((2, 16, 128), F32),
-            pltpu.VMEM((16, 128), F32),
             pltpu.VMEM((128, BLK_DEV * 128), BF16),
             pltpu.VMEM((80, BLK_DEV * 128), F32),
-            pltpu.VMEM((96, 128), F32),
+            pltpu.VMEM((12, 8, 128), F32),
             pltpu.VMEM((128, 3 * CH), F32),
             pltpu.VMEM((128, 3 * CH), BF16),
             pltpu.VMEM((9 * CH, 2 * CH), BF16),
@@ -515,9 +548,9 @@
             pltpu.VMEM((2, 24, CH), F32),
             pltpu.VMEM((10, COLS_DEV, 2 * CH), BF16),
             pltpu.VMEM((ROWS_DEV, COLS_DEV, CH), F32),
-            pltpu.VMEM((2, 2, 2, CH), F32),
-            pltpu.VMEM((2, 15, 2, CH), F32),
-            pltpu.VMEM((2, 31, 2, CH), F32),
+            pltpu.VMEM((2, 2, 3, CH), F32),
+            pltpu.VMEM((2, 15, 3, CH), F32),
+            pltpu.VMEM((2, 31, 3, CH), F32),
             pltpu.SemaphoreType.DMA((9,)),
             pltpu.SemaphoreType.DMA,
             pltpu.SemaphoreType.DMA((10,)),

time: 55 us -> 58.2 us (1.058)
  Pallas kernels: 53.3 us -> 56.5 us
    pallas_call x1, Pallas kernels: 53.3 us -> 56.5 us  [per_device(): pl.pallas_call(kernel, name='stem', out_shape=(pltpu.VMEM((ROWS_DEV, COLS...]
where the time goes in v6:
time: 58.2 us; the launch traced here: 58.1 us
  Pallas kernels  56.5 us (97%)
  other arithmetic  0.87 us (1%)
  between operations  0.67 us (1%)
    pallas_call x1, Pallas kernels, per_device(): pl.pallas_call(kernel, name='stem', out_shape=(pltpu.VMEM((ROWS_DEV, COLS...  56.5 us

profile of v6, /device:TPU:1, one launch (start us, length us, event | category | flops | bytes accessed | tf_op | source)
XLA Modules:
  0.0 58.1 jit_solution(359001692409345965)
XLA Ops:
  0.7 56.5 %stem.1 = (f32[8,128,128]{2,1,0:T(8,128)S(1)}, f32[3,128]{1,0:T(4,128)S(1)}) custom-call(s32[1,4]{1,0:T(1,128)} %src_hbm.1, s32[1]{0:T(128)S(6)} %copy.11.cnt_ref, bf16[12,4,32]{2,1,0:T(4,128)(2,1)} %bitcast.13, bf16[128,1024]{1,0:T(8,128)(2,1)} %bitcast.12, f32[3,3,12,128]{3,2,1,0:T(8,128)} %ca_ref.1, f32[3,3,128,128]{3,2,1,0:T(8,128)} %cb_ref.1, ...), custom_call_target="tpu_custom_call" | custom-call | tf_op jit(solution)/shard_map/stem/pallas_call | solution.py:513
  57.2 0.9 %multiply_convert_fusion = bf16[8,128,128]{2,1,0:T(8,128)(2,1)} fusion(f32[8,128,128]{2,1,0:T(8,128)S(1)} %get-tuple-element.7, f32[128]{0:T(128)S(1)} %get-tuple-element.10, f32[128]{0:T(128)S(1)} %get-tuple-element.11, f32[128]{0:T(128)S(1)} %get-tuple-element.9), kind=kLoop, calls=%fused_computation | loop fusion | flops 1048576 | bytes 787968 | tf_op jit(solution)/shard_map/convert_element_type | solution.py:567
  (1 shorter events, 0.0 us)

commit v7 on v5

--- a/solution.py
+++ b/solution.py
@@ -188,8 +188,8 @@
     src_hbm, cnt_ref, coarse_ref, remap_ref, ca_ref, cb_ref, gain_a_ref, shift_a_ref, gain_b_ref, shift_b_ref,
     hb_ref, fin_ref,
     src_ref, coarse_v, remap_v, ca_v, cb_v, vec_v,
-    tt, row_out, col_out, corner_out, mate_out, next_out,
-    row_in, col_in, corner_in, mate_in, next_in,
+    tt, row_out, col_out, corner_out, mate_out, far_out,
+    row_in, col_in, corner_in, mate_in, far_in,
     copies, choices, side, wa32, wa, wba, wbb,
     xs, gs, ha, hl, act, hb,
     stat, buf_x, buf_z,
@@ -200,17 +200,16 @@
     z_mates = along_z(place)
     xy_mates = across(place)
     lon_mates = coarse_mates(place)
-    row_up, row_down = lax.rem(row + 15, 16), lax.rem(row + 1, 16)
     lon_left, lon_right = lax.rem(lon + 31, 32), lax.rem(lon + 1, 32)
+    odd = lax.rem(row, 2)
+    is_odd = odd == 1
+    early = lax.rem(lax.div(row, 2), 2) == 0
+    near_row = row + 1 - 2 * odd
+    far_row = lax.rem(row + 2 * odd + 15, 16)
     halo = [
-        (row_down, lon), (row_up, lon),
-        (row, lon_right), (row, lon_left),
-        (row_down, lon_right), (row_up, lon_right),
-        (row_down, lon_left), (row_up, lon_left),
+        (far_row, lon), (far_row, lon_right), (far_row, lon_left), (near_row, lon),
+        (near_row, lon_right), (near_row, lon_left), (row, lon_right), (row, lon_left),
     ]
-    odd = lax.rem(row, 2)
-    core_mate = (row + 1 - 2 * odd, lon)
-    far_mate = (lax.rem(row + 2 * odd + 15, 16), lon)
     barrier = pltpu.get_barrier_semaphore()
     partners = halo + lon_mates + z_mates + xy_mates
     for mate in partners:
@@ -253,13 +252,13 @@
     loads[1].wait()
     at = iota((224, 1), 0)
     inner = at & 15
-    cell = jnp.where(at < 128, at + odd * (7 * COLS_DEV), -1)
+    cell = at + odd * (7 * COLS_DEV)
     column = (inner & 7) * COLS_DEV + (inner >> 3)
     cell = jnp.where((at >= 128) & (at < 144), column + 126, cell)
     cell = jnp.where((at >= 144) & (at < 160), column, cell)
-    for i, (row0, col0) in enumerate(((6, 126), (0, 126), (6, 0), (0, 0))):
-        here = (at >= 160 + 16 * i) & (at < 164 + 16 * i)
-        cell = jnp.where(here, (row0 + (inner >> 1)) * COLS_DEV + col0 + (inner & 1), cell)
+    for i, (row0, col0) in enumerate(((6 * odd, 126), (6 * odd, 0), (6 - 6 * odd, 126), (6 - 6 * odd, 0))):
+        here = jnp.where(inner < 4, (row0 + (inner >> 1)) * COLS_DEV + col0 + (inner & 1), -1)
+        cell = jnp.where((at >= 160 + 16 * i) & (at < 176 + 16 * i), here, cell)
     pick = jnp.where(iota((224, 1024), 1) == cell, 1.0, 0.0).astype(BF16)
     weights = dot(pick, remap_v[...], ((1,), (1,))).astype(BF16)
     row_out[0:128, :] = weights[0:128]
@@ -272,6 +271,7 @@
         corner_out[i] = jnp.where(iota((16, 128), 0) < 8, cells, own_choice).astype(BF16)
     side[...] = jnp.zeros_like(side)
     hl[...] = jnp.zeros_like(hl)
+    xs[...] = jnp.zeros_like(xs)
 
     loads[2].wait()
     wa32[...] = jnp.zeros_like(wa32)
@@ -305,11 +305,16 @@
         )
         copy.start()
 
-    send(row_out, row_in, far_mate, 0, 0)
-    for i in range(4):
-        send(corner_out.at[i], corner_in.at[i], halo[4 + i], 1, 1)
+    @pl.when(early)
+    def _():
+        send(row_out, row_in, halo[0], 0, 0)
+
     for i in range(2):
-        send(col_out.at[i], col_in.at[i], halo[2 + i], 8, 2)
+        send(corner_out.at[i], corner_in.at[i], halo[1 + i], 1, 1)
+    for i in range(2):
+        send(col_out.at[i], col_in.at[i], halo[6 + i], 8, 2)
+    for i in range(2):
+        send(corner_out.at[2 + i], corner_in.at[2 + i], halo[4 + i], 9, 12)
     along_lon = [
         pltpu.make_async_remote_copy(
             src_ref=tt.at[2], dst_ref=tt.at[slot], send_sem=send_sem.at[7], recv_sem=recv_sem.at[8 + i],
@@ -335,12 +340,12 @@
 
     four = jnp.concatenate([remap_v[:, 0:256], remap_v[:, 768:1024]], axis=1)
     four = dot(blocks, four)
-    is_odd = odd == 1
     mate_out[0] = jnp.where(is_odd, four[:, 0:128], four[:, 384:512])
     mate_out[1] = jnp.where(is_odd, four[:, 128:256], four[:, 256:384])
-    next_out[...] = jnp.where(is_odd, four[:, 256:384], four[:, 128:256])
-    send(mate_out, mate_in, core_mate, 2, 3)
-    send(next_out, next_in, far_mate, 9, 12)
+    far_out[0] = jnp.where(is_odd, four[:, 384:512], four[:, 0:128])
+    far_out[1] = jnp.where(is_odd, four[:, 256:384], four[:, 128:256])
+    send(far_out, far_in, halo[0], 10, 13)
+    send(mate_out, mate_in, halo[3], 2, 3)
 
     spread_blocks = dot(blocks, spread_var, ((0,), (0,))).astype(BF16)
     fine = dot(remap_v[...], spread_blocks, ((0,), (0,)))
@@ -376,44 +381,66 @@
     xs[10 - 9 * odd] = placed(mate_in[0])
     xs[11 - 11 * odd] = placed(mate_in[1])
 
-    pltpu.make_async_copy(col_in, col_in, recv_sem.at[2]).wait()
-    pltpu.make_async_copy(corner_in, corner_in, recv_sem.at[1]).wait()
-    pltpu.make_async_copy(row_in, row_in, recv_sem.at[0]).wait()
     far_known = jnp.where(is_odd, not_last, not_first)
 
     def fine_of(cells, choice, first_tile, known):
         held = chosen(choice.astype(F32), first_tile) * known
         return dot(cells, held.astype(BF16), ((1,), (1,)))
 
-    parts = [
-        fine_of(row_in[0:128, :], row_in[128:129, :], 1, far_known),
+    def spread_cells(parts):
+        high, low = split(jnp.concatenate(parts, axis=0))
+        return dot(jnp.concatenate([high, low], axis=1), spread_msg)
+
+    def put_corner(cells, first_row, place):
+        for n in range(4):
+            side[first_row + (n >> 1), place + (n & 1) : place + (n & 1) + 1, :] = cells[n : n + 1]
+
+    pltpu.make_async_copy(col_in, col_in, recv_sem.at[2]).wait()
+    pltpu.make_async_copy(corner_in.at[pl.ds(2, 2)], corner_in.at[pl.ds(2, 2)], recv_sem.at[12]).wait()
+    cells = spread_cells([
         fine_of(col_in[0, 0:16, :], col_in[0, 16:17, :], 0, 1.0),
         fine_of(col_in[1, 0:16, :], col_in[1, 16:17, :], 2, 1.0),
-    ]
-    for i, (first_tile, known) in enumerate(((0, not_first), (0, not_last), (2, not_first), (2, not_last))):
-        parts.append(fine_of(corner_in[i], corner_in[i, 8:9, :], first_tile, known))
-    high, low = split(jnp.concatenate(parts, axis=0))
-    cells = dot(jnp.concatenate([high, low], axis=1), spread_msg)
-    xs[1 + 9 * odd] = cells[0:128].astype(BF16)
-    for i, first in enumerate((6, 0)):
+        fine_of(corner_in[2], corner_in[2, 8:9, :], 0, 1.0),
+        fine_of(corner_in[3], corner_in[3, 8:9, :], 2, 1.0),
+    ])
+    for i, place_at in enumerate((6, 0)):
         for n in range(16):
-            line = ((n & 7) + 2) * 8 + first + (n >> 3)
-            side[line : line + 1, :] = cells[128 + 16 * i + n : 129 + 16 * i + n]
-    for i, first in enumerate((6, 86, 0, 80)):
-        for n in range(4):
-            line = first + (n >> 1) * 8 + (n & 1)
-            side[line : line + 1, :] = cells[160 + 16 * i + n : 161 + 16 * i + n]
-    edge = side[...].reshape(12, 8, 128)
+            at_col = place_at + (n >> 3)
+            side[(n & 7) + 2, at_col : at_col + 1, :] = cells[16 * i + n : 16 * i + n + 1]
+    put_corner(cells[32:48], 10 - 10 * odd, 6)
+    put_corner(cells[48:64], 10 - 10 * odd, 0)
+    near_border, far_border, near_beyond, far_beyond = 8 - 7 * odd, 1 + 7 * odd, 9 - 9 * odd, 9 * odd
+    taps([near_border])
+
+    pltpu.make_async_copy(corner_in.at[pl.ds(0, 2)], corner_in.at[pl.ds(0, 2)], recv_sem.at[1]).wait()
+    cells = spread_cells([
+        fine_of(corner_in[0], corner_in[0, 8:9, :], 0, far_known),
+        fine_of(corner_in[1], corner_in[1, 8:9, :], 2, far_known),
+    ])
+    put_corner(cells[0:16], 10 * odd, 6)
+    put_corner(cells[16:32], 10 * odd, 0)
     side_lane = jnp.broadcast_to(lane.reshape(1, 1, 128), (10, 8, 128))
-    side_patches = patches(edge[0:10], edge[1:11], edge[2:12], side_lane).reshape(80, 128)
+    side_patches = patches(side[0:10], side[1:11], side[2:12], side_lane).reshape(80, 128)
     side_taps = dot(side_patches, wa[...]).reshape(10, 8, 3 * CH)
     for dx in range(3):
         piece = side_taps[:, :, dx * CH : (dx + 1) * CH]
         gs[dx, :, LEFT:MAIN, :] = piece
         gs[dx, :, RIGHT : RIGHT + 8, :] = piece
-    taps([1, 8])
-    for i in range(1, 9):
+    for i in [near_border] + list(range(2, 8)):
         ha[i, MAIN:RIGHT, :] = joined(i, MAIN, 128)
+
+    @pl.when(early)
+    def _():
+        pltpu.make_async_copy(far_in, far_in, recv_sem.at[13]).wait()
+        xs[1 + 9 * odd] = placed(far_in[0] * far_known)
+
+    @pl.when(jnp.logical_not(early))
+    def _():
+        pltpu.make_async_copy(row_in, row_in, recv_sem.at[0]).wait()
+        xs[1 + 9 * odd] = spread_cells([fine_of(row_in[0:128, :], row_in[128:129, :], 1, far_known)]).astype(BF16)
+
+    taps([far_border])
+    ha[far_border, MAIN:RIGHT, :] = joined(far_border, MAIN, 128)
 
     def all_reduce(turn, mean, dev, beside):
         cells = ROWS_DEV * COLS_DEV
@@ -437,16 +464,20 @@
         for load in loads[3:]:
             load.wait()
         prepare_b(cb_v, wba, wbb)
-        pltpu.make_async_copy(next_in, next_in, recv_sem.at[12]).wait()
-        xs[11 * odd] = placed(next_in[...] * far_known)
-        taps([0, 9])
-        for i in (0, 9):
+
+        @pl.when(jnp.logical_not(early))
+        def _():
+            pltpu.make_async_copy(far_in, far_in, recv_sem.at[13]).wait()
+
+        xs[11 * odd] = placed(far_in[1] * far_known)
+        taps([near_beyond, far_beyond])
+        for i in (near_beyond, far_beyond):
             ha[i, MAIN:RIGHT, :] = joined(i, MAIN, 128)
         for i in range(10):
             hl[0, i : i + 1, :] = joined(i, MAIN - 1, 1)
             hl[1, i : i + 1, :] = joined(i, RIGHT, 1)
 
-    mean, dev = local_stats([ha[i, MAIN:RIGHT, :] for i in range(1, 9)])
+    mean, dev = local_stats([ha[i, MAIN:RIGHT, :] for i in [2, 3, 4, 5, 6, 7, near_border, far_border]])
     mean, inverse = all_reduce(0, mean, dev, around_a)
 
     second_conv(ha, hl, act, gs, hb, wba, wbb, mean, inverse * vec_v[0], vec_v[1], not_first, not_last)
@@ -459,11 +490,15 @@
     fin_ref[2:3, :] = vec_v[3]
     store.wait()
 
-    pltpu.make_async_copy(row_in, row_in, send_sem.at[0]).wait()
-    pltpu.make_async_copy(corner_in, corner_in, send_sem.at[1]).wait()
+    @pl.when(early)
+    def _():
+        pltpu.make_async_copy(row_in, row_in, send_sem.at[0]).wait()
+
+    pltpu.make_async_copy(far_in, far_in, send_sem.at[10]).wait()
+    pltpu.make_async_copy(corner_in.at[pl.ds(0, 2)], corner_in.at[pl.ds(0, 2)], send_sem.at[1]).wait()
+    pltpu.make_async_copy(corner_in.at[pl.ds(2, 2)], corner_in.at[pl.ds(2, 2)], send_sem.at[9]).wait()
     pltpu.make_async_copy(col_in, col_in, send_sem.at[8]).wait()
     pltpu.make_async_copy(mate_in, mate_in, send_sem.at[2]).wait()
-    pltpu.make_async_copy(next_in, next_in, send_sem.at[9]).wait()
     pltpu.make_async_copy(tt.at[pl.ds(0, 4)], tt.at[pl.ds(0, 4)], send_sem.at[7]).wait()
     for turn in range(2):
         pltpu.make_async_copy(buf_z.at[turn], buf_z.at[turn], send_sem.at[3 + 2 * turn]).wait()
@@ -496,15 +531,15 @@
             pltpu.VMEM((2, 32, 128), BF16),
             pltpu.VMEM((4, 16, 128), BF16),
             pltpu.VMEM((2, 16, 128), F32),
-            pltpu.VMEM((16, 128), F32),
+            pltpu.VMEM((2, 16, 128), F32),
             pltpu.VMEM((144, 128), BF16),
             pltpu.VMEM((2, 32, 128), BF16),
             pltpu.VMEM((4, 16, 128), BF16),
             pltpu.VMEM((2, 16, 128), F32),
-            pltpu.VMEM((16, 128), F32),
+            pltpu.VMEM((2, 16, 128), F32),
             pltpu.VMEM((128, BLK_DEV * 128), BF16),
             pltpu.VMEM((80, BLK_DEV * 128), F32),
-            pltpu.VMEM((96, 128), F32),
+            pltpu.VMEM((12, 8, 128), F32),
             pltpu.VMEM((128, 3 * CH), F32),
             pltpu.VMEM((128, 3 * CH), BF16),
             pltpu.VMEM((9 * CH, 2 * CH), BF16),
@@ -520,8 +555,8 @@
             pltpu.VMEM((2, 31, 2, CH), F32),
             pltpu.SemaphoreType.DMA((9,)),
             pltpu.SemaphoreType.DMA,
-            pltpu.SemaphoreType.DMA((10,)),
-            pltpu.SemaphoreType.DMA((13,)),
+            pltpu.SemaphoreType.DMA((11,)),
+            pltpu.SemaphoreType.DMA((14,)),
         ],
         compiler_params=pltpu.CompilerParams(
             collective_id=0, has_side_effects=True, vmem_limit_bytes=60 * 1024 * 1024

time: 55 us -> 57.5 us (1.045)
  Pallas kernels: 53.3 us -> 55.9 us
    pallas_call x1, Pallas kernels: 53.3 us -> 55.9 us  [per_device(): pl.pallas_call(kernel, name='stem', out_shape=(pltpu.VMEM((ROWS_DEV, COLS...]
where the time goes in v7:
time: 57.5 us; the launch traced here: 57.4 us
  Pallas kernels  55.9 us (97%)
  other arithmetic  0.87 us (2%)
  between operations  0.67 us (1%)
    pallas_call x1, Pallas kernels, per_device(): pl.pallas_call(kernel, name='stem', out_shape=(pltpu.VMEM((ROWS_DEV, COLS...  55.9 us

profile of v7, /device:TPU:1, one launch (start us, length us, event | category | flops | bytes accessed | tf_op | source)
XLA Modules:
  0.0 57.4 jit_solution(3927093598454002913)
XLA Ops:
  0.7 55.9 %stem.1 = (f32[8,128,128]{2,1,0:T(8,128)S(1)}, f32[3,128]{1,0:T(4,128)S(1)}) custom-call(s32[1,4]{1,0:T(1,128)} %src_hbm.1, s32[1]{0:T(128)S(6)} %copy.11.cnt_ref, bf16[12,4,32]{2,1,0:T(4,128)(2,1)} %bitcast.13, bf16[128,1024]{1,0:T(8,128)(2,1)} %bitcast.12, f32[3,3,12,128]{3,2,1,0:T(8,128)} %ca_ref.1, f32[3,3,128,128]{3,2,1,0:T(8,128)} %cb_ref.1, ...), custom_call_target="tpu_custom_call" | custom-call | tf_op jit(solution)/shard_map/stem/pallas_call | solution.py:513
  56.5 0.9 %multiply_convert_fusion = bf16[8,128,128]{2,1,0:T(8,128)(2,1)} fusion(f32[8,128,128]{2,1,0:T(8,128)S(1)} %get-tuple-element.7, f32[128]{0:T(128)S(1)} %get-tuple-element.10, f32[128]{0:T(128)S(1)} %get-tuple-element.11, f32[128]{0:T(128)S(1)} %get-tuple-element.9), kind=kLoop, calls=%fused_computation | loop fusion | flops 1048576 | bytes 787968 | tf_op jit(solution)/shard_map/convert_element_type | solution.py:569
  (1 shorter events, 0.0 us)

commit v8 on v7

--- a/solution.py
+++ b/solution.py
@@ -89,18 +89,23 @@
     return total
 
 
-def local_stats(rows):
-    cells = len(rows) * rows[0].shape[0]
-    about = jnp.sum(rows[0], axis=0, keepdims=True) * (1.0 / rows[0].shape[0])
-    first, second = 0.0, 0.0
+def add_rows(rows, about, first=0.0, second=0.0):
     for r in rows:
         off = r - about
         first = first + off
         second = second + off * off
+    return first, second
+
+
+def row_mean(r):
+    return jnp.sum(r, axis=0, keepdims=True) * (1.0 / r.shape[0])
+
+
+def channel_stats(about, first, second):
+    cells = ROWS_DEV * COLS_DEV
     first = jnp.sum(first, axis=0, keepdims=True)
     mean_off = first * (1.0 / cells)
-    dev = jnp.sum(second, axis=0, keepdims=True) - first * mean_off
-    return about + mean_off, dev
+    return about + mean_off, jnp.sum(second, axis=0, keepdims=True) - first * mean_off
 
 
 def to_groups(mean, dev, cells):
@@ -188,8 +193,8 @@
     src_hbm, cnt_ref, coarse_ref, remap_ref, ca_ref, cb_ref, gain_a_ref, shift_a_ref, gain_b_ref, shift_b_ref,
     hb_ref, fin_ref,
     src_ref, coarse_v, remap_v, ca_v, cb_v, vec_v,
-    tt, row_out, col_out, corner_out, mate_out, far_out,
-    row_in, col_in, corner_in, mate_in, far_in,
+    tt, row_out, col_out, corner_out, mate_out, next_out, choice_out,
+    row_in, col_in, corner_in, mate_in, next_in, choice_in,
     copies, choices, side, wa32, wa, wba, wbb,
     xs, gs, ha, hl, act, hb,
     stat, buf_x, buf_z,
@@ -203,7 +208,6 @@
     lon_left, lon_right = lax.rem(lon + 31, 32), lax.rem(lon + 1, 32)
     odd = lax.rem(row, 2)
     is_odd = odd == 1
-    early = lax.rem(lax.div(row, 2), 2) == 0
     near_row = row + 1 - 2 * odd
     far_row = lax.rem(row + 2 * odd + 15, 16)
     halo = [
@@ -261,14 +265,14 @@
         cell = jnp.where((at >= 160 + 16 * i) & (at < 176 + 16 * i), here, cell)
     pick = jnp.where(iota((224, 1024), 1) == cell, 1.0, 0.0).astype(BF16)
     weights = dot(pick, remap_v[...], ((1,), (1,))).astype(BF16)
-    row_out[0:128, :] = weights[0:128]
-    row_out[128:144, :] = choice_tile
+    row_out[...] = weights[0:128]
+    choice_out[...] = own_choice
     for i in range(2):
         col_out[i, 0:16, :] = weights[128 + 16 * i : 144 + 16 * i]
         col_out[i, 16:32, :] = choice_tile
     for i in range(4):
         cells = weights[160 + 16 * i : 176 + 16 * i].astype(F32)
-        corner_out[i] = jnp.where(iota((16, 128), 0) < 8, cells, own_choice).astype(BF16)
+        corner_out[i] = jnp.where(iota((8, 128), 0) < 4, cells[0:8], own_choice)
     side[...] = jnp.zeros_like(side)
     hl[...] = jnp.zeros_like(hl)
     xs[...] = jnp.zeros_like(xs)
@@ -305,16 +309,14 @@
         )
         copy.start()
 
-    @pl.when(early)
-    def _():
-        send(row_out, row_in, halo[0], 0, 0)
-
+    send(row_out, row_in, halo[0], 0, 0)
+    send(choice_out, choice_in, halo[0], 11, 14)
     for i in range(2):
-        send(corner_out.at[i], corner_in.at[i], halo[1 + i], 1, 1)
+        send(corner_out.at[i, pl.ds(0, 5)], corner_in.at[i, pl.ds(0, 5)], halo[1 + i], 1, 1)
     for i in range(2):
         send(col_out.at[i], col_in.at[i], halo[6 + i], 8, 2)
-    for i in range(2):
-        send(corner_out.at[2 + i], corner_in.at[2 + i], halo[4 + i], 9, 12)
+    for i in range(2, 4):
+        send(corner_out.at[i, pl.ds(0, 5)], corner_in.at[i, pl.ds(0, 5)], halo[2 + i], 9, 12)
     along_lon = [
         pltpu.make_async_remote_copy(
             src_ref=tt.at[2], dst_ref=tt.at[slot], send_sem=send_sem.at[7], recv_sem=recv_sem.at[8 + i],
@@ -342,9 +344,8 @@
     four = dot(blocks, four)
     mate_out[0] = jnp.where(is_odd, four[:, 0:128], four[:, 384:512])
     mate_out[1] = jnp.where(is_odd, four[:, 128:256], four[:, 256:384])
-    far_out[0] = jnp.where(is_odd, four[:, 384:512], four[:, 0:128])
-    far_out[1] = jnp.where(is_odd, four[:, 256:384], four[:, 128:256])
-    send(far_out, far_in, halo[0], 10, 13)
+    next_out[...] = jnp.where(is_odd, four[:, 256:384], four[:, 128:256])
+    send(next_out, next_in, halo[0], 10, 13)
     send(mate_out, mate_in, halo[3], 2, 3)
 
     spread_blocks = dot(blocks, spread_var, ((0,), (0,))).astype(BF16)
@@ -385,7 +386,7 @@
 
     def fine_of(cells, choice, first_tile, known):
         held = chosen(choice.astype(F32), first_tile) * known
-        return dot(cells, held.astype(BF16), ((1,), (1,)))
+        return dot(cells.astype(BF16), held.astype(BF16), ((1,), (1,)))
 
     def spread_cells(parts):
         high, low = split(jnp.concatenate(parts, axis=0))
@@ -395,52 +396,59 @@
         for n in range(4):
             side[first_row + (n >> 1), place + (n & 1) : place + (n & 1) + 1, :] = cells[n : n + 1]
 
+    def corners(first):
+        some = corner_in.at[pl.ds(first, 2), pl.ds(0, 5)]
+        return pltpu.make_async_copy(some, some, recv_sem.at[1 if first == 0 else 12])
+
     pltpu.make_async_copy(col_in, col_in, recv_sem.at[2]).wait()
-    pltpu.make_async_copy(corner_in.at[pl.ds(2, 2)], corner_in.at[pl.ds(2, 2)], recv_sem.at[12]).wait()
+    corners(2).wait()
     cells = spread_cells([
         fine_of(col_in[0, 0:16, :], col_in[0, 16:17, :], 0, 1.0),
         fine_of(col_in[1, 0:16, :], col_in[1, 16:17, :], 2, 1.0),
-        fine_of(corner_in[2], corner_in[2, 8:9, :], 0, 1.0),
-        fine_of(corner_in[3], corner_in[3, 8:9, :], 2, 1.0),
+        fine_of(corner_in[2], corner_in[2, 4:5, :], 0, 1.0),
+        fine_of(corner_in[3], corner_in[3, 4:5, :], 2, 1.0),
     ])
     for i, place_at in enumerate((6, 0)):
         for n in range(16):
             at_col = place_at + (n >> 3)
             side[(n & 7) + 2, at_col : at_col + 1, :] = cells[16 * i + n : 16 * i + n + 1]
-    put_corner(cells[32:48], 10 - 10 * odd, 6)
-    put_corner(cells[48:64], 10 - 10 * odd, 0)
+    put_corner(cells[32:40], 10 - 10 * odd, 6)
+    put_corner(cells[40:48], 10 - 10 * odd, 0)
     near_border, far_border, near_beyond, far_beyond = 8 - 7 * odd, 1 + 7 * odd, 9 - 9 * odd, 9 * odd
     taps([near_border])
 
-    pltpu.make_async_copy(corner_in.at[pl.ds(0, 2)], corner_in.at[pl.ds(0, 2)], recv_sem.at[1]).wait()
+    def side_taps():
+        side_lane = jnp.broadcast_to(lane.reshape(1, 1, 128), (10, 8, 128))
+        side_patches = patches(side[0:10], side[1:11], side[2:12], side_lane).reshape(80, 128)
+        result = dot(side_patches, wa[...]).reshape(10, 8, 3 * CH)
+        for dx in range(3):
+            piece = result[:, :, dx * CH : (dx + 1) * CH]
+            gs[dx, :, LEFT:MAIN, :] = piece
+            gs[dx, :, RIGHT : RIGHT + 8, :] = piece
+
+    side_taps()
+    inner_rows = [2, 3, 4, 5, 6, 7, near_border]
+    for i in inner_rows:
+        ha[i, MAIN:RIGHT, :] = joined(i, MAIN, 128)
+    about = row_mean(ha[2, MAIN:RIGHT, :])
+    first, second = add_rows([ha[i, MAIN:RIGHT, :] for i in inner_rows], about)
+
+    corners(0).wait()
+    pltpu.make_async_copy(choice_in, choice_in, recv_sem.at[14]).wait()
+    pltpu.make_async_copy(row_in, row_in, recv_sem.at[0]).wait()
     cells = spread_cells([
-        fine_of(corner_in[0], corner_in[0, 8:9, :], 0, far_known),
-        fine_of(corner_in[1], corner_in[1, 8:9, :], 2, far_known),
+        fine_of(row_in[...], choice_in[...], 1, far_known),
+        fine_of(corner_in[0], corner_in[0, 4:5, :], 0, far_known),
+        fine_of(corner_in[1], corner_in[1, 4:5, :], 2, far_known),
     ])
-    put_corner(cells[0:16], 10 * odd, 6)
-    put_corner(cells[16:32], 10 * odd, 0)
-    side_lane = jnp.broadcast_to(lane.reshape(1, 1, 128), (10, 8, 128))
-    side_patches = patches(side[0:10], side[1:11], side[2:12], side_lane).reshape(80, 128)
-    side_taps = dot(side_patches, wa[...]).reshape(10, 8, 3 * CH)
-    for dx in range(3):
-        piece = side_taps[:, :, dx * CH : (dx + 1) * CH]
-        gs[dx, :, LEFT:MAIN, :] = piece
-        gs[dx, :, RIGHT : RIGHT + 8, :] = piece
-    for i in [near_border] + list(range(2, 8)):
-        ha[i, MAIN:RIGHT, :] = joined(i, MAIN, 128)
-
-    @pl.when(early)
-    def _():
-        pltpu.make_async_copy(far_in, far_in, recv_sem.at[13]).wait()
-        xs[1 + 9 * odd] = placed(far_in[0] * far_known)
-
-    @pl.when(jnp.logical_not(early))
-    def _():
-        pltpu.make_async_copy(row_in, row_in, recv_sem.at[0]).wait()
-        xs[1 + 9 * odd] = spread_cells([fine_of(row_in[0:128, :], row_in[128:129, :], 1, far_known)]).astype(BF16)
-
+    xs[1 + 9 * odd] = cells[0:128].astype(BF16)
+    put_corner(cells[128:136], 10 * odd, 6)
+    put_corner(cells[136:144], 10 * odd, 0)
+    side_taps()
     taps([far_border])
-    ha[far_border, MAIN:RIGHT, :] = joined(far_border, MAIN, 128)
+    border = joined(far_border, MAIN, 128)
+    ha[far_border, MAIN:RIGHT, :] = border
+    mean, dev = channel_stats(about, *add_rows([border], about, first, second))
 
     def all_reduce(turn, mean, dev, beside):
         cells = ROWS_DEV * COLS_DEV
@@ -464,12 +472,8 @@
         for load in loads[3:]:
             load.wait()
         prepare_b(cb_v, wba, wbb)
-
-        @pl.when(jnp.logical_not(early))
-        def _():
-            pltpu.make_async_copy(far_in, far_in, recv_sem.at[13]).wait()
-
-        xs[11 * odd] = placed(far_in[1] * far_known)
+        pltpu.make_async_copy(next_in, next_in, recv_sem.at[13]).wait()
+        xs[11 * odd] = placed(next_in[...] * far_known)
         taps([near_beyond, far_beyond])
         for i in (near_beyond, far_beyond):
             ha[i, MAIN:RIGHT, :] = joined(i, MAIN, 128)
@@ -477,26 +481,25 @@
             hl[0, i : i + 1, :] = joined(i, MAIN - 1, 1)
             hl[1, i : i + 1, :] = joined(i, RIGHT, 1)
 
-    mean, dev = local_stats([ha[i, MAIN:RIGHT, :] for i in [2, 3, 4, 5, 6, 7, near_border, far_border]])
     mean, inverse = all_reduce(0, mean, dev, around_a)
 
     second_conv(ha, hl, act, gs, hb, wba, wbb, mean, inverse * vec_v[0], vec_v[1], not_first, not_last)
     store = pltpu.make_async_copy(hb, hb_ref, out_sem)
     store.start()
-    mean, dev = local_stats([hb[i] for i in range(8)])
+    about = row_mean(hb[0])
+    mean, dev = channel_stats(about, *add_rows([hb[i] for i in range(8)], about))
     mean, inverse = all_reduce(1, mean, dev, lambda: None)
     fin_ref[0:1, :] = mean
     fin_ref[1:2, :] = inverse * vec_v[2]
     fin_ref[2:3, :] = vec_v[3]
     store.wait()
 
-    @pl.when(early)
-    def _():
-        pltpu.make_async_copy(row_in, row_in, send_sem.at[0]).wait()
-
-    pltpu.make_async_copy(far_in, far_in, send_sem.at[10]).wait()
-    pltpu.make_async_copy(corner_in.at[pl.ds(0, 2)], corner_in.at[pl.ds(0, 2)], send_sem.at[1]).wait()
-    pltpu.make_async_copy(corner_in.at[pl.ds(2, 2)], corner_in.at[pl.ds(2, 2)], send_sem.at[9]).wait()
+    pltpu.make_async_copy(row_in, row_in, send_sem.at[0]).wait()
+    pltpu.make_async_copy(choice_in, choice_in, send_sem.at[11]).wait()
+    pltpu.make_async_copy(next_in, next_in, send_sem.at[10]).wait()
+    for first, sem in ((0, 1), (2, 9)):
+        some = corner_in.at[pl.ds(first, 2), pl.ds(0, 5)]
+        pltpu.make_async_copy(some, some, send_sem.at[sem]).wait()
     pltpu.make_async_copy(col_in, col_in, send_sem.at[8]).wait()
     pltpu.make_async_copy(mate_in, mate_in, send_sem.at[2]).wait()
     pltpu.make_async_copy(tt.at[pl.ds(0, 4)], tt.at[pl.ds(0, 4)], send_sem.at[7]).wait()
@@ -527,16 +530,18 @@
             pltpu.VMEM((3, 3, CH, CH), F32),
             pltpu.VMEM((4, 1, CH), F32),
             pltpu.VMEM((5, 16, 128), BF16),
-            pltpu.VMEM((144, 128), BF16),
+            pltpu.VMEM((128, 128), BF16),
             pltpu.VMEM((2, 32, 128), BF16),
-            pltpu.VMEM((4, 16, 128), BF16),
+            pltpu.VMEM((4, 8, 128), F32),
             pltpu.VMEM((2, 16, 128), F32),
+            pltpu.VMEM((16, 128), F32),
+            pltpu.VMEM((1, 128), F32),
+            pltpu.VMEM((128, 128), BF16),
+            pltpu.VMEM((2, 32, 128), BF16),
+            pltpu.VMEM((4, 8, 128), F32),
             pltpu.VMEM((2, 16, 128), F32),
-            pltpu.VMEM((144, 128), BF16),
-            pltpu.VMEM((2, 32, 128), BF16),
-            pltpu.VMEM((4, 16, 128), BF16),
-            pltpu.VMEM((2, 16, 128), F32),
-            pltpu.VMEM((2, 16, 128), F32),
+            pltpu.VMEM((16, 128), F32),
+            pltpu.VMEM((1, 128), F32),
             pltpu.VMEM((128, BLK_DEV * 128), BF16),
             pltpu.VMEM((80, BLK_DEV * 128), F32),
             pltpu.VMEM((12, 8, 128), F32),
@@ -555,8 +560,8 @@
             pltpu.VMEM((2, 31, 2, CH), F32),
             pltpu.SemaphoreType.DMA((9,)),
             pltpu.SemaphoreType.DMA,
-            pltpu.SemaphoreType.DMA((11,)),
-            pltpu.SemaphoreType.DMA((14,)),
+            pltpu.SemaphoreType.DMA((12,)),
+            pltpu.SemaphoreType.DMA((15,)),
         ],
         compiler_params=pltpu.CompilerParams(
             collective_id=0, has_side_effects=True, vmem_limit_bytes=60 * 1024 * 1024

time: 57.5 us -> 54.8 us (0.953)
  Pallas kernels: 55.9 us -> 53.1 us
    pallas_call x1, Pallas kernels: 55.9 us -> 53.1 us  [per_device(): pl.pallas_call(kernel, name='stem', out_shape=(pltpu.VMEM((ROWS_DEV, COLS...]
where the time goes in v8:
time: 54.8 us; the launch traced here: 54.7 us
  Pallas kernels  53.1 us (97%)
  other arithmetic  0.87 us (2%)
  between operations  0.67 us (1%)
    pallas_call x1, Pallas kernels, per_device(): pl.pallas_call(kernel, name='stem', out_shape=(pltpu.VMEM((ROWS_DEV, COLS...  53.1 us

profile of v8, /device:TPU:1, one launch (start us, length us, event | category | flops | bytes accessed | tf_op | source)
XLA Modules:
  0.0 54.7 jit_solution(12306975766606698633)
XLA Ops:
  0.7 53.1 %stem.1 = (f32[8,128,128]{2,1,0:T(8,128)S(1)}, f32[3,128]{1,0:T(4,128)S(1)}) custom-call(s32[1,4]{1,0:T(1,128)} %src_hbm.1, s32[1]{0:T(128)S(6)} %copy.11.cnt_ref, bf16[12,4,32]{2,1,0:T(4,128)(2,1)} %bitcast.13, bf16[128,1024]{1,0:T(8,128)(2,1)} %bitcast.12, f32[3,3,12,128]{3,2,1,0:T(8,128)} %ca_ref.1, f32[3,3,128,128]{3,2,1,0:T(8,128)} %cb_ref.1, ...), custom_call_target="tpu_custom_call" | custom-call | tf_op jit(solution)/shard_map/stem/pallas_call | solution.py:516
  53.8 0.9 %multiply_convert_fusion = bf16[8,128,128]{2,1,0:T(8,128)(2,1)} fusion(f32[8,128,128]{2,1,0:T(8,128)S(1)} %get-tuple-element.7, f32[128]{0:T(128)S(1)} %get-tuple-element.10, f32[128]{0:T(128)S(1)} %get-tuple-element.11, f32[128]{0:T(128)S(1)} %get-tuple-element.9), kind=kLoop, calls=%fused_computation | loop fusion | flops 1048576 | bytes 787968 | tf_op jit(solution)/shard_map/convert_element_type | solution.py:574
  (1 shorter events, 0.0 us)

commit v9 on v8

--- a/solution.py
+++ b/solution.py
@@ -309,14 +309,13 @@
         )
         copy.start()
 
+    for i in range(2):
+        send(col_out.at[i], col_in.at[i], halo[6 + i], 8, 2)
+    for i in range(4):
+        out, into = (1, 1) if i < 2 else (9, 12)
+        send(corner_out.at[i, pl.ds(0, 5)], corner_in.at[i, pl.ds(0, 5)], halo[(1, 2, 4, 5)[i]], out, into)
     send(row_out, row_in, halo[0], 0, 0)
     send(choice_out, choice_in, halo[0], 11, 14)
-    for i in range(2):
-        send(corner_out.at[i, pl.ds(0, 5)], corner_in.at[i, pl.ds(0, 5)], halo[1 + i], 1, 1)
-    for i in range(2):
-        send(col_out.at[i], col_in.at[i], halo[6 + i], 8, 2)
-    for i in range(2, 4):
-        send(corner_out.at[i, pl.ds(0, 5)], corner_in.at[i, pl.ds(0, 5)], halo[2 + i], 9, 12)
     along_lon = [
         pltpu.make_async_remote_copy(
             src_ref=tt.at[2], dst_ref=tt.at[slot], send_sem=send_sem.at[7], recv_sem=recv_sem.at[8 + i],

time: 54.8 us -> 54.5 us (level)
  no operation moved by 1% of the time
where the time goes in v9:
time: 54.5 us; the launch traced here: 54.4 us
  Pallas kernels  52.8 us (97%)
  other arithmetic  0.87 us (2%)
  between operations  0.67 us (1%)
    pallas_call x1, Pallas kernels, per_device(): pl.pallas_call(kernel, name='stem', out_shape=(pltpu.VMEM((ROWS_DEV, COLS...  52.8 us

profile of v9, /device:TPU:1, one launch (start us, length us, event | category | flops | bytes accessed | tf_op | source)
XLA Modules:
  0.0 54.4 jit_solution(1531936216167579220)
XLA Ops:
  0.7 52.8 %stem.1 = (f32[8,128,128]{2,1,0:T(8,128)S(1)}, f32[3,128]{1,0:T(4,128)S(1)}) custom-call(s32[1,4]{1,0:T(1,128)} %src_hbm.1, s32[1]{0:T(128)S(6)} %copy.11.cnt_ref, bf16[12,4,32]{2,1,0:T(4,128)(2,1)} %bitcast.13, bf16[128,1024]{1,0:T(8,128)(2,1)} %bitcast.12, f32[3,3,12,128]{3,2,1,0:T(8,128)} %ca_ref.1, f32[3,3,128,128]{3,2,1,0:T(8,128)} %cb_ref.1, ...), custom_call_target="tpu_custom_call" | custom-call | tf_op jit(solution)/shard_map/stem/pallas_call | solution.py:515
  53.5 0.9 %multiply_convert_fusion = bf16[8,128,128]{2,1,0:T(8,128)(2,1)} fusion(f32[8,128,128]{2,1,0:T(8,128)S(1)} %get-tuple-element.7, f32[128]{0:T(128)S(1)} %get-tuple-element.10, f32[128]{0:T(128)S(1)} %get-tuple-element.11, f32[128]{0:T(128)S(1)} %get-tuple-element.9), kind=kLoop, calls=%fused_computation | loop fusion | flops 1048576 | bytes 787968 | tf_op jit(solution)/shard_map/convert_element_type | solution.py:573
  (1 shorter events, 0.0 us)

commit v10 on v8

--- a/solution.py
+++ b/solution.py
@@ -117,12 +117,11 @@
 
 def merge(mean, dev, others, cells):
     count = others.shape[0] + 1
-    means = others[:, 0:1, :]
-    whole = (mean + jnp.sum(means, axis=0)) * (1.0 / count)
-    off = means - whole
-    own = mean - whole
-    spread = own * own + jnp.sum(off * off, axis=0)
-    return whole, dev + jnp.sum(others[:, 1:2, :], axis=0) + cells * spread
+    off = others[:, 0:1, :] - mean
+    first = jnp.sum(off, axis=0)
+    second = jnp.sum(others[:, 1:2, :] + cells * (off * off), axis=0)
+    mean_off = first * (1.0 / count)
+    return mean + mean_off, dev + second - cells * first * mean_off
 
 
 LEFT, MAIN, RIGHT, WIDE = 8, 16, 144, 160
@@ -208,6 +207,7 @@
     lon_left, lon_right = lax.rem(lon + 31, 32), lax.rem(lon + 1, 32)
     odd = lax.rem(row, 2)
     is_odd = odd == 1
+    has_far = jnp.where(is_odd, row < 15, row > 0)
     near_row = row + 1 - 2 * odd
     far_row = lax.rem(row + 2 * odd + 15, 16)
     halo = [
@@ -215,7 +215,13 @@
         (near_row, lon_right), (near_row, lon_left), (row, lon_right), (row, lon_left),
     ]
     barrier = pltpu.get_barrier_semaphore()
-    partners = halo + lon_mates + z_mates + xy_mates
+    partners = halo[3:] + lon_mates + z_mates + xy_mates
+
+    @pl.when(has_far)
+    def _():
+        for mate in halo[:3]:
+            pl.semaphore_signal(barrier, inc=1, device_id=mate, device_id_type=MESH)
+
     for mate in partners:
         pl.semaphore_signal(barrier, inc=1, device_id=mate, device_id_type=MESH)
 
@@ -300,7 +306,14 @@
     not_first = jnp.where(row > 0, 1.0, 0.0).astype(F32)
     not_last = jnp.where(row < 15, 1.0, 0.0).astype(F32)
 
-    pl.semaphore_wait(barrier, len(partners))
+    @pl.when(jnp.logical_not(has_far))
+    def _():
+        row_in[...] = jnp.zeros_like(row_in)
+        choice_in[...] = jnp.zeros_like(choice_in)
+        next_in[...] = jnp.zeros_like(next_in)
+        corner_in[0:2] = jnp.zeros((2, 8, 128), F32)
+
+    pl.semaphore_wait(barrier, len(partners) + 3 * jnp.where(has_far, 1, 0))
 
     def send(src, dst, mate, out, into):
         copy = pltpu.make_async_remote_copy(
@@ -309,14 +322,18 @@
         )
         copy.start()
 
-    send(row_out, row_in, halo[0], 0, 0)
-    send(choice_out, choice_in, halo[0], 11, 14)
-    for i in range(2):
-        send(corner_out.at[i, pl.ds(0, 5)], corner_in.at[i, pl.ds(0, 5)], halo[1 + i], 1, 1)
     for i in range(2):
         send(col_out.at[i], col_in.at[i], halo[6 + i], 8, 2)
-    for i in range(2, 4):
+    for i in (2, 3):
         send(corner_out.at[i, pl.ds(0, 5)], corner_in.at[i, pl.ds(0, 5)], halo[2 + i], 9, 12)
+
+    @pl.when(has_far)
+    def _():
+        for i in (0, 1):
+            send(corner_out.at[i, pl.ds(0, 5)], corner_in.at[i, pl.ds(0, 5)], halo[1 + i], 1, 1)
+        send(row_out, row_in, halo[0], 0, 0)
+        send(choice_out, choice_in, halo[0], 11, 14)
+
     along_lon = [
         pltpu.make_async_remote_copy(
             src_ref=tt.at[2], dst_ref=tt.at[slot], send_sem=send_sem.at[7], recv_sem=recv_sem.at[8 + i],
@@ -345,8 +362,12 @@
     mate_out[0] = jnp.where(is_odd, four[:, 0:128], four[:, 384:512])
     mate_out[1] = jnp.where(is_odd, four[:, 128:256], four[:, 256:384])
     next_out[...] = jnp.where(is_odd, four[:, 256:384], four[:, 128:256])
-    send(next_out, next_in, halo[0], 10, 13)
     send(mate_out, mate_in, halo[3], 2, 3)
+
+    @pl.when(has_far)
+    def _():
+        send(next_out, next_in, halo[0], 10, 13)
+
 
     spread_blocks = dot(blocks, spread_var, ((0,), (0,))).astype(BF16)
     fine = dot(remap_v[...], spread_blocks, ((0,), (0,)))
@@ -433,9 +454,12 @@
     about = row_mean(ha[2, MAIN:RIGHT, :])
     first, second = add_rows([ha[i, MAIN:RIGHT, :] for i in inner_rows], about)
 
-    corners(0).wait()
-    pltpu.make_async_copy(choice_in, choice_in, recv_sem.at[14]).wait()
-    pltpu.make_async_copy(row_in, row_in, recv_sem.at[0]).wait()
+    @pl.when(has_far)
+    def _():
+        corners(0).wait()
+        pltpu.make_async_copy(choice_in, choice_in, recv_sem.at[14]).wait()
+        pltpu.make_async_copy(row_in, row_in, recv_sem.at[0]).wait()
+
     cells = spread_cells([
         fine_of(row_in[...], choice_in[...], 1, far_known),
         fine_of(corner_in[0], corner_in[0, 4:5, :], 0, far_known),
@@ -461,25 +485,33 @@
                     src_ref=stat.at[turn, stage], dst_ref=buf.at[turn, j], send_sem=send_sem.at[sem - 1], recv_sem=recv_sem.at[sem],
                     device_id=mate, device_id_type=MESH,
                 ).start()
-            if stage == 0:
-                beside()
+            beside(stage)
             pltpu.make_async_copy(buf.at[turn], buf.at[turn], recv_sem.at[sem]).wait()
             mean, dev = merge(mean, dev, buf[turn], cells)
             cells = cells * (len(mates) + 1)
         return to_groups(mean, dev, cells)
 
-    def around_a():
-        for load in loads[3:]:
-            load.wait()
-        prepare_b(cb_v, wba, wbb)
-        pltpu.make_async_copy(next_in, next_in, recv_sem.at[13]).wait()
-        xs[11 * odd] = placed(next_in[...] * far_known)
-        taps([near_beyond, far_beyond])
-        for i in (near_beyond, far_beyond):
+    def around_a(stage):
+        if stage == 0:
+
+            for load in loads[3:]:
+                load.wait()
+            prepare_b(cb_v, wba, wbb)
+            new_rows, all_rows = [near_beyond], list(range(1, 9)) + [near_beyond]
+        else:
+
+            @pl.when(has_far)
+            def _():
+                pltpu.make_async_copy(next_in, next_in, recv_sem.at[13]).wait()
+
+            xs[11 * odd] = placed(next_in[...] * far_known)
+            new_rows, all_rows = [far_beyond], [far_beyond]
+        taps(new_rows)
+        for i in new_rows:
             ha[i, MAIN:RIGHT, :] = joined(i, MAIN, 128)
-        for i in range(10):
-            hl[0, i : i + 1, :] = joined(i, MAIN - 1, 1)
-            hl[1, i : i + 1, :] = joined(i, RIGHT, 1)
+        for i in all_rows:
+            hl[0, pl.ds(i, 1), :] = joined(i, MAIN - 1, 1)
+            hl[1, pl.ds(i, 1), :] = joined(i, RIGHT, 1)
 
     mean, inverse = all_reduce(0, mean, dev, around_a)
 
@@ -488,18 +520,22 @@
     store.start()
     about = row_mean(hb[0])
     mean, dev = channel_stats(about, *add_rows([hb[i] for i in range(8)], about))
-    mean, inverse = all_reduce(1, mean, dev, lambda: None)
+    mean, inverse = all_reduce(1, mean, dev, lambda stage: None)
     fin_ref[0:1, :] = mean
     fin_ref[1:2, :] = inverse * vec_v[2]
     fin_ref[2:3, :] = vec_v[3]
     store.wait()
 
-    pltpu.make_async_copy(row_in, row_in, send_sem.at[0]).wait()
-    pltpu.make_async_copy(choice_in, choice_in, send_sem.at[11]).wait()
-    pltpu.make_async_copy(next_in, next_in, send_sem.at[10]).wait()
-    for first, sem in ((0, 1), (2, 9)):
-        some = corner_in.at[pl.ds(first, 2), pl.ds(0, 5)]
-        pltpu.make_async_copy(some, some, send_sem.at[sem]).wait()
+    @pl.when(has_far)
+    def _():
+        pltpu.make_async_copy(row_in, row_in, send_sem.at[0]).wait()
+        pltpu.make_async_copy(choice_in, choice_in, send_sem.at[11]).wait()
+        pltpu.make_async_copy(next_in, next_in, send_sem.at[10]).wait()
+        some = corner_in.at[pl.ds(0, 2), pl.ds(0, 5)]
+        pltpu.make_async_copy(some, some, send_sem.at[1]).wait()
+
+    some = corner_in.at[pl.ds(2, 2), pl.ds(0, 5)]
+    pltpu.make_async_copy(some, some, send_sem.at[9]).wait()
     pltpu.make_async_copy(col_in, col_in, send_sem.at[8]).wait()
     pltpu.make_async_copy(mate_in, mate_in, send_sem.at[2]).wait()
     pltpu.make_async_copy(tt.at[pl.ds(0, 4)], tt.at[pl.ds(0, 4)], send_sem.at[7]).wait()

time: 54.8 us -> 53.3 us (0.973)
  Pallas kernels: 53.1 us -> 51.6 us
    pallas_call x1, Pallas kernels: 53.1 us -> 51.6 us  [per_device(): pl.pallas_call(kernel, name='stem', out_shape=(pltpu.VMEM((ROWS_DEV, COLS...]
where the time goes in v10:
time: 53.3 us; the launch traced here: 53.1 us
  Pallas kernels  51.6 us (97%)
  other arithmetic  0.87 us (2%)
  between operations  0.67 us (1%)
    pallas_call x1, Pallas kernels, per_device(): pl.pallas_call(kernel, name='stem', out_shape=(pltpu.VMEM((ROWS_DEV, COLS...  51.6 us

profile of v10, /device:TPU:1, one launch (start us, length us, event | category | flops | bytes accessed | tf_op | source)
XLA Modules:
  0.0 53.1 jit_solution(12637856048113087590)
XLA Ops:
  0.7 51.6 %stem.1 = (f32[8,128,128]{2,1,0:T(8,128)S(1)}, f32[3,128]{1,0:T(4,128)S(1)}) custom-call(s32[1,4]{1,0:T(1,128)} %src_hbm.1, s32[1]{0:T(128)S(6)} %copy.11.cnt_ref, bf16[12,4,32]{2,1,0:T(4,128)(2,1)} %bitcast.13, bf16[128,1024]{1,0:T(8,128)(2,1)} %bitcast.12, f32[3,3,12,128]{3,2,1,0:T(8,128)} %ca_ref.1, f32[3,3,128,128]{3,2,1,0:T(8,128)} %cb_ref.1, ...), custom_call_target="tpu_custom_call" | custom-call | tf_op jit(solution)/shard_map/stem/pallas_call | solution.py:552
  52.3 0.9 %multiply_convert_fusion = bf16[8,128,128]{2,1,0:T(8,128)(2,1)} fusion(f32[8,128,128]{2,1,0:T(8,128)S(1)} %get-tuple-element.7, f32[128]{0:T(128)S(1)} %get-tuple-element.10, f32[128]{0:T(128)S(1)} %get-tuple-element.11, f32[128]{0:T(128)S(1)} %get-tuple-element.9), kind=kLoop, calls=%fused_computation | loop fusion | flops 1048576 | bytes 787968 | tf_op jit(solution)/shard_map/convert_element_type | solution.py:610
  (1 shorter events, 0.0 us)

commit v11 on v10

--- a/solution.py
+++ b/solution.py
@@ -97,31 +97,36 @@
     return first, second
 
 
-def row_mean(r):
-    return jnp.sum(r, axis=0, keepdims=True) * (1.0 / r.shape[0])
-
-
-def channel_stats(about, first, second):
-    cells = ROWS_DEV * COLS_DEV
-    first = jnp.sum(first, axis=0, keepdims=True)
+def group_mean(r):
+    return over_group(jnp.sum(r, axis=0, keepdims=True)) * (1.0 / (PER_GROUP * r.shape[0]))
+
+
+def pack(mean, dev):
+    place = iota((1, CH), 1) & (PER_GROUP - 1)
+    return jnp.where(place == 0, mean, jnp.where(place == 1, dev, 0.0))
+
+
+def group_stats(about, first, second):
+    cells = ROWS_DEV * COLS_DEV * PER_GROUP
+    first = over_group(jnp.sum(first, axis=0, keepdims=True))
+    second = over_group(jnp.sum(second, axis=0, keepdims=True))
     mean_off = first * (1.0 / cells)
-    return about + mean_off, jnp.sum(second, axis=0, keepdims=True) - first * mean_off
-
-
-def to_groups(mean, dev, cells):
-    whole = over_group(mean) * (1.0 / PER_GROUP)
-    apart = mean - whole
-    spread = over_group(dev + cells * (apart * apart)) * (1.0 / (cells * PER_GROUP))
-    return whole, lax.rsqrt(spread + eps)
-
-
-def merge(mean, dev, others, cells):
+    return pack(about + mean_off, second - first * mean_off)
+
+
+def merge(packed, others, cells):
     count = others.shape[0] + 1
-    off = others[:, 0:1, :] - mean
+    off = others - packed
     first = jnp.sum(off, axis=0)
-    second = jnp.sum(others[:, 1:2, :] + cells * (off * off), axis=0)
-    mean_off = first * (1.0 / count)
-    return mean + mean_off, dev + second - cells * first * mean_off
+    apart = cells * (jnp.sum(off * off, axis=0) - first * first * (1.0 / count))
+    return pack(packed + first * (1.0 / count), packed * count + first + pltpu.roll(apart, 1, 1))
+
+
+def unpack(packed, cells):
+    place = iota((1, CH), 1) & (PER_GROUP - 1)
+    mean = over_group(jnp.where(place == 0, packed, 0.0))
+    dev = over_group(jnp.where(place == 1, packed, 0.0))
+    return mean, lax.rsqrt(dev * (1.0 / cells) + eps)
 
 
 LEFT, MAIN, RIGHT, WIDE = 8, 16, 144, 160
@@ -451,7 +456,7 @@
     inner_rows = [2, 3, 4, 5, 6, 7, near_border]
     for i in inner_rows:
         ha[i, MAIN:RIGHT, :] = joined(i, MAIN, 128)
-    about = row_mean(ha[2, MAIN:RIGHT, :])
+    about = group_mean(ha[2, MAIN:RIGHT, :])
     first, second = add_rows([ha[i, MAIN:RIGHT, :] for i in inner_rows], about)
 
     @pl.when(has_far)
@@ -472,14 +477,13 @@
     taps([far_border])
     border = joined(far_border, MAIN, 128)
     ha[far_border, MAIN:RIGHT, :] = border
-    mean, dev = channel_stats(about, *add_rows([border], about, first, second))
-
-    def all_reduce(turn, mean, dev, beside):
-        cells = ROWS_DEV * COLS_DEV
+    sums = group_stats(about, *add_rows([border], about, first, second))
+
+    def all_reduce(turn, packed, beside):
+        cells = ROWS_DEV * COLS_DEV * PER_GROUP
         for stage, (mates, buf) in enumerate(((z_mates, buf_z), (xy_mates, buf_x))):
             sem = 4 + turn * 2 + stage
-            stat[turn, stage, 0:1, :] = mean
-            stat[turn, stage, 1:2, :] = dev
+            stat[turn, stage] = packed
             for j, mate in enumerate(mates):
                 pltpu.make_async_remote_copy(
                     src_ref=stat.at[turn, stage], dst_ref=buf.at[turn, j], send_sem=send_sem.at[sem - 1], recv_sem=recv_sem.at[sem],
@@ -487,9 +491,9 @@
                 ).start()
             beside(stage)
             pltpu.make_async_copy(buf.at[turn], buf.at[turn], recv_sem.at[sem]).wait()
-            mean, dev = merge(mean, dev, buf[turn], cells)
+            packed = merge(packed, buf[turn], cells)
             cells = cells * (len(mates) + 1)
-        return to_groups(mean, dev, cells)
+        return unpack(packed, cells)
 
     def around_a(stage):
         if stage == 0:
@@ -513,14 +517,14 @@
             hl[0, pl.ds(i, 1), :] = joined(i, MAIN - 1, 1)
             hl[1, pl.ds(i, 1), :] = joined(i, RIGHT, 1)
 
-    mean, inverse = all_reduce(0, mean, dev, around_a)
+    mean, inverse = all_reduce(0, sums, around_a)
 
     second_conv(ha, hl, act, gs, hb, wba, wbb, mean, inverse * vec_v[0], vec_v[1], not_first, not_last)
     store = pltpu.make_async_copy(hb, hb_ref, out_sem)
     store.start()
-    about = row_mean(hb[0])
-    mean, dev = channel_stats(about, *add_rows([hb[i] for i in range(8)], about))
-    mean, inverse = all_reduce(1, mean, dev, lambda stage: None)
+    about = group_mean(hb[0])
+    sums = group_stats(about, *add_rows([hb[i] for i in range(8)], about))
+    mean, inverse = all_reduce(1, sums, lambda stage: None)
     fin_ref[0:1, :] = mean
     fin_ref[1:2, :] = inverse * vec_v[2]
     fin_ref[2:3, :] = vec_v[3]
@@ -591,9 +595,9 @@
             pltpu.VMEM((2, 24, CH), F32),
             pltpu.VMEM((10, COLS_DEV, 2 * CH), BF16),
             pltpu.VMEM((ROWS_DEV, COLS_DEV, CH), F32),
-            pltpu.VMEM((2, 2, 2, CH), F32),
-            pltpu.VMEM((2, 15, 2, CH), F32),
-            pltpu.VMEM((2, 31, 2, CH), F32),
+            pltpu.VMEM((2, 2, 1, CH), F32),
+            pltpu.VMEM((2, 15, 1, CH), F32),
+            pltpu.VMEM((2, 31, 1, CH), F32),
             pltpu.SemaphoreType.DMA((9,)),
             pltpu.SemaphoreType.DMA,
             pltpu.SemaphoreType.DMA((12,)),

time: 53.3 us -> 53.1 us (level)
  no operation moved by 1% of the time
where the time goes in v11:
time: 53.1 us; the launch traced here: 53 us
  Pallas kernels  51.4 us (97%)
  other arithmetic  0.87 us (2%)
  between operations  0.67 us (1%)
    pallas_call x1, Pallas kernels, per_device(): pl.pallas_call(kernel, name='stem', out_shape=(pltpu.VMEM((ROWS_DEV, COLS...  51.4 us

profile of v11, /device:TPU:1, one launch (start us, length us, event | category | flops | bytes accessed | tf_op | source)
XLA Modules:
  0.0 53.0 jit_solution(2733321031763293961)
XLA Ops:
  0.7 51.4 %stem.1 = (f32[8,128,128]{2,1,0:T(8,128)S(1)}, f32[3,128]{1,0:T(4,128)S(1)}) custom-call(s32[1,4]{1,0:T(1,128)} %src_hbm.1, s32[1]{0:T(128)S(6)} %copy.11.cnt_ref, bf16[12,4,32]{2,1,0:T(4,128)(2,1)} %bitcast.13, bf16[128,1024]{1,0:T(8,128)(2,1)} %bitcast.12, f32[3,3,12,128]{3,2,1,0:T(8,128)} %ca_ref.1, f32[3,3,128,128]{3,2,1,0:T(8,128)} %cb_ref.1, ...), custom_call_target="tpu_custom_call" | custom-call | tf_op jit(solution)/shard_map/stem/pallas_call | solution.py:556
  52.1 0.9 %multiply_convert_fusion = bf16[8,128,128]{2,1,0:T(8,128)(2,1)} fusion(f32[8,128,128]{2,1,0:T(8,128)S(1)} %get-tuple-element.7, f32[128]{0:T(128)S(1)} %get-tuple-element.10, f32[128]{0:T(128)S(1)} %get-tuple-element.11, f32[128]{0:T(128)S(1)} %get-tuple-element.9), kind=kLoop, calls=%fused_computation | loop fusion | flops 1048576 | bytes 787968 | tf_op jit(solution)/shard_map/convert_element_type | solution.py:614
  (1 shorter events, 0.0 us)

commit v12 on v11

--- a/solution.py
+++ b/solution.py
@@ -195,14 +195,14 @@
 
 def kernel(
     src_hbm, cnt_ref, coarse_ref, remap_ref, ca_ref, cb_ref, gain_a_ref, shift_a_ref, gain_b_ref, shift_b_ref,
-    hb_ref, fin_ref,
+    out_ref,
     src_ref, coarse_v, remap_v, ca_v, cb_v, vec_v,
     tt, row_out, col_out, corner_out, mate_out, next_out, choice_out,
-    row_in, col_in, corner_in, mate_in, next_in, choice_in,
+    row_in, col_in, corner_in, mate_in, next_in, choice_in, side_choice,
     copies, choices, side, wa32, wa, wba, wbb,
     xs, gs, ha, hl, act, hb,
     stat, buf_x, buf_z,
-    in_sem, out_sem, send_sem, recv_sem,
+    in_sem, send_sem, recv_sem,
 ):
     place = coords()
     row, lon = place[0], place[1]
@@ -249,7 +249,6 @@
         local = lax.rem(src_ref[0, k] - (lon - 1) * BLK_DEV + 2 * NBLK, NBLK)
         local = jnp.where(k < cnt_ref[0], local, -64)
         own_choice = jnp.where((lane >> 5) == k, local.astype(F32), own_choice)
-    choice_tile = jnp.broadcast_to(own_choice, (16, 128)).astype(BF16)
 
     for q in range(BLK_DEV):
         want = q * BCELLS + (lane & (BCELLS - 1))
@@ -279,8 +278,7 @@
     row_out[...] = weights[0:128]
     choice_out[...] = own_choice
     for i in range(2):
-        col_out[i, 0:16, :] = weights[128 + 16 * i : 144 + 16 * i]
-        col_out[i, 16:32, :] = choice_tile
+        col_out[i] = weights[128 + 16 * i : 144 + 16 * i]
     for i in range(4):
         cells = weights[160 + 16 * i : 176 + 16 * i].astype(F32)
         corner_out[i] = jnp.where(iota((8, 128), 0) < 4, cells[0:8], own_choice)
@@ -329,6 +327,7 @@
 
     for i in range(2):
         send(col_out.at[i], col_in.at[i], halo[6 + i], 8, 2)
+        send(choice_out, side_choice.at[i], halo[6 + i], 12, 15)
     for i in (2, 3):
         send(corner_out.at[i, pl.ds(0, 5)], corner_in.at[i, pl.ds(0, 5)], halo[2 + i], 9, 12)
 
@@ -427,10 +426,11 @@
         return pltpu.make_async_copy(some, some, recv_sem.at[1 if first == 0 else 12])
 
     pltpu.make_async_copy(col_in, col_in, recv_sem.at[2]).wait()
+    pltpu.make_async_copy(side_choice, side_choice, recv_sem.at[15]).wait()
     corners(2).wait()
     cells = spread_cells([
-        fine_of(col_in[0, 0:16, :], col_in[0, 16:17, :], 0, 1.0),
-        fine_of(col_in[1, 0:16, :], col_in[1, 16:17, :], 2, 1.0),
+        fine_of(col_in[0], side_choice[0], 0, 1.0),
+        fine_of(col_in[1], side_choice[1], 2, 1.0),
         fine_of(corner_in[2], corner_in[2, 4:5, :], 0, 1.0),
         fine_of(corner_in[3], corner_in[3, 4:5, :], 2, 1.0),
     ])
@@ -520,15 +520,12 @@
     mean, inverse = all_reduce(0, sums, around_a)
 
     second_conv(ha, hl, act, gs, hb, wba, wbb, mean, inverse * vec_v[0], vec_v[1], not_first, not_last)
-    store = pltpu.make_async_copy(hb, hb_ref, out_sem)
-    store.start()
     about = group_mean(hb[0])
     sums = group_stats(about, *add_rows([hb[i] for i in range(8)], about))
     mean, inverse = all_reduce(1, sums, lambda stage: None)
-    fin_ref[0:1, :] = mean
-    fin_ref[1:2, :] = inverse * vec_v[2]
-    fin_ref[2:3, :] = vec_v[3]
-    store.wait()
+    scale = inverse * vec_v[2]
+    for i in range(8):
+        out_ref[i] = activate(hb[i], mean, scale, vec_v[3]).astype(BF16)
 
     @pl.when(has_far)
     def _():
@@ -541,6 +538,7 @@
     some = corner_in.at[pl.ds(2, 2), pl.ds(0, 5)]
     pltpu.make_async_copy(some, some, send_sem.at[9]).wait()
     pltpu.make_async_copy(col_in, col_in, send_sem.at[8]).wait()
+    pltpu.make_async_copy(side_choice, side_choice, send_sem.at[12]).wait()
     pltpu.make_async_copy(mate_in, mate_in, send_sem.at[2]).wait()
     pltpu.make_async_copy(tt.at[pl.ds(0, 4)], tt.at[pl.ds(0, 4)], send_sem.at[7]).wait()
     for turn in range(2):
@@ -553,15 +551,12 @@
 ):
     anywhere = pl.BlockSpec(memory_space=pl.ANY)
     vectors = [v.reshape(1, CH) for v in (gain_a, shift_a, gain_b, shift_b)]
-    hidden, final = pl.pallas_call(
+    return pl.pallas_call(
         kernel,
         name="stem",
-        out_shape=(
-            pltpu.VMEM((ROWS_DEV, COLS_DEV, CH), F32),
-            pltpu.VMEM((3, CH), F32),
-        ),
+        out_shape=pltpu.VMEM((ROWS_DEV, COLS_DEV, CH), BF16),
         in_specs=[anywhere, pl.BlockSpec(memory_space=pltpu.SMEM)] + [anywhere] * 8,
-        out_specs=(anywhere, pl.BlockSpec(memory_space=pltpu.VMEM)),
+        out_specs=pl.BlockSpec(memory_space=pltpu.VMEM),
         scratch_shapes=[
             pltpu.SMEM((1, SLOTS), jnp.int32),
             pltpu.VMEM((VARS, BLK_DEV, BCELLS), BF16),
@@ -571,17 +566,18 @@
             pltpu.VMEM((4, 1, CH), F32),
             pltpu.VMEM((5, 16, 128), BF16),
             pltpu.VMEM((128, 128), BF16),
-            pltpu.VMEM((2, 32, 128), BF16),
+            pltpu.VMEM((2, 16, 128), BF16),
             pltpu.VMEM((4, 8, 128), F32),
             pltpu.VMEM((2, 16, 128), F32),
             pltpu.VMEM((16, 128), F32),
             pltpu.VMEM((1, 128), F32),
             pltpu.VMEM((128, 128), BF16),
-            pltpu.VMEM((2, 32, 128), BF16),
+            pltpu.VMEM((2, 16, 128), BF16),
             pltpu.VMEM((4, 8, 128), F32),
             pltpu.VMEM((2, 16, 128), F32),
             pltpu.VMEM((16, 128), F32),
             pltpu.VMEM((1, 128), F32),
+            pltpu.VMEM((2, 1, 128), F32),
             pltpu.VMEM((128, BLK_DEV * 128), BF16),
             pltpu.VMEM((80, BLK_DEV * 128), F32),
             pltpu.VMEM((12, 8, 128), F32),
@@ -599,9 +595,8 @@
             pltpu.VMEM((2, 15, 1, CH), F32),
             pltpu.VMEM((2, 31, 1, CH), F32),
             pltpu.SemaphoreType.DMA((9,)),
-            pltpu.SemaphoreType.DMA,
-            pltpu.SemaphoreType.DMA((12,)),
-            pltpu.SemaphoreType.DMA((15,)),
+            pltpu.SemaphoreType.DMA((13,)),
+            pltpu.SemaphoreType.DMA((16,)),
         ],
         compiler_params=pltpu.CompilerParams(
             collective_id=0, has_side_effects=True, vmem_limit_bytes=60 * 1024 * 1024
@@ -610,8 +605,6 @@
         src_blocks, slot_counts, jnp.transpose(coarse, (1, 0, 2)), remap_tiles.reshape(SLOTS * BCELLS, 1024),
         conv_a, conv_b, *vectors,
     )
-    normed = (hidden - final[0]) * final[1] + final[2]
-    return jax.nn.silu(normed).astype(BF16)
 
 
 def solution(mesh):

time: 53.1 us -> 52.8 us (level)
  other arithmetic: 0.87 us -> 0 us
  local copies, waits for them, and re-layouts: 0.01 us -> 0.71 us
    convert_element_type x1 -> x0, other arithmetic: 0.87 us -> none  [per_device(): return jax.nn.silu(normed).astype(BF16)]
    unnamed x0 -> x1, local copies, waits for them, and re-layouts: none -> 0.71 us
where the time goes in v12:
time: 52.8 us; the launch traced here: 52.7 us
  Pallas kernels  51.3 us (97%)
  local copies, waits for them, and re-layouts  0.71 us (1%)
  between operations  0.66 us (1%)
    pallas_call x1, Pallas kernels, per_device(): pl.pallas_call(kernel, name='stem', out_shape=pltpu.VMEM((ROWS_DEV, COLS_...  51.3 us

profile of v12, /device:TPU:1, one launch (start us, length us, event | category | flops | bytes accessed | tf_op | source)
XLA Modules:
  0.0 52.7 jit_solution(434757137666716119)
XLA Ops:
  0.7 51.3 %stem.1 = bf16[8,128,128]{2,1,0:T(8,128)(2,1)S(1)} custom-call(s32[1,4]{1,0:T(1,128)} %src_hbm.1, s32[1]{0:T(128)S(6)} %copy.13.cnt_ref, bf16[12,4,32]{2,1,0:T(4,128)(2,1)} %bitcast.7, bf16[128,1024]{1,0:T(8,128)(2,1)} %bitcast.6, f32[3,3,12,128]{3,2,1,0:T(8,128)} %ca_ref.1, f32[3,3,128,128]{3,2,1,0:T(8,128)} %cb_ref.1, f32[1,128]{1,0:T(1,128)} %bitcast.8, ...), custom_call_target="tpu_custom_call" | custom-call | tf_op jit(solution)/shard_map/stem/pallas_call | solution.py:554
  52.0 0.7 %copy.12 = bf16[8,128,128]{2,1,0:T(8,128)(2,1)} copy(bf16[8,128,128]{2,1,0:T(8,128)(2,1)S(1)} %stem.1) | data formatting | bytes 524288

commit v13 on v12

--- a/solution.py
+++ b/solution.py
@@ -286,6 +286,54 @@
     hl[...] = jnp.zeros_like(hl)
     xs[...] = jnp.zeros_like(xs)
 
+    twelfth_l = (lane * 43) >> 9
+    var_l = jnp.where(lane < 9 * VARS, lane - 12 * twelfth_l, 4096)
+    part_l = twelfth_l - 3 * ((twelfth_l * 11) >> 5)
+    want = jnp.where(part_l == 1, var_l + 16, var_l)
+    spread_msg = jnp.where(iota((32, 128), 0) == want, 1.0, 0.0).astype(BF16)
+    spread_var = jnp.where(iota((16, 128), 0) == var_l, 1.0, 0.0).astype(BF16)
+    not_first = jnp.where(row > 0, 1.0, 0.0).astype(F32)
+    not_last = jnp.where(row < 15, 1.0, 0.0).astype(F32)
+
+    @pl.when(jnp.logical_not(has_far))
+    def _():
+        row_in[...] = jnp.zeros_like(row_in)
+        choice_in[...] = jnp.zeros_like(choice_in)
+        next_in[...] = jnp.zeros_like(next_in)
+        corner_in[0:2] = jnp.zeros((2, 8, 128), F32)
+
+    pl.semaphore_wait(barrier, len(partners) + 3 * jnp.where(has_far, 1, 0))
+
+    def send(src, dst, mate, out, into):
+        copy = pltpu.make_async_remote_copy(
+            src_ref=src, dst_ref=dst, send_sem=send_sem.at[out], recv_sem=recv_sem.at[into],
+            device_id=mate, device_id_type=MESH,
+        )
+        copy.start()
+
+    for i in range(2):
+        send(col_out.at[i], col_in.at[i], halo[6 + i], 8, 2)
+        send(choice_out, side_choice.at[i], halo[6 + i], 12, 15)
+    for i in (2, 3):
+        send(corner_out.at[i, pl.ds(0, 5)], corner_in.at[i, pl.ds(0, 5)], halo[2 + i], 9, 12)
+
+    @pl.when(has_far)
+    def _():
+        for i in (0, 1):
+            send(corner_out.at[i, pl.ds(0, 5)], corner_in.at[i, pl.ds(0, 5)], halo[1 + i], 1, 1)
+        send(row_out, row_in, halo[0], 0, 0)
+        send(choice_out, choice_in, halo[0], 11, 14)
+
+    along_lon = [
+        pltpu.make_async_remote_copy(
+            src_ref=tt.at[2], dst_ref=tt.at[slot], send_sem=send_sem.at[7], recv_sem=recv_sem.at[8 + i],
+            device_id=mate, device_id_type=MESH,
+        )
+        for i, (slot, mate) in enumerate(zip((0, 1, 3, 4), lon_mates))
+    ]
+    for copy in along_lon:
+        copy.start()
+
     loads[2].wait()
     wa32[...] = jnp.zeros_like(wa32)
     for dy in range(3):
@@ -299,54 +347,6 @@
     whole = wa32[...]
     high, low = split(whole)
     wa[...] = jnp.where(part_of == 2, low.astype(F32), high.astype(F32)).astype(BF16)
-
-    twelfth_l = (lane * 43) >> 9
-    var_l = jnp.where(lane < 9 * VARS, lane - 12 * twelfth_l, 4096)
-    part_l = twelfth_l - 3 * ((twelfth_l * 11) >> 5)
-    want = jnp.where(part_l == 1, var_l + 16, var_l)
-    spread_msg = jnp.where(iota((32, 128), 0) == want, 1.0, 0.0).astype(BF16)
-    spread_var = jnp.where(iota((16, 128), 0) == var_l, 1.0, 0.0).astype(BF16)
-    not_first = jnp.where(row > 0, 1.0, 0.0).astype(F32)
-    not_last = jnp.where(row < 15, 1.0, 0.0).astype(F32)
-
-    @pl.when(jnp.logical_not(has_far))
-    def _():
-        row_in[...] = jnp.zeros_like(row_in)
-        choice_in[...] = jnp.zeros_like(choice_in)
-        next_in[...] = jnp.zeros_like(next_in)
-        corner_in[0:2] = jnp.zeros((2, 8, 128), F32)
-
-    pl.semaphore_wait(barrier, len(partners) + 3 * jnp.where(has_far, 1, 0))
-
-    def send(src, dst, mate, out, into):
-        copy = pltpu.make_async_remote_copy(
-            src_ref=src, dst_ref=dst, send_sem=send_sem.at[out], recv_sem=recv_sem.at[into],
-            device_id=mate, device_id_type=MESH,
-        )
-        copy.start()
-
-    for i in range(2):
-        send(col_out.at[i], col_in.at[i], halo[6 + i], 8, 2)
-        send(choice_out, side_choice.at[i], halo[6 + i], 12, 15)
-    for i in (2, 3):
-        send(corner_out.at[i, pl.ds(0, 5)], corner_in.at[i, pl.ds(0, 5)], halo[2 + i], 9, 12)
-
-    @pl.when(has_far)
-    def _():
-        for i in (0, 1):
-            send(corner_out.at[i, pl.ds(0, 5)], corner_in.at[i, pl.ds(0, 5)], halo[1 + i], 1, 1)
-        send(row_out, row_in, halo[0], 0, 0)
-        send(choice_out, choice_in, halo[0], 11, 14)
-
-    along_lon = [
-        pltpu.make_async_remote_copy(
-            src_ref=tt.at[2], dst_ref=tt.at[slot], send_sem=send_sem.at[7], recv_sem=recv_sem.at[8 + i],
-            device_id=mate, device_id_type=MESH,
-        )
-        for i, (slot, mate) in enumerate(zip((0, 1, 3, 4), lon_mates))
-    ]
-    for copy in along_lon:
-        copy.start()
 
     for copy in along_lon:
         copy.wait_recv()

time: 52.8 us -> 52.8 us (level)
  no operation moved by 1% of the time
where the time goes in v13:
time: 52.8 us; the launch traced here: 52.7 us
  Pallas kernels  51.3 us (97%)
  local copies, waits for them, and re-layouts  0.71 us (1%)
  between operations  0.66 us (1%)
    pallas_call x1, Pallas kernels, per_device(): pl.pallas_call(kernel, name='stem', out_shape=pltpu.VMEM((ROWS_DEV, COLS_...  51.3 us

profile of v13, /device:TPU:1, one launch (start us, length us, event | category | flops | bytes accessed | tf_op | source)
XLA Modules:
  0.0 52.7 jit_solution(7911137544953735058)
XLA Ops:
  0.7 51.3 %stem.1 = bf16[8,128,128]{2,1,0:T(8,128)(2,1)S(1)} custom-call(s32[1,4]{1,0:T(1,128)} %src_hbm.1, s32[1]{0:T(128)S(6)} %copy.13.cnt_ref, bf16[12,4,32]{2,1,0:T(4,128)(2,1)} %bitcast.7, bf16[128,1024]{1,0:T(8,128)(2,1)} %bitcast.6, f32[3,3,12,128]{3,2,1,0:T(8,128)} %ca_ref.1, f32[3,3,128,128]{3,2,1,0:T(8,128)} %cb_ref.1, f32[1,128]{1,0:T(1,128)} %bitcast.8, ...), custom_call_target="tpu_custom_call" | custom-call | tf_op jit(solution)/shard_map/stem/pallas_call | solution.py:554
  52.0 0.7 %copy.12 = bf16[8,128,128]{2,1,0:T(8,128)(2,1)} copy(bf16[8,128,128]{2,1,0:T(8,128)(2,1)S(1)} %stem.1) | data formatting | bytes 524288
